TPU v7x, 128 devices: a whole 4x4x4 slice. The times are simulated.
128 devices in a mesh: sec: 16 (over z, y), mpo: 8 (over x, core).
Axes of the slice: x: 4, y: 4, z: 4, core: 2. Of those that a mesh axis runs over, the one named last changes fastest.
Arguments:
- psi: bfloat16 [256, 8, 64, 128], P('sec'), may hold values from -6 to 6
- left_env: bfloat16 [32, 256, 64, 64], P('mpo', 'sec'), may hold values from -0.125 to 0.125
- right_env: bfloat16 [32, 256, 128, 128], P('mpo', 'sec'), may hold values from -0.5 to 0.5
- source: int32 [32, 256], P('mpo', 'sec'), may hold values from 0 to 255, as said below
- active: int32 [32, 256], P('mpo', 'sec'), may hold values 0 or 1
Outputs:
- h_psi: bfloat16 [256, 8, 64, 128], P('sec', 'mpo')
Inputs may be any that keep to these rules, and one draw needn't show every extreme that they name: `source`: among the 4 x 16 entries of each aligned block (MPO indices w0 * 4 onward, sectors s0 * 16 onward), at most 8 name sectors of any one aligned group of 16 sectors, and exactly 8 name sectors of the block's own group s0.
All inputs are finite; a program needn't handle non-finite values. No bound on the sum of `active` on one device may be relied on, other than what follows from the above.
Results may differ from a plain program's by a relative error of at most 0.0049.
Values may be sent and summed in bfloat16 or wider, within the bound.
No kernel may reach another device: no remote copies, remote signals or barrier semaphores. Data moves between devices by JAX's collectives and lax.ppermute only.
A program may use at most 128 MiB of HBM per device.

v0:
```python
import jax
import jax.numpy as jnp
from jax import lax
from jax.sharding import PartitionSpec as P

CAP = 8


def per_device(psi, left_env, right_env, source, active):
    sec_local = psi.shape[0]
    mpo_local = source.shape[0]
    pair_count = mpo_local * sec_local
    capacity = CAP
    block_shape = psi.shape[1:]
    flat_source = source.reshape(pair_count)
    entry_ids = jnp.arange(pair_count, dtype=jnp.int32)
    empty = jnp.zeros((pair_count,) + block_shape, jnp.bfloat16)
    piece = lax.all_gather(psi, "sec", axis=0, tiled=True)
    piece_rows = piece.shape[0]
    limit = min(pair_count, -(-piece_rows // sec_local) * capacity)
    inside = ((flat_source >= 0) & (flat_source < piece_rows)).astype(jnp.int32)
    slots = jnp.cumsum(inside) - 1
    picker = inside[:, None] * (
        slots[:, None] == jnp.arange(limit, dtype=jnp.int32)[None, :]
    ).astype(jnp.int32)
    filled = jnp.sum(picker, axis=0)
    targets = jnp.sum(picker * entry_ids[:, None], axis=0)
    targets = jnp.where(filled > 0, targets, pair_count)
    rows_wanted = jnp.sum(picker * flat_source[:, None], axis=0)
    chosen = jnp.take(piece, rows_wanted, axis=0)
    needed = empty.at[targets].set(chosen, mode="drop")
    needed = needed.reshape((mpo_local, sec_local) + block_shape)
    applied = jnp.einsum(
        "wsab,wsvbc->wsvac", left_env, needed, preferred_element_type=jnp.float32
    ).astype(jnp.bfloat16)
    combined = jnp.einsum(
        "wsvac,wscd->wsvad", applied, right_env, preferred_element_type=jnp.float32
    )
    partial_value = jnp.sum(combined * active[:, :, None, None, None].astype(jnp.float32), axis=0)
    summed = lax.psum(partial_value, "mpo")
    share_size = partial_value.shape[1] // lax.axis_size("mpo")
    summed = lax.dynamic_slice_in_dim(summed, lax.axis_index("mpo") * share_size, share_size, 1)
    return summed.astype(jnp.bfloat16)


def solution(mesh):
    placed = (
        P("sec", None, None, None),
        P("mpo", "sec", None, None),
        P("mpo", "sec", None, None),
        P("mpo", "sec"),
        P("mpo", "sec"),
    )
    return jax.shard_map(
        per_device,
        mesh=mesh,
        in_specs=placed,
        out_specs=P("sec", "mpo", None, None),
        check_vma=False,
    )
```

profile of v0, /device:TPU:1, one launch (start us, length us, event | category | flops | bytes accessed | tf_op | source)
XLA Modules:
  0.0 326.7 jit_solution(14127867577117415385)
XLA Ops:
  6.5 0.0 copy-start
  6.5 0.0 all-gather.2.cloned.1.call-start
  6.5 0.7 all-gather.2.cloned.1.call-update
  7.3 0.8 reshape.108
  8.0 0.7 and_convert_fusion.1
  8.7 0.1 reshape.129
  8.8 0.7 convert_element_type.36
  9.5 0.1 reduce-window.8
  9.6 0.1 add_reduce_fusion
  9.7 0.1 fusion.8
  9.9 200.1 %all-gather.2.cloned.1.call-done = bf16[256,8,64,128]{3,2,1,0:T(8,128)(2,1)} async-done(((bf16[16,8,64,128]{3,2,1,0:T(8,128)(2,1)}), bf16[256,8,64,128]{3,2,1,0:T(8,128)(2,1)}) %all-gather.2.cloned.1.call-update) | async-done | bytes 33554448 | tf_op jit(solution)/shard_map/all_gather | solution.py:18
  210.0 7.6 %gather_fusion = bf16[64,8,64,128]{3,2,1,0:T(8,128)(2,1)} fusion(bf16[256,8,64,128]{3,2,1,0:T(8,128)(2,1)} %all-gather.2.cloned.1.call-done, s32[1024]{0:T(1024)S(1)} %pad_clamp_fusion), kind=kCustom, calls=%fused_computation | custom fusion | bytes 16777472 | tf_op jit(solution)/shard_map/jit(_take)/gather | solution.py:30
  217.6 7.4 %broadcast_select_fusion = bf16[64,8,64,128]{3,2,1,0:T(8,128)(2,1)} fusion(bf16[64,8,64,128]{3,2,1,0:T(8,128)(2,1)} %gather_fusion, pred[64]{0:T(512)(128)(4,1)S(1)} %compare_and_fusion), kind=kLoop, calls=%fused_computation.5 | loop fusion | flops 4194304 | bytes 16777280 | tf_op jit(solution)/shard_map/jit(_take)/select_n | solution.py:30
  225.0 5.4 %broadcast_in_dim.25 = bf16[64,8,64,128]{3,2,1,0:T(8,128)(2,1)} broadcast(bf16[]{:T(256)} %constant.11.clone.1), dimensions={} | broadcast | bytes 8388610 | tf_op jit(solution)/shard_map/broadcast_in_dim | solution.py:17
  230.4 0.0 copy-start.1
  230.4 22.2 %scatter_fusion = bf16[64,8,64,128]{3,2,1,0:T(8,128)(2,1)} fusion(bf16[64,8,64,128]{3,2,1,0:T(8,128)(2,1)} %broadcast_in_dim.25, s32[64]{0:T(128)S(1)} %get-tuple-element.8, bf16[64,8,64,128]{3,2,1,0:T(8,128)(2,1)} %broadcast_select_fusion), kind=kCustom, calls=%fused_computation.1 | custom fusion | bytes 25166080 | tf_op jit(solution)/shard_map/scatter | solution.py:31
  252.6 0.0 copy-done
  252.6 0.0 copy-done.1
  252.6 9.4 %multiply_reduce_fusion = f32[16,8,64,128]{3,2,1,0:T(8,128)} fusion(f32[4,16]{1,0:T(4,128)S(1)} %convert_element_type.36, bf16[4,16,8,64,128]{4,3,2,1,0:T(8,128)(2,1)} %bitcast.26, bf16[4,16,128,128]{3,2,1,0:T(8,128)(2,1)S(1)} %copy-done, bf16[4,16,64,64]{3,2,1,0:T(8,128)(2,1)S(1)} %copy-done.1), kind=kOutput, calls=%fused_computation.2 | convolution fusion | flops 1622147072 | bytes 15204608 | tf_op jit(solution)/shard_map/wsvac,wscd->wsvad/dot_general | solution.py:36
  262.0 56.1 %all-reduce.1 = bf16[16,8,64,128]{3,2,1,0:T(8,128)(2,1)} all-reduce(f32[16,8,64,128]{3,2,1,0:T(8,128)} %multiply_reduce_fusion), channel_id=1, replica_groups=mesh['sec'=16,'mpo'=8] {'mpo'}, use_global_device_ids=true, to_apply=%region_6.7 | all-reduce | flops 1048576 | bytes 6291456 | tf_op jit(solution)/shard_map/psum | solution.py:40
  318.1 1.7 dynamic-slice_convert_fusion
  (4 shorter events, 0.0 us)
Async XLA Ops:
  6.5 246.1 %copy-start = (bf16[4,16,128,128]{3,2,1,0:T(8,128)(2,1)S(1)}, bf16[4,16,128,128]{3,2,1,0:T(8,128)(2,1)}, u32[]{:S(2)}) copy-start(bf16[4,16,128,128]{3,2,1,0:T(8,128)(2,1)} %param.7) | copy-start | bytes 6291460
  6.5 203.4 %all-gather.2.cloned.1.call-start = ((), (), s32[]{:S(2)}) async-start(), calls=%async_computation | async-start | bytes 35651584 | tf_op jit(solution)/shard_map/all_gather | solution.py:18
  230.4 22.2 %copy-start.1 = (bf16[4,16,64,64]{3,2,1,0:T(8,128)(2,1)S(1)}, bf16[4,16,64,64]{3,2,1,0:T(8,128)(2,1)}, u32[]{:S(2)}) copy-start(bf16[4,16,64,64]{3,2,1,0:T(8,128)(2,1)} %param.6) | copy-start | bytes 1572868
Sparse Core Ops, SparseCore 0:
  9.5 200.4 all-gather.1
where the time goes:
time: 329 us; the launch traced here: 327 us
  waiting for transfers between devices  201 us (61%)
  blocking collectives  56.1 us (17%)
  local copies, waits for them, and re-layouts  37.7 us (11%)
  between operations  13.4 us (4%)
  matrix products  9.4 us (3%)
  other arithmetic  9.15 us (3%)
    all_gather x1, waiting for transfers between devices, per_device(): piece = lax.all_gather(psi, 'sec', axis=0, tiled=True)  200 us
    psum x1, blocking collectives, per_device(): summed = lax.psum(partial_value, 'mpo')  56.1 us
    scatter x1, local copies, waits for them, and re-layouts, per_device(): needed = empty.at[targets].set(chosen, mode='drop')  22.2 us
    dot_general x1, matrix products, per_device(): jnp.einsum('wsvac,wscd->wsvad', applied, right_env, preferred_element_typ...  9.4 us
    gather x1, local copies, waits for them, and re-layouts, per_device(): chosen = jnp.take(piece, rows_wanted, axis=0)  7.6 us
    select_n x1, other arithmetic, per_device(): chosen = jnp.take(piece, rows_wanted, axis=0)  7.45 us
  transfers between devices with their start and end apart: 1, of which 1 were waited for; matrix products, arithmetic and copies ran while one was open for 1% of the time, Pallas kernels for 0%

commit v1 on v0

v1 whole, which is shorter than its diff:
```python
import jax
import jax.numpy as jnp
from jax import lax
from jax.experimental import pallas as pl
from jax.experimental.pallas import tpu as pltpu
from jax.sharding import PartitionSpec as P

SIDE = 4
N_MPO = 8
BF = jnp.bfloat16
F32 = jnp.float32


def mpo_perm(fn):
    return [(m, fn(m)) for m in range(N_MPO)]


CORE = mpo_perm(lambda m: m ^ 1)
FAR = mpo_perm(lambda m: m ^ 4)
X_UP = mpo_perm(lambda m: (m + 2) % N_MPO)
X_DOWN = mpo_perm(lambda m: (m - 2) % N_MPO)


def ring_perm(first, step):
    pairs = []
    for z in range(SIDE):
        for y in range(SIDE):
            for m in range(N_MPO):
                if (m % 2 == 0) == first:
                    to = ((z + step) % SIDE) * SIDE + y
                else:
                    to = z * SIDE + (y + step) % SIDE
                pairs.append(((z * SIDE + y) * N_MPO + m, to * N_MPO + m))
    return pairs


A_UP, A_DOWN = ring_perm(True, 1), ring_perm(True, -1)
B_UP, B_DOWN = ring_perm(False, 1), ring_perm(False, -1)


def over_all(x, perm):
    return lax.ppermute(x, ("sec", "mpo"), perm)


def over_mpo(x, perm):
    return lax.ppermute(x, "mpo", perm)


def slot_of(t):
    return jnp.where(t == 0, 0, jnp.where(t == 3, 1, jnp.where(t == 1, 2, 3)))


def kernel(code_ref, c_ref, p_ref, n_ref, f0, f1, o0, o1, *refs):
    l_refs, r_refs, (out_ref, psi, sems) = refs[:4], refs[4:8], refs[8:]
    s = pl.program_id(0)
    sec = psi.shape[2]

    @pl.when(s == 0)
    def _():
        copies = [
            pltpu.make_async_copy(c_ref, psi.at[:, 0:4], sems.at[0]),
            pltpu.make_async_copy(p_ref, psi.at[:, 4:8], sems.at[1]),
            pltpu.make_async_copy(n_ref, psi.at[:, 8:12], sems.at[2]),
            pltpu.make_async_copy(f0, psi.at[0, 12:14], sems.at[3]),
            pltpu.make_async_copy(f1, psi.at[0, 14:16], sems.at[4]),
            pltpu.make_async_copy(o0, psi.at[1, 12:14], sems.at[5]),
            pltpu.make_async_copy(o1, psi.at[1, 14:16], sems.at[6]),
        ]
        for copy in copies:
            copy.start()
        for copy in copies:
            copy.wait()

    applied = []
    for g in range(4):
        for w in range(4):
            code = code_ref[g, w, s]
            at = jnp.maximum(code, 0)
            slot, row = at // sec, at % sec
            keep = jnp.where(code >= 0, 1.0, 0.0)
            packed = l_refs[g][w, 0]
            half = packed.shape[1] // 2
            left = jnp.concatenate([packed[:, :half], packed[:, half:]], axis=0)
            block = jnp.concatenate([psi[0, slot, row], psi[1, slot, row]], axis=1)
            value = jnp.dot(left, block, preferred_element_type=F32) * keep
            value = value.astype(BF)
            cols = value.shape[1] // 2
            applied.append(jnp.concatenate([value[:, :cols], value[:, cols:]], axis=0))
    total = None
    for g in range(4):
        rows = jnp.concatenate(applied[4 * g : 4 * g + 4], axis=1)
        right = r_refs[g][:, 0]
        right = right.reshape(right.shape[0] * right.shape[1], right.shape[2])
        term = jnp.dot(rows, right, preferred_element_type=F32)
        total = term if total is None else total + term
    out_ref[...] = total.reshape(out_ref.shape)


def compute(codes, pieces, lefts, rights):
    sec = codes.shape[2]
    v, _, _, dl, dr = pieces[0].shape
    any_spec = pl.BlockSpec(memory_space=pl.ANY)

    def env(x):
        return pl.BlockSpec((x.shape[0], 1) + x.shape[2:], lambda s, *_: (0, s, 0, 0))

    return pl.pallas_call(
        kernel,
        out_shape=jax.ShapeDtypeStruct((v, sec, dl, dr), F32),
        grid_spec=pltpu.PrefetchScalarGridSpec(
            num_scalar_prefetch=1,
            grid=(sec,),
            in_specs=[any_spec] * 7 + [env(x) for x in lefts + rights],
            out_specs=pl.BlockSpec((v, 1, dl, dr), lambda s, *_: (0, s, 0, 0)),
            scratch_shapes=[
                pltpu.VMEM((v, 16, sec, dl, dr), BF),
                pltpu.SemaphoreType.DMA((7,)),
            ],
        ),
        compiler_params=pltpu.CompilerParams(vmem_limit_bytes=32 * 2**20),
    )(codes, *pieces, *lefts, *rights)


def per_device(psi, left_env, right_env, source, active):
    sec_local = psi.shape[0]
    half = sec_local // 2
    m = lax.axis_index("mpo")
    sec = lax.axis_index("sec")

    def vector(v):
        return lax.dynamic_slice_in_dim(psi, v, 1, 1)[:, 0]

    own = jnp.stack([vector(m ^ 4), vector(m)])
    up = over_all(own, A_UP)
    down = over_all(own, A_DOWN)
    across = jnp.stack([over_all(up[0], A_UP), over_all(down[1], A_DOWN)])
    line = jnp.stack([own, up, down, across], axis=1)
    line_up = over_all(line, B_UP)
    line_down = over_all(line, B_DOWN)
    far0 = over_all(line_up[0, :2], B_UP)
    far1 = over_all(line_down[0, 2:], B_DOWN)
    near0 = over_all(line_up[1, :2], B_UP)
    near1 = over_all(line_down[1, 2:], B_DOWN)
    pieces = [line, line_up, line_down, far0, far1, near0, near1]

    rows = left_env.shape[2] // 2
    packed = jnp.concatenate([left_env[:, :, :rows], left_env[:, :, rows:]], axis=3)
    masked = jnp.where(active > 0, source, -1)

    def spread(x):
        mine = over_mpo(x, CORE)
        others = jnp.concatenate(
            [over_mpo(x[:, :half], X_DOWN), over_mpo(x[:, half:], X_UP)], axis=1
        )
        return [x, mine, others, over_mpo(others, CORE)]

    rights = spread(right_env)
    lefts = spread(packed)
    wanted = jnp.stack(spread(masked))

    group, row = wanted // sec_local, wanted % sec_local
    from_z = (group // SIDE - sec // SIDE) % SIDE
    from_y = (group % SIDE - sec % SIDE) % SIDE
    first = jnp.where(m % 2 == 0, from_z, from_y)
    second = jnp.where(m % 2 == 0, from_y, from_z)
    slot = slot_of(second) * SIDE + slot_of(first)
    codes = jnp.where(wanted >= 0, slot * sec_local + row, -1)

    partial = compute(codes, pieces, lefts, rights)
    arrived = over_mpo(partial[0].astype(BF), FAR)
    return (partial[1] + arrived.astype(F32)).astype(BF)[:, None]


def solution(mesh):
    placed = (
        P("sec", None, None, None),
        P("mpo", "sec", None, None),
        P("mpo", "sec", None, None),
        P("mpo", "sec"),
        P("mpo", "sec"),
    )
    return jax.shard_map(
        per_device,
        mesh=mesh,
        in_specs=placed,
        out_specs=P("sec", "mpo", None, None),
        check_vma=False,
    )
```

time: 329 us -> 127 us (0.39)
  waiting for transfers between devices: 201 us -> 57.9 us
  blocking collectives: 56.1 us -> 0 us
  starting transfers between devices: 0.01 us -> 32.2 us
  local copies, waits for them, and re-layouts: 37.7 us -> 18 us
  Pallas kernels: 0 us -> 16.1 us
  between operations: 13.4 us -> 0.18 us
  matrix products: 9.4 us -> 0 us
  other arithmetic: 9.15 us -> 1.97 us
    all_gather x1 -> x0, waiting for transfers between devices: 200 us -> none  [per_device(): piece = lax.all_gather(psi, 'sec', axis=0, tiled=True)]
    ppermute x0 -> x23, waiting for transfers between devices: none -> 57.9 us  [the longest x13 37.6 us: over_mpo(): return lax.ppermute(x, 'mpo', perm)]
    psum x1 -> x0, blocking collectives: 56.1 us -> none  [per_device(): summed = lax.psum(partial_value, 'mpo')]
    ppermute x0 -> x23, starting transfers between devices: none -> 32.2 us  [the longest x13 16.2 us: over_mpo(): return lax.ppermute(x, 'mpo', perm)]
    scatter x1 -> x0, local copies, waits for them, and re-layouts: 22.2 us -> none  [per_device(): needed = empty.at[targets].set(chosen, mode='drop')]
    pallas_call x0 -> x1, Pallas kernels: none -> 16.1 us  [compute(): pl.pallas_call(kernel, out_shape=jax.ShapeDtypeStruct((v, sec, dl, dr), F...]
    unnamed x4 -> x34, local copies, waits for them, and re-layouts: 0.01 us -> 12.6 us
    dot_general x1 -> x0, matrix products: 9.4 us -> none  [per_device(): jnp.einsum('wsvac,wscd->wsvad', applied, right_env, preferred_element_typ...]
  transfers between devices with their start and end apart: 1 -> 23, of which waited for: 1 -> 11; matrix products, arithmetic and copies ran while one was open for 1% -> 5% of each run, Pallas kernels for 0% -> 0%
where the time goes in v1:
time: 127 us; the launch traced here: 126 us
  waiting for transfers between devices  57.9 us (46%)
  starting transfers between devices  32.2 us (25%)
  local copies, waits for them, and re-layouts  18 us (14%)
  Pallas kernels  16.1 us (13%)
  other arithmetic  1.97 us (2%)
    ppermute x13, waiting for transfers between devices, over_mpo(): return lax.ppermute(x, 'mpo', perm)  37.6 us
    ppermute x10, waiting for transfers between devices, over_all(): return lax.ppermute(x, ('sec', 'mpo'), perm)  20.3 us
    ppermute x13, starting transfers between devices, over_mpo(): return lax.ppermute(x, 'mpo', perm)  16.2 us
    pallas_call x1, Pallas kernels, compute(): pl.pallas_call(kernel, out_shape=jax.ShapeDtypeStruct((v, sec, dl, dr), F...  16.1 us
    ppermute x10, starting transfers between devices, over_all(): return lax.ppermute(x, ('sec', 'mpo'), perm)  16 us
    unnamed x34, local copies, waits for them, and re-layouts  12.6 us
  transfers between devices with their start and end apart: 23, of which 11 were waited for; matrix products, arithmetic and copies ran while one was open for 5% of the time, Pallas kernels for 0%

profile of v1, /device:TPU:1, one launch (start us, length us, event | category | flops | bytes accessed | tf_op | source)
XLA Modules:
  0.0 126.3 jit_solution(15181832948696587697)
XLA Ops:
  0.0 1.2 dynamic-slice_bitcast_fusion.1
  1.3 2.2 %collective-permute-start.4 = (bf16[2,16,64,128]{3,2,1,0:T(8,128)(2,1)S(1)}, bf16[2,16,64,128]{3,2,1,0:T(8,128)(2,1)S(1)}, u32[]{:S(2)}, u32[]{:S(2)}) collective-permute-start(bf16[2,16,64,128]{3,2,1,0:T(8,128)(2,1)S(1)} %get-tuple-element.18), channel_id=1, source_target_pairs={{0,32},{1,9},{2,34},{3,11},{4,36},{5,13},{6,38},{7,15},{8,40},{9,1... | collective-permute-start | bytes 1572872 | tf_op jit(solution)/shard_map/ppermute | solution.py:42
  3.5 1.5 %collective-permute-start.5 = (bf16[2,16,64,128]{3,2,1,0:T(8,128)(2,1)S(1)}, bf16[2,16,64,128]{3,2,1,0:T(8,128)(2,1)S(1)}, u32[]{:S(2)}, u32[]{:S(2)}) collective-permute-start(bf16[2,16,64,128]{3,2,1,0:T(8,128)(2,1)S(1)} %get-tuple-element.18), channel_id=1, source_target_pairs={{0,96},{1,25},{2,98},{3,27},{4,100},{5,29},{6,102},{7,31},{8,104},... | collective-permute-start | bytes 1572872 | tf_op jit(solution)/shard_map/ppermute | solution.py:42
  5.0 6.8 %collective-permute-done.4 = bf16[2,16,64,128]{3,2,1,0:T(8,128)(2,1)S(1)} collective-permute-done((bf16[2,16,64,128]{3,2,1,0:T(8,128)(2,1)S(1)}, bf16[2,16,64,128]{3,2,1,0:T(8,128)(2,1)S(1)}, u32[]{:S(2)}, u32[]{:S(2)}) %collective-permute-start.4) | collective-permute-done | bytes 524320 | tf_op jit(solution)/shard_map/ppermute | solution.py:42
  11.8 0.1 collective-permute-start.6
  11.9 2.7 %collective-permute-start.7 = (bf16[16,64,128]{2,1,0:T(8,128)(2,1)S(1)}, bf16[16,64,128]{2,1,0:T(8,128)(2,1)S(1)}, u32[]{:S(2)}, u32[]{:S(2)}) collective-permute-start(bf16[16,64,128]{2,1,0:T(8,128)(2,1)S(1)} %slice_bitcast_fusion.5), channel_id=1, source_target_pairs={{0,96},{1,25},{2,98},{3,27},{4,100},{5,29},{6,102},{7,31},{8,104},... | collective-permute-start | bytes 786440 | tf_op jit(solution)/shard_map/ppermute | solution.py:42
  14.7 0.1 fusion.16
  14.8 2.5 %collective-permute-start.19 = (bf16[4,8,128,128]{3,2,1,0:T(8,128)(2,1)S(1)}, bf16[4,8,128,128]{3,2,1,0:T(8,128)(2,1)S(1)}, u32[]{:S(2)}, u32[]{:S(2)}) collective-permute-start(bf16[4,8,128,128]{3,2,1,0:T(8,128)(2,1)S(1)} %get-tuple-element.6), channel_id=1, source_target_pairs={{0,6},{1,7},{2,0},{3,1},{4,2},{5,3},{6,4},{7,5},{8,14},{9,15},{10,... | collective-permute-start | bytes 3145736 | tf_op jit(solution)/shard_map/ppermute | solution.py:46
  17.4 1.3 collective-permute-done.6
  18.7 0.3 pad_maximum_fusion.c_ref
  19.0 3.8 %collective-permute-start.9 = (bf16[2,4,16,64,128]{4,3,2,1,0:T(8,128)(2,1)S(1)}, bf16[2,4,16,64,128]{4,3,2,1,0:T(8,128)(2,1)S(1)}, u32[]{:S(2)}, u32[]{:S(2)}) collective-permute-start(bf16[2,4,16,64,128]{4,3,2,1,0:T(8,128)(2,1)S(1)} %pad_maximum_fusion.c_ref), channel_id=1, source_target_pairs={{0,24},{1,97},{2,26},{3,99},{4,28},{5,101},{6,30},{7,103},{8,0},{9... | collective-permute-start | bytes 6291464 | tf_op jit(solution)/shard_map/ppermute | solution.py:42
  22.8 2.4 %collective-permute-start.18 = (bf16[4,16,128,128]{3,2,1,0:T(8,128)(2,1)S(1)}, bf16[4,16,128,128]{3,2,1,0:T(8,128)(2,1)S(1)}, u32[]{:S(2)}, u32[]{:S(2)}) collective-permute-start(bf16[4,16,128,128]{3,2,1,0:T(8,128)(2,1)S(1)} %copy-done), channel_id=1, source_target_pairs={{0,1},{1,0},{2,3},{3,2},{4,5},{5,4},{6,7},{7,6},{8,9},{9,8},{10,11... | collective-permute-start | bytes 6291464 | tf_op jit(solution)/shard_map/ppermute | solution.py:46
  25.2 0.4 collective-permute-start.8
  25.7 11.3 %collective-permute-done.19 = bf16[4,8,128,128]{3,2,1,0:T(8,128)(2,1)S(1)} collective-permute-done((bf16[4,8,128,128]{3,2,1,0:T(8,128)(2,1)S(1)}, bf16[4,8,128,128]{3,2,1,0:T(8,128)(2,1)S(1)}, u32[]{:S(2)}, u32[]{:S(2)}) %collective-permute-start.19) | collective-permute-done | bytes 1048608 | tf_op jit(solution)/shard_map/ppermute | solution.py:46
  37.0 3.4 %collective-permute-start.1 = (s32[4,8]{1,0:T(4,128)S(1)}, s32[4,8]{1,0:T(4,128)S(1)}, u32[]{:S(2)}, u32[]{:S(2)}) collective-permute-start(s32[4,8]{1,0:T(4,128)S(1)} %get-tuple-element.19), channel_id=1, source_target_pairs={{0,6},{1,7},{2,0},{3,1},{4,2},{5,3},{6,4},{7,5},{8,14},{9,15},{10,... | collective-permute-start | bytes 392 | tf_op jit(solution)/shard_map/ppermute | solution.py:46
  40.4 1.2 constant_dynamic-update-slice_fusion.3
  41.6 1.2 constant_dynamic-update-slice_fusion.2.refs_6_
  42.8 4.0 %collective-permute-start.21 = (bf16[4,16,128,128]{3,2,1,0:T(8,128)(2,1)}, bf16[4,16,128,128]{3,2,1,0:T(8,128)(2,1)}, u32[]{:S(2)}, u32[]{:S(2)}) collective-permute-start(bf16[4,16,128,128]{3,2,1,0:T(8,128)(2,1)} %constant_dynamic-update-slice_fusion.2.refs_6_), channel_id=1, source_target_pairs={{0,1},{1,0},{2,3},{3,2},{4,5},{5,4},{6,7},{7,6},{8,9},{9,8},{10,11... | collective-permute-start | bytes 6291464 | tf_op jit(solution)/shard_map/ppermute | solution.py:46
  46.8 0.1 fusion.17
  47.0 0.3 fusion.3
  47.3 3.6 %collective-permute-done.2 = s32[4,8]{1,0:T(4,128)S(1)} collective-permute-done((s32[4,8]{1,0:T(4,128)S(1)}, s32[4,8]{1,0:T(4,128)S(1)}, u32[]{:S(2)}, u32[]{:S(2)}) %collective-permute-start.2) | collective-permute-done | bytes 160 | tf_op jit(solution)/shard_map/ppermute | solution.py:46
  50.9 7.0 %collective-permute-done.15 = bf16[4,8,32,128]{3,2,1,0:T(8,128)(2,1)S(1)} collective-permute-done((bf16[4,8,32,128]{3,2,1,0:T(8,128)(2,1)S(1)}, bf16[4,8,32,128]{3,2,1,0:T(8,128)(2,1)S(1)}, u32[]{:S(2)}, u32[]{:S(2)}) %collective-permute-start.15) | collective-permute-done | bytes 262176 | tf_op jit(solution)/shard_map/ppermute | solution.py:46
  57.9 0.3 pad_maximum_fusion.2.refs_0_
  58.3 6.9 %collective-permute-done.16 = bf16[4,8,32,128]{3,2,1,0:T(8,128)(2,1)S(1)} collective-permute-done((bf16[4,8,32,128]{3,2,1,0:T(8,128)(2,1)S(1)}, bf16[4,8,32,128]{3,2,1,0:T(8,128)(2,1)S(1)}, u32[]{:S(2)}, u32[]{:S(2)}) %collective-permute-start.16) | collective-permute-done | bytes 262176 | tf_op jit(solution)/shard_map/ppermute | solution.py:46
  65.2 2.7 %collective-permute-start = (s32[4,16]{1,0:T(4,128)S(1)}, s32[4,16]{1,0:T(4,128)S(1)}, u32[]{:S(2)}, u32[]{:S(2)}) collective-permute-start(s32[4,16]{1,0:T(4,128)S(1)} %compare_select_fusion), channel_id=1, source_target_pairs={{0,1},{1,0},{2,3},{3,2},{4,5},{5,4},{6,7},{7,6},{8,9},{9,8},{10,11... | collective-permute-start | bytes 776 | tf_op jit(solution)/shard_map/ppermute | solution.py:46
  67.9 0.8 collective-permute-done
  68.7 0.3 collective-permute-start.14
  69.0 0.2 collective-permute-start.17
  69.2 1.3 %slice_bitcast_fusion.1 = (bf16[2,16,64,128]{3,2,1,0:T(8,128)(2,1)}, bf16[2,16,64,128]{3,2,1,0:T(8,128)(2,1)}) fusion(bf16[2,4,16,64,128]{4,3,2,1,0:T(8,128)(2,1)S(1)} %collective-permute-done.9.n_ref), kind=kLoop, calls=%fused_computation.5 | loop fusion | bytes 2097152 | tf_op jit(solution)/shard_map/squeeze | solution.py:143
  70.5 0.4 collective-permute-start.3
  70.9 1.3 %slice_bitcast_fusion.2 = (bf16[2,16,64,128]{3,2,1,0:T(8,128)(2,1)}, bf16[2,16,64,128]{3,2,1,0:T(8,128)(2,1)}) fusion(bf16[2,4,16,64,128]{4,3,2,1,0:T(8,128)(2,1)S(1)} %collective-permute-done.8.p_ref), kind=kLoop, calls=%fused_computation.6 | loop fusion | bytes 2097152 | tf_op jit(solution)/shard_map/squeeze | solution.py:142
  72.2 3.8 %collective-permute-start.13 = (bf16[2,16,64,128]{3,2,1,0:T(8,128)(2,1)}, bf16[2,16,64,128]{3,2,1,0:T(8,128)(2,1)}, u32[]{:S(2)}, u32[]{:S(2)}) collective-permute-start(bf16[2,16,64,128]{3,2,1,0:T(8,128)(2,1)} %get-tuple-element.7), channel_id=1, source_target_pairs={{0,24},{1,97},{2,26},{3,99},{4,28},{5,101},{6,30},{7,103},{8,0},{9... | collective-permute-start | bytes 1572872 | tf_op jit(solution)/shard_map/ppermute | solution.py:42
  75.9 0.8 copy-done.9
  76.7 0.8 copy-done.11
  77.6 1.4 %collective-permute-start.12 = (bf16[2,16,64,128]{3,2,1,0:T(8,128)(2,1)}, bf16[2,16,64,128]{3,2,1,0:T(8,128)(2,1)}, u32[]{:S(2)}, u32[]{:S(2)}) collective-permute-start(bf16[2,16,64,128]{3,2,1,0:T(8,128)(2,1)} %get-tuple-element.9), channel_id=1, source_target_pairs={{0,8},{1,33},{2,10},{3,35},{4,12},{5,37},{6,14},{7,39},{8,16},{9,4... | collective-permute-start | bytes 1572872 | tf_op jit(solution)/shard_map/ppermute | solution.py:42
  79.0 1.3 %copy-done.7 = bf16[4,16,128,128]{3,2,1,0:T(8,128)(2,1)} copy-done((bf16[4,16,128,128]{3,2,1,0:T(8,128)(2,1)}, bf16[4,16,128,128]{3,2,1,0:T(8,128)(2,1)S(1)}, u32[]{:S(2)}) %copy-start.7) | copy-done | bytes 2097176
  80.5 1.8 %collective-permute-done.13.o1 = bf16[2,16,64,128]{3,2,1,0:T(8,128)(2,1)} collective-permute-done((bf16[2,16,64,128]{3,2,1,0:T(8,128)(2,1)}, bf16[2,16,64,128]{3,2,1,0:T(8,128)(2,1)}, u32[]{:S(2)}, u32[]{:S(2)}) %collective-permute-start.13) | collective-permute-done | bytes 524320 | tf_op jit(solution)/shard_map/ppermute | solution.py:42
  82.4 5.6 %collective-permute-done.11.f1 = bf16[2,16,64,128]{3,2,1,0:T(8,128)(2,1)} collective-permute-done((bf16[2,16,64,128]{3,2,1,0:T(8,128)(2,1)}, bf16[2,16,64,128]{3,2,1,0:T(8,128)(2,1)}, u32[]{:S(2)}, u32[]{:S(2)}) %collective-permute-start.11) | collective-permute-done | bytes 524320 | tf_op jit(solution)/shard_map/ppermute | solution.py:42
  88.0 4.8 %collective-permute-done.10.f0 = bf16[2,16,64,128]{3,2,1,0:T(8,128)(2,1)} collective-permute-done((bf16[2,16,64,128]{3,2,1,0:T(8,128)(2,1)}, bf16[2,16,64,128]{3,2,1,0:T(8,128)(2,1)}, u32[]{:S(2)}, u32[]{:S(2)}) %collective-permute-start.10) | collective-permute-done | bytes 524320 | tf_op jit(solution)/shard_map/ppermute | solution.py:42
  92.8 1.6 %copy-done.2 = bf16[2,4,16,64,128]{4,3,2,1,0:T(8,128)(2,1)S(1)} copy-done((bf16[2,4,16,64,128]{4,3,2,1,0:T(8,128)(2,1)S(1)}, bf16[2,4,16,64,128]{4,3,2,1,0:T(8,128)(2,1)}, u32[]{:S(2)}) %copy-start.2) | copy-done | bytes 2097176
  94.4 1.6 %copy-done.4 = bf16[2,4,16,64,128]{4,3,2,1,0:T(8,128)(2,1)S(1)} copy-done((bf16[2,4,16,64,128]{4,3,2,1,0:T(8,128)(2,1)S(1)}, bf16[2,4,16,64,128]{4,3,2,1,0:T(8,128)(2,1)}, u32[]{:S(2)}) %copy-start.4) | copy-done | bytes 2097176
  95.9 1.6 %copy-done.6 = bf16[2,4,16,64,128]{4,3,2,1,0:T(8,128)(2,1)S(1)} copy-done((bf16[2,4,16,64,128]{4,3,2,1,0:T(8,128)(2,1)S(1)}, bf16[2,4,16,64,128]{4,3,2,1,0:T(8,128)(2,1)}, u32[]{:S(2)}) %copy-start.6) | copy-done | bytes 2097176
  97.5 1.6 %copy-done.8 = bf16[4,16,128,128]{3,2,1,0:T(8,128)(2,1)S(1)} copy-done((bf16[4,16,128,128]{3,2,1,0:T(8,128)(2,1)S(1)}, bf16[4,16,128,128]{3,2,1,0:T(8,128)(2,1)}, u32[]{:S(2)}) %copy-start.8) | copy-done | bytes 2097176
  99.1 1.0 copy-done.10
  100.2 1.0 copy-done.12
  101.2 16.1 %shard_map.55 = f32[2,16,64,128]{3,2,1,0:T(8,128)S(1)} custom-call(s32[4,4,16]{2,1,0:T(4,128)S(1)} %fusion.11.code_ref, bf16[2,4,16,64,128]{4,3,2,1,0:T(8,128)(2,1)S(1)} %copy-done.2, bf16[2,4,16,64,128]{4,3,2,1,0:T(8,128)(2,1)S(1)} %copy-done.6, bf16[2,4,16,64,128]{4,3,2,1,0:T(8,128)(2,1)S(1)} %copy-done.4, ...), custom_call_target="tpu_custom_call" | custom-call | tf_op jit(solution)/shard_map/pallas_call | solution.py:107
  117.5 8.1 %collective-permute-done.22 = bf16[16,64,128]{2,1,0:T(8,128)(2,1)S(1)} collective-permute-done((bf16[16,64,128]{2,1,0:T(8,128)(2,1)S(1)}, bf16[16,64,128]{2,1,0:T(8,128)(2,1)S(1)}, u32[]{:S(2)}, u32[]{:S(2)}) %collective-permute-start.22) | collective-permute-done | bytes 262176 | tf_op jit(solution)/shard_map/ppermute | solution.py:46
  125.5 0.8 fusion.4
  (54 shorter events, 0.8 us)
Async XLA Ops:
  0.0 14.7 %copy-start = (bf16[4,16,128,128]{3,2,1,0:T(8,128)(2,1)S(1)}, bf16[4,16,128,128]{3,2,1,0:T(8,128)(2,1)}, u32[]{:S(2)}) copy-start(bf16[4,16,128,128]{3,2,1,0:T(8,128)(2,1)} %refs_4_.1) | copy-start | bytes 6291460
  1.3 10.5 %collective-permute-start.4 = (bf16[2,16,64,128]{3,2,1,0:T(8,128)(2,1)S(1)}, bf16[2,16,64,128]{3,2,1,0:T(8,128)(2,1)S(1)}, u32[]{:S(2)}, u32[]{:S(2)}) collective-permute-start(bf16[2,16,64,128]{3,2,1,0:T(8,128)(2,1)S(1)} %get-tuple-element.18), channel_id=1, source_target_pairs={{0,32},{1,9},{2,34},{3,11},{4,36},{5,13},{6,38},{7,15},{8,40},{9,1... | collective-permute-start | bytes 1572872 | tf_op jit(solution)/shard_map/ppermute | solution.py:42
  3.5 8.4 %collective-permute-start.5 = (bf16[2,16,64,128]{3,2,1,0:T(8,128)(2,1)S(1)}, bf16[2,16,64,128]{3,2,1,0:T(8,128)(2,1)S(1)}, u32[]{:S(2)}, u32[]{:S(2)}) collective-permute-start(bf16[2,16,64,128]{3,2,1,0:T(8,128)(2,1)S(1)} %get-tuple-element.18), channel_id=1, source_target_pairs={{0,96},{1,25},{2,98},{3,27},{4,100},{5,29},{6,102},{7,31},{8,104},... | collective-permute-start | bytes 1572872 | tf_op jit(solution)/shard_map/ppermute | solution.py:42
  11.8 6.8 %collective-permute-start.6 = (bf16[16,64,128]{2,1,0:T(8,128)(2,1)S(1)}, bf16[16,64,128]{2,1,0:T(8,128)(2,1)S(1)}, u32[]{:S(2)}, u32[]{:S(2)}) collective-permute-start(bf16[16,64,128]{2,1,0:T(8,128)(2,1)S(1)} %slice_bitcast_fusion.6), channel_id=1, source_target_pairs={{0,32},{1,9},{2,34},{3,11},{4,36},{5,13},{6,38},{7,15},{8,40},{9,1... | collective-permute-start | bytes 786440 | tf_op jit(solution)/shard_map/ppermute | solution.py:42
  11.9 6.7 %collective-permute-start.7 = (bf16[16,64,128]{2,1,0:T(8,128)(2,1)S(1)}, bf16[16,64,128]{2,1,0:T(8,128)(2,1)S(1)}, u32[]{:S(2)}, u32[]{:S(2)}) collective-permute-start(bf16[16,64,128]{2,1,0:T(8,128)(2,1)S(1)} %slice_bitcast_fusion.5), channel_id=1, source_target_pairs={{0,96},{1,25},{2,98},{3,27},{4,100},{5,29},{6,102},{7,31},{8,104},... | collective-permute-start | bytes 786440 | tf_op jit(solution)/shard_map/ppermute | solution.py:42
  14.8 22.2 %collective-permute-start.19 = (bf16[4,8,128,128]{3,2,1,0:T(8,128)(2,1)S(1)}, bf16[4,8,128,128]{3,2,1,0:T(8,128)(2,1)S(1)}, u32[]{:S(2)}, u32[]{:S(2)}) collective-permute-start(bf16[4,8,128,128]{3,2,1,0:T(8,128)(2,1)S(1)} %get-tuple-element.6), channel_id=1, source_target_pairs={{0,6},{1,7},{2,0},{3,1},{4,2},{5,3},{6,4},{7,5},{8,14},{9,15},{10,... | collective-permute-start | bytes 3145736 | tf_op jit(solution)/shard_map/ppermute | solution.py:46
  17.4 24.2 %collective-permute-start.20 = (bf16[4,8,128,128]{3,2,1,0:T(8,128)(2,1)S(1)}, bf16[4,8,128,128]{3,2,1,0:T(8,128)(2,1)S(1)}, u32[]{:S(2)}, u32[]{:S(2)}) collective-permute-start(bf16[4,8,128,128]{3,2,1,0:T(8,128)(2,1)S(1)} %get-tuple-element.5), channel_id=1, source_target_pairs={{0,2},{1,3},{2,4},{3,5},{4,6},{5,7},{6,0},{7,1},{8,10},{9,11},{10,... | collective-permute-start | bytes 3145736 | tf_op jit(solution)/shard_map/ppermute | solution.py:46
  18.7 6.9 %copy-start.14 = (s32[4,16]{1,0:T(4,128)S(1)}, s32[4,16]{1,0:T(4,128)}, u32[]{:S(2)}) copy-start(s32[4,16]{1,0:T(4,128)} %param.8) | copy-start | bytes 772
  18.7 6.9 %copy-start.15 = (s32[4,16]{1,0:T(4,128)S(1)}, s32[4,16]{1,0:T(4,128)}, u32[]{:S(2)}) copy-start(s32[4,16]{1,0:T(4,128)} %param.9) | copy-start | bytes 772
  19.0 23.8 %copy-start.1 = (bf16[2,4,16,64,128]{4,3,2,1,0:T(8,128)(2,1)}, bf16[2,4,16,64,128]{4,3,2,1,0:T(8,128)(2,1)S(1)}, u32[]{:S(2)}) copy-start(bf16[2,4,16,64,128]{4,3,2,1,0:T(8,128)(2,1)S(1)} %pad_maximum_fusion.c_ref) | copy-start | bytes 6291460
  19.0 50.0 %collective-permute-start.9 = (bf16[2,4,16,64,128]{4,3,2,1,0:T(8,128)(2,1)S(1)}, bf16[2,4,16,64,128]{4,3,2,1,0:T(8,128)(2,1)S(1)}, u32[]{:S(2)}, u32[]{:S(2)}) collective-permute-start(bf16[2,4,16,64,128]{4,3,2,1,0:T(8,128)(2,1)S(1)} %pad_maximum_fusion.c_ref), channel_id=1, source_target_pairs={{0,24},{1,97},{2,26},{3,99},{4,28},{5,101},{6,30},{7,103},{8,0},{9... | collective-permute-start | bytes 6291464 | tf_op jit(solution)/shard_map/ppermute | solution.py:42
  22.8 56.2 %collective-permute-start.18 = (bf16[4,16,128,128]{3,2,1,0:T(8,128)(2,1)S(1)}, bf16[4,16,128,128]{3,2,1,0:T(8,128)(2,1)S(1)}, u32[]{:S(2)}, u32[]{:S(2)}) collective-permute-start(bf16[4,16,128,128]{3,2,1,0:T(8,128)(2,1)S(1)} %copy-done), channel_id=1, source_target_pairs={{0,1},{1,0},{2,3},{3,2},{4,5},{5,4},{6,7},{7,6},{8,9},{9,8},{10,11... | collective-permute-start | bytes 6291464 | tf_op jit(solution)/shard_map/ppermute | solution.py:46
  25.2 45.3 %collective-permute-start.8 = (bf16[2,4,16,64,128]{4,3,2,1,0:T(8,128)(2,1)S(1)}, bf16[2,4,16,64,128]{4,3,2,1,0:T(8,128)(2,1)S(1)}, u32[]{:S(2)}, u32[]{:S(2)}) collective-permute-start(bf16[2,4,16,64,128]{4,3,2,1,0:T(8,128)(2,1)S(1)} %pad_maximum_fusion.c_ref), channel_id=1, source_target_pairs={{0,8},{1,33},{2,10},{3,35},{4,12},{5,37},{6,14},{7,39},{8,16},{9,4... | collective-permute-start | bytes 6291464 | tf_op jit(solution)/shard_map/ppermute | solution.py:42
  37.0 9.9 %copy-start.13 = (bf16[4,16,64,64]{3,2,1,0:T(8,128)(2,1)S(1)}, bf16[4,16,64,64]{3,2,1,0:T(8,128)(2,1)}, u32[]{:S(2)}) copy-start(bf16[4,16,64,64]{3,2,1,0:T(8,128)(2,1)} %param.6) | copy-start | bytes 1572868
  37.0 10.0 %collective-permute-start.1 = (s32[4,8]{1,0:T(4,128)S(1)}, s32[4,8]{1,0:T(4,128)S(1)}, u32[]{:S(2)}, u32[]{:S(2)}) collective-permute-start(s32[4,8]{1,0:T(4,128)S(1)} %get-tuple-element.19), channel_id=1, source_target_pairs={{0,6},{1,7},{2,0},{3,1},{4,2},{5,3},{6,4},{7,5},{8,14},{9,15},{10,... | collective-permute-start | bytes 392 | tf_op jit(solution)/shard_map/ppermute | solution.py:46
  42.8 37.7 %collective-permute-start.21 = (bf16[4,16,128,128]{3,2,1,0:T(8,128)(2,1)}, bf16[4,16,128,128]{3,2,1,0:T(8,128)(2,1)}, u32[]{:S(2)}, u32[]{:S(2)}) collective-permute-start(bf16[4,16,128,128]{3,2,1,0:T(8,128)(2,1)} %constant_dynamic-update-slice_fusion.2.refs_6_), channel_id=1, source_target_pairs={{0,1},{1,0},{2,3},{3,2},{4,5},{5,4},{6,7},{7,6},{8,9},{9,8},{10,11... | collective-permute-start | bytes 6291464 | tf_op jit(solution)/shard_map/ppermute | solution.py:46
  46.9 4.0 %collective-permute-start.2 = (s32[4,8]{1,0:T(4,128)S(1)}, s32[4,8]{1,0:T(4,128)S(1)}, u32[]{:S(2)}, u32[]{:S(2)}) collective-permute-start(s32[4,8]{1,0:T(4,128)S(1)} %get-tuple-element.20), channel_id=1, source_target_pairs={{0,2},{1,3},{2,4},{3,5},{4,6},{5,7},{6,0},{7,1},{8,10},{9,11},{10,... | collective-permute-start | bytes 392 | tf_op jit(solution)/shard_map/ppermute | solution.py:46
  50.9 7.0 %collective-permute-start.15 = (bf16[4,8,32,128]{3,2,1,0:T(8,128)(2,1)S(1)}, bf16[4,8,32,128]{3,2,1,0:T(8,128)(2,1)S(1)}, u32[]{:S(2)}, u32[]{:S(2)}) collective-permute-start(bf16[4,8,32,128]{3,2,1,0:T(8,128)(2,1)S(1)} %get-tuple-element.14), channel_id=1, source_target_pairs={{0,6},{1,7},{2,0},{3,1},{4,2},{5,3},{6,4},{7,5},{8,14},{9,15},{10,... | collective-permute-start | bytes 786440 | tf_op jit(solution)/shard_map/ppermute | solution.py:46
  57.9 7.2 %collective-permute-start.16 = (bf16[4,8,32,128]{3,2,1,0:T(8,128)(2,1)S(1)}, bf16[4,8,32,128]{3,2,1,0:T(8,128)(2,1)S(1)}, u32[]{:S(2)}, u32[]{:S(2)}) collective-permute-start(bf16[4,8,32,128]{3,2,1,0:T(8,128)(2,1)S(1)} %get-tuple-element.13), channel_id=1, source_target_pairs={{0,2},{1,3},{2,4},{3,5},{4,6},{5,7},{6,0},{7,1},{8,10},{9,11},{10,... | collective-permute-start | bytes 786440 | tf_op jit(solution)/shard_map/ppermute | solution.py:46
  65.2 3.5 %collective-permute-start = (s32[4,16]{1,0:T(4,128)S(1)}, s32[4,16]{1,0:T(4,128)S(1)}, u32[]{:S(2)}, u32[]{:S(2)}) collective-permute-start(s32[4,16]{1,0:T(4,128)S(1)} %compare_select_fusion), channel_id=1, source_target_pairs={{0,1},{1,0},{2,3},{3,2},{4,5},{5,4},{6,7},{7,6},{8,9},{9,8},{10,11... | collective-permute-start | bytes 776 | tf_op jit(solution)/shard_map/ppermute | solution.py:46
  68.7 7.3 %collective-permute-start.14 = (bf16[4,16,32,128]{3,2,1,0:T(8,128)(2,1)S(1)}, bf16[4,16,32,128]{3,2,1,0:T(8,128)(2,1)S(1)}, u32[]{:S(2)}, u32[]{:S(2)}) collective-permute-start(bf16[4,16,32,128]{3,2,1,0:T(8,128)(2,1)S(1)} %pad_maximum_fusion.2.refs_0_), channel_id=1, source_target_pairs={{0,1},{1,0},{2,3},{3,2},{4,5},{5,4},{6,7},{7,6},{8,9},{9,8},{10,11... | collective-permute-start | bytes 1572872 | tf_op jit(solution)/shard_map/ppermute | solution.py:46
  69.0 3.2 %copy-start.3 = (bf16[2,4,16,64,128]{4,3,2,1,0:T(8,128)(2,1)}, bf16[2,4,16,64,128]{4,3,2,1,0:T(8,128)(2,1)S(1)}, u32[]{:S(2)}) copy-start(bf16[2,4,16,64,128]{4,3,2,1,0:T(8,128)(2,1)S(1)} %collective-permute-done.9.n_ref) | copy-start | bytes 6291460
  69.0 7.7 %collective-permute-start.17 = (bf16[4,16,32,128]{3,2,1,0:T(8,128)(2,1)S(1)}, bf16[4,16,32,128]{3,2,1,0:T(8,128)(2,1)S(1)}, u32[]{:S(2)}, u32[]{:S(2)}) collective-permute-start(bf16[4,16,32,128]{3,2,1,0:T(8,128)(2,1)S(1)} %constant_dynamic-update-slice_fusion.refs_2_), channel_id=1, source_target_pairs={{0,1},{1,0},{2,3},{3,2},{4,5},{5,4},{6,7},{7,6},{8,9},{9,8},{10,11... | collective-permute-start | bytes 1572872 | tf_op jit(solution)/shard_map/ppermute | solution.py:46
  70.4 8.6 %copy-start.5 = (bf16[2,4,16,64,128]{4,3,2,1,0:T(8,128)(2,1)}, bf16[2,4,16,64,128]{4,3,2,1,0:T(8,128)(2,1)S(1)}, u32[]{:S(2)}) copy-start(bf16[2,4,16,64,128]{4,3,2,1,0:T(8,128)(2,1)S(1)} %collective-permute-done.8.p_ref) | copy-start | bytes 6291460
  70.5 1.7 %collective-permute-start.3 = (s32[4,16]{1,0:T(4,128)S(1)}, s32[4,16]{1,0:T(4,128)S(1)}, u32[]{:S(2)}, u32[]{:S(2)}) collective-permute-start(s32[4,16]{1,0:T(4,128)S(1)} %pad_add_fusion.1), channel_id=1, source_target_pairs={{0,1},{1,0},{2,3},{3,2},{4,5},{5,4},{6,7},{7,6},{8,9},{9,8},{10,11... | collective-permute-start | bytes 776 | tf_op jit(solution)/shard_map/ppermute | solution.py:46
  72.2 10.2 %collective-permute-start.13 = (bf16[2,16,64,128]{3,2,1,0:T(8,128)(2,1)}, bf16[2,16,64,128]{3,2,1,0:T(8,128)(2,1)}, u32[]{:S(2)}, u32[]{:S(2)}) collective-permute-start(bf16[2,16,64,128]{3,2,1,0:T(8,128)(2,1)} %get-tuple-element.7), channel_id=1, source_target_pairs={{0,24},{1,97},{2,26},{3,99},{4,28},{5,101},{6,30},{7,103},{8,0},{9... | collective-permute-start | bytes 1572872 | tf_op jit(solution)/shard_map/ppermute | solution.py:42
  75.9 0.8 copy-start.9
  76.7 11.2 %collective-permute-start.11 = (bf16[2,16,64,128]{3,2,1,0:T(8,128)(2,1)}, bf16[2,16,64,128]{3,2,1,0:T(8,128)(2,1)}, u32[]{:S(2)}, u32[]{:S(2)}) collective-permute-start(bf16[2,16,64,128]{3,2,1,0:T(8,128)(2,1)} %get-tuple-element.8), channel_id=1, source_target_pairs={{0,24},{1,97},{2,26},{3,99},{4,28},{5,101},{6,30},{7,103},{8,0},{9... | collective-permute-start | bytes 1572872 | tf_op jit(solution)/shard_map/ppermute | solution.py:42
  76.7 0.8 copy-start.11
  77.6 10.4 %collective-permute-start.12 = (bf16[2,16,64,128]{3,2,1,0:T(8,128)(2,1)}, bf16[2,16,64,128]{3,2,1,0:T(8,128)(2,1)}, u32[]{:S(2)}, u32[]{:S(2)}) collective-permute-start(bf16[2,16,64,128]{3,2,1,0:T(8,128)(2,1)} %get-tuple-element.9), channel_id=1, source_target_pairs={{0,8},{1,33},{2,10},{3,35},{4,12},{5,37},{6,14},{7,39},{8,16},{9,4... | collective-permute-start | bytes 1572872 | tf_op jit(solution)/shard_map/ppermute | solution.py:42
  79.0 1.3 %copy-start.7 = (bf16[4,16,128,128]{3,2,1,0:T(8,128)(2,1)}, bf16[4,16,128,128]{3,2,1,0:T(8,128)(2,1)S(1)}, u32[]{:S(2)}) copy-start(bf16[4,16,128,128]{3,2,1,0:T(8,128)(2,1)S(1)} %collective-permute-done.18.refs_5_) | copy-start | bytes 6291460
  80.4 12.4 %collective-permute-start.10 = (bf16[2,16,64,128]{3,2,1,0:T(8,128)(2,1)}, bf16[2,16,64,128]{3,2,1,0:T(8,128)(2,1)}, u32[]{:S(2)}, u32[]{:S(2)}) collective-permute-start(bf16[2,16,64,128]{3,2,1,0:T(8,128)(2,1)} %get-tuple-element.10), channel_id=1, source_target_pairs={{0,8},{1,33},{2,10},{3,35},{4,12},{5,37},{6,14},{7,39},{8,16},{9,4... | collective-permute-start | bytes 1572872 | tf_op jit(solution)/shard_map/ppermute | solution.py:42
  92.8 1.6 %copy-start.2 = (bf16[2,4,16,64,128]{4,3,2,1,0:T(8,128)(2,1)S(1)}, bf16[2,4,16,64,128]{4,3,2,1,0:T(8,128)(2,1)}, u32[]{:S(2)}) copy-start(bf16[2,4,16,64,128]{4,3,2,1,0:T(8,128)(2,1)} %copy-done.1) | copy-start | bytes 6291460
  94.3 1.6 %copy-start.4 = (bf16[2,4,16,64,128]{4,3,2,1,0:T(8,128)(2,1)S(1)}, bf16[2,4,16,64,128]{4,3,2,1,0:T(8,128)(2,1)}, u32[]{:S(2)}) copy-start(bf16[2,4,16,64,128]{4,3,2,1,0:T(8,128)(2,1)} %copy-done.3) | copy-start | bytes 6291460
  95.9 1.6 %copy-start.6 = (bf16[2,4,16,64,128]{4,3,2,1,0:T(8,128)(2,1)S(1)}, bf16[2,4,16,64,128]{4,3,2,1,0:T(8,128)(2,1)}, u32[]{:S(2)}) copy-start(bf16[2,4,16,64,128]{4,3,2,1,0:T(8,128)(2,1)} %copy-done.5) | copy-start | bytes 6291460
  97.5 1.6 %copy-start.8 = (bf16[4,16,128,128]{3,2,1,0:T(8,128)(2,1)S(1)}, bf16[4,16,128,128]{3,2,1,0:T(8,128)(2,1)}, u32[]{:S(2)}) copy-start(bf16[4,16,128,128]{3,2,1,0:T(8,128)(2,1)} %copy-done.7) | copy-start | bytes 6291460
  99.1 1.0 copy-start.10
  100.2 1.0 copy-start.12
  117.4 8.2 %collective-permute-start.22 = (bf16[16,64,128]{2,1,0:T(8,128)(2,1)S(1)}, bf16[16,64,128]{2,1,0:T(8,128)(2,1)S(1)}, u32[]{:S(2)}, u32[]{:S(2)}) collective-permute-start(bf16[16,64,128]{2,1,0:T(8,128)(2,1)S(1)} %fusion.5), channel_id=1, source_target_pairs={{0,4},{1,5},{2,6},{3,7},{4,0},{5,1},{6,2},{7,3},{8,12},{9,13},{10,... | collective-permute-start | bytes 786440 | tf_op jit(solution)/shard_map/ppermute | solution.py:46

commit v2 on v0

v2 whole, which is shorter than its diff:
```python
import functools

import jax
import jax.numpy as jnp
from jax import lax
from jax.experimental import pallas as pl
from jax.experimental.pallas import tpu as pltpu
from jax.sharding import PartitionSpec as P

SIDE = 4
N_MPO = 8
BF = jnp.bfloat16
F32 = jnp.float32
PIECE, PIECES = 64, 4
PAIRS = 256
UNROLL = 16


def mpo_perm(fn):
    return [(m, fn(m)) for m in range(N_MPO)]


CORE = mpo_perm(lambda m: m ^ 1)
FAR = mpo_perm(lambda m: m ^ 4)
X_APART = mpo_perm(lambda m: (m - 2 + 4 * (m % 2)) % N_MPO)


def ring_perm(first, step):
    pairs = []
    for z in range(SIDE):
        for y in range(SIDE):
            for m in range(N_MPO):
                if (m % 2 == 0) == first:
                    to = ((z + step) % SIDE) * SIDE + y
                else:
                    to = z * SIDE + (y + step) % SIDE
                pairs.append(((z * SIDE + y) * N_MPO + m, to * N_MPO + m))
    return pairs


A_UP, A_DOWN, A_TWO = ring_perm(True, 1), ring_perm(True, -1), ring_perm(True, 2)
B_UP, B_DOWN = ring_perm(False, 1), ring_perm(False, -1)


def over_all(x, perm):
    return lax.ppermute(x, ("sec", "mpo"), perm)


def over_mpo(x, perm):
    return lax.ppermute(x, "mpo", perm)


def order(t):
    return jnp.where(t == 0, 0, jnp.where(t == 3, 1, jnp.where(t == 1, 2, 3)))


def list_kernel(place_ref, entry_ref, list_ref):
    def step(i, carry):
        list_ref[place_ref[i]] = entry_ref[i]
        return carry

    lax.fori_loop(0, place_ref.shape[0], step, 0, unroll=16)


def make_lists(codes):
    pair = lax.broadcasted_iota(jnp.int32, codes.shape, 0)
    row = jnp.where(codes >= 0, codes // PIECE, PIECES)
    rows = lax.broadcasted_iota(jnp.int32, (PIECES + 1, PAIRS), 0)
    chosen = (row[None] == rows).astype(jnp.int32)
    before = jnp.cumsum(chosen, axis=1) - chosen
    place = row * PAIRS + jnp.sum(before * chosen, axis=0)
    smem = pl.BlockSpec(memory_space=pltpu.SMEM)
    lists = pl.pallas_call(
        list_kernel,
        out_shape=jax.ShapeDtypeStruct(((PIECES + 1) * PAIRS,), jnp.int32),
        in_specs=[smem, smem],
        out_specs=smem,
    )(place, codes % PIECE * PAIRS + pair)
    return lists, jnp.sum(chosen, axis=1)


def term_kernel(lines, n_vec, n_env, fresh, list_ref, count_ref, *refs):
    envs, refs = refs[:n_env], refs[n_env:]
    psi_refs, refs = refs[: len(lines) * n_vec], refs[len(lines) * n_vec :]
    if not fresh:
        acc_refs, refs = refs[:n_vec], refs[n_vec:]
    out_refs, totals = refs[:n_vec], refs[n_vec:]
    sec, dl, dr = out_refs[0].shape

    for v in range(n_vec):
        if fresh:
            totals[v][...] = jnp.zeros_like(totals[v])
        else:
            totals[v][0:sec] = acc_refs[v][...]

    def rows_of(pair, first, last):
        value, start = None, 0
        for env in envs:
            size = env.shape[0]
            here = env[jnp.clip(pair - start, 0, size - 1), first:last, :]
            value = here if value is None else jnp.where(pair >= start, here, value)
            start += size
        return value

    def add(psis, line):
        count = count_ref[line]

        def step(i, carry):
            entries = []
            for u in range(UNROLL):
                there = i * UNROLL + u < count
                entry = jnp.where(there, list_ref[line * PAIRS + i * UNROLL + u], 0)
                pair = entry % PAIRS
                entries.append((entry // PAIRS, pair, jnp.where(there, pair % sec, sec)))
            values = []
            for at, pair, _ in entries:
                packed = rows_of(pair, dr, dr + dl // 2)
                left = jnp.concatenate([packed[:, :dl], packed[:, dl:]], axis=0)
                blocks = [psi[at] for psi in psis]
                block = blocks[0] if n_vec == 1 else jnp.concatenate(blocks, axis=1)
                value = jnp.dot(left, block, preferred_element_type=F32).astype(BF)
                if n_vec > 1:
                    value = jnp.concatenate(
                        [value[:, v * dr : (v + 1) * dr] for v in range(n_vec)], axis=0
                    )
                values.append(value)
            terms = []
            for value, (_, pair, _) in zip(values, entries):
                right = rows_of(pair, 0, dr)
                terms.append(jnp.dot(value, right, preferred_element_type=F32))
            for term, (_, _, to) in zip(terms, entries):
                for v in range(n_vec):
                    totals[v][to] += term[v * dl : (v + 1) * dl]
            return carry

        lax.fori_loop(0, (count + UNROLL - 1) // UNROLL, step, 0)

    for p, line in enumerate(lines):
        add(psi_refs[p * n_vec : (p + 1) * n_vec], line)
    for v in range(n_vec):
        out_refs[v][...] = totals[v][0:sec].astype(out_refs[v].dtype)


def add_terms(rows, lists, counts, envs, psis, accs, sec, dtype=F32):
    n_vec = len(psis[0])
    flat = [x for piece in psis for x in piece]
    _, dl, dr = flat[0].shape
    smem = pl.BlockSpec(memory_space=pltpu.SMEM)
    vmem = pl.BlockSpec(memory_space=pltpu.VMEM)
    return pl.pallas_call(
        functools.partial(term_kernel, rows, n_vec, len(envs), accs is None),
        out_shape=[jax.ShapeDtypeStruct((sec, dl, dr), dtype)] * n_vec,
        in_specs=[smem, smem] + [vmem] * (len(envs) + len(flat) + len(accs or [])),
        out_specs=[vmem] * n_vec,
        scratch_shapes=[pltpu.VMEM((sec + 1, dl, dr), F32)] * n_vec,
        compiler_params=pltpu.CompilerParams(vmem_limit_bytes=24 * 2**20),
        cost_estimate=pl.CostEstimate(
            flops=int(3e9), bytes_accessed=int(1.2e7), transcendentals=0
        ),
    )(lists, counts, *envs, *flat, *(accs or []))


def join_kernel(*refs):
    *arrays, out, sems = refs
    copies = []
    for k, ref in enumerate(arrays):
        size = ref.shape[0]
        copies.append(pltpu.make_async_copy(ref, out.at[k * size : (k + 1) * size], sems.at[k]))
    for copy in copies:
        copy.start()
    for copy in copies:
        copy.wait()


def join(arrays):
    first = arrays[0]
    return pl.pallas_call(
        join_kernel,
        out_shape=jax.ShapeDtypeStruct((first.shape[0] * len(arrays),) + first.shape[1:], first.dtype),
        in_specs=[pl.BlockSpec(memory_space=pl.ANY)] * len(arrays),
        out_specs=pl.BlockSpec(memory_space=pltpu.VMEM),
        scratch_shapes=[pltpu.SemaphoreType.DMA((len(arrays),))],
        compiler_params=pltpu.CompilerParams(vmem_limit_bytes=12 * 2**20),
        cost_estimate=pl.CostEstimate(flops=0, bytes_accessed=int(1e7), transcendentals=0),
    )(*arrays)


def copy_all(pairs, sems):
    copies = [pltpu.make_async_copy(x, y, sems.at[k]) for k, (x, y) in enumerate(pairs)]
    for copy in copies:
        copy.start()
    for copy in copies:
        copy.wait()


def start_kernel(psi, left, right, own, env, left_tile, sems):
    m = lax.axis_index("mpo")
    w_local, sec, dl, _ = left.shape
    dr = right.shape[3]
    rows = dl // 2
    takes = [pltpu.make_async_copy(psi.at[:, v], own.at[k], sems.at[k]) for k, v in enumerate((m ^ 4, m))]
    rights = [
        pltpu.make_async_copy(
            right.at[w], env.at[w * sec : (w + 1) * sec, 0:dr], sems.at[2 + w]
        )
        for w in range(w_local)
    ]
    load = pltpu.make_async_copy(left, left_tile, sems.at[2 + w_local])
    for copy in [*takes, load, *rights]:
        copy.start()
    load.wait()
    for w in range(w_local):
        tile = left_tile[w]
        env[w * sec : (w + 1) * sec, dr : dr + rows] = jnp.concatenate(
            [tile[:, :rows], tile[:, rows:]], axis=2
        )
    for copy in [*takes, *rights]:
        copy.wait()


def start(psi, left, right):
    w_local, sec, dl, _ = left.shape
    dr = right.shape[3]
    anywhere = pl.BlockSpec(memory_space=pltpu.HBM)
    return pl.pallas_call(
        start_kernel,
        out_shape=[
            jax.ShapeDtypeStruct((2, sec, dl, dr), BF),
            jax.ShapeDtypeStruct((w_local * sec, dr + dl // 2, dr), BF),
        ],
        in_specs=[anywhere] * 3,
        out_specs=[pl.BlockSpec(memory_space=pltpu.VMEM)] * 2,
        scratch_shapes=[
            pltpu.VMEM(left.shape, BF),
            pltpu.SemaphoreType.DMA((3 + w_local,)),
        ],
        compiler_params=pltpu.CompilerParams(vmem_limit_bytes=12 * 2**20),
        cost_estimate=pl.CostEstimate(flops=0, bytes_accessed=int(6e6), transcendentals=0),
    )(psi, left, right)


def line_kernel(*refs):
    *arrays, first, second, sems = refs
    size = arrays[0].shape[1]
    pairs = []
    for v, out in enumerate((first, second)):
        for k, x in enumerate(arrays):
            pairs.append((x.at[v], out.at[k * size : (k + 1) * size]))
    copy_all(pairs, sems)


def make_lines(arrays):
    _, size, dl, dr = arrays[0].shape
    out = jax.ShapeDtypeStruct((size * len(arrays), dl, dr), arrays[0].dtype)
    anywhere = pl.BlockSpec(memory_space=pl.ANY)
    return pl.pallas_call(
        line_kernel,
        out_shape=[out, out],
        in_specs=[anywhere] * len(arrays),
        out_specs=[pl.BlockSpec(memory_space=pltpu.VMEM)] * 2,
        scratch_shapes=[pltpu.SemaphoreType.DMA((2 * len(arrays),))],
        cost_estimate=pl.CostEstimate(flops=0, bytes_accessed=int(4e6), transcendentals=0),
    )(*arrays)


def per_device(psi, left_env, right_env, source, active):
    sec_local = psi.shape[0]
    m = lax.axis_index("mpo")
    sec = lax.axis_index("sec")
    dl, dr = psi.shape[2:]

    own, env = start(psi, left_env, right_env)
    up = over_all(own, A_UP)
    down = over_all(own, A_DOWN)
    across = over_all(own, A_TWO)

    env_core = over_mpo(env, CORE)
    masked = jnp.where(active > 0, source, -1)
    masked_apart = over_mpo(masked, X_APART)
    both = jnp.stack([masked, masked_apart])
    both_core = over_mpo(both, CORE)
    to_send, both = lax.optimization_barrier((env, both))
    env_apart = over_mpo(to_send, X_APART)

    across, env_core, both, both_core = lax.optimization_barrier((across, env_core, both, both_core))
    lines = make_lines([own, up, down, across])

    wanted = jnp.stack([both[0], both_core[0], both[1], both_core[1]])
    group, row = wanted // sec_local, wanted % sec_local
    from_z = (group // SIDE - sec // SIDE) % SIDE
    from_y = (group % SIDE - sec % SIDE) % SIDE
    first = jnp.where(m % 2 == 0, from_z, from_y)
    second = jnp.where(m % 2 == 0, from_y, from_z)
    slot = order(second) * SIDE + order(first)
    codes = jnp.where(wanted >= 0, slot * sec_local + row, -1)
    lists, counts = make_lists(codes.reshape(-1))

    lines_up = [over_all(line, B_UP) for line in lines]
    lines_down = [over_all(line, B_DOWN) for line in lines]
    lasts = [over_all(lines_up[0], B_UP), over_all(lines_down[1], B_DOWN)]
    env_apart, _, _, lists, counts = lax.optimization_barrier(
        (env_apart, lines_up[0], lines_down[1], lists, counts)
    )
    envs = [join([env, env_core]), env_apart, over_mpo(env_apart, CORE)]
    pieces = [[x[v] for x in (lines, lines_up, lines_down, lasts)] for v in range(2)]

    def added(v, rows, sums, kind=F32):
        return add_terms(rows, lists, counts, envs, [[pieces[v][k]] for k in rows], sums, sec_local, kind)

    (away,) = added(0, (2, 3), added(0, (0, 1), None), BF)
    arrived = over_mpo(away, FAR)
    (home,) = added(1, (1, 3), added(1, (0, 2), None))
    return (home + arrived.astype(F32)).astype(BF)[:, None]


def solution(mesh):
    placed = (
        P("sec", None, None, None),
        P("mpo", "sec", None, None),
        P("mpo", "sec", None, None),
        P("mpo", "sec"),
        P("mpo", "sec"),
    )
    return jax.shard_map(
        per_device,
        mesh=mesh,
        in_specs=placed,
        out_specs=P("sec", "mpo", None, None),
        check_vma=False,
    )
```

time: 329 us -> 88.2 us (0.27)
  waiting for transfers between devices: 201 us -> 20.6 us
  blocking collectives: 56.1 us -> 0 us
  local copies, waits for them, and re-layouts: 37.7 us -> 4.88 us
  Pallas kernels: 0 us -> 30.4 us
  starting transfers between devices: 0.01 us -> 27.6 us
  between operations: 13.4 us -> 0.18 us
  matrix products: 9.4 us -> 0 us
  other arithmetic: 9.15 us -> 3.72 us
    all_gather x1 -> x0, waiting for transfers between devices: 200 us -> none  [per_device(): piece = lax.all_gather(psi, 'sec', axis=0, tiled=True)]
    psum x1 -> x0, blocking collectives: 56.1 us -> none  [per_device(): summed = lax.psum(partial_value, 'mpo')]
    pallas_call x0 -> x8, Pallas kernels: none -> 30.4 us  [the longest x4 21.1 us: add_terms(): pl.pallas_call(functools.partial(term_kernel, rows, n_vec, len(envs), acc...]
    ppermute x0 -> x15, starting transfers between devices: none -> 27.6 us  [the longest x9 14.3 us: over_all(): return lax.ppermute(x, ('sec', 'mpo'), perm)]
    scatter x1 -> x0, local copies, waits for them, and re-layouts: 22.2 us -> none  [per_device(): needed = empty.at[targets].set(chosen, mode='drop')]
    ppermute x0 -> x15, waiting for transfers between devices: none -> 20.6 us  [the longest x9 14.2 us: over_all(): return lax.ppermute(x, ('sec', 'mpo'), perm)]
    dot_general x1 -> x0, matrix products: 9.4 us -> none  [per_device(): jnp.einsum('wsvac,wscd->wsvad', applied, right_env, preferred_element_typ...]
    gather x1 -> x0, local copies, waits for them, and re-layouts: 7.6 us -> none  [per_device(): chosen = jnp.take(piece, rows_wanted, axis=0)]
  transfers between devices with their start and end apart: 1 -> 15, of which waited for: 1 -> 7; matrix products, arithmetic and copies ran while one was open for 1% -> 4% of each run, Pallas kernels for 0% -> 32%
where the time goes in v2:
time: 88.2 us; the launch traced here: 87.4 us
  Pallas kernels  30.4 us (34%)
  starting transfers between devices  27.6 us (31%)
  waiting for transfers between devices  20.6 us (23%)
  local copies, waits for them, and re-layouts  4.88 us (6%)
  other arithmetic  3.72 us (4%)
    pallas_call x4, Pallas kernels, add_terms(): pl.pallas_call(functools.partial(term_kernel, rows, n_vec, len(envs), acc...  21.1 us
    ppermute x9, starting transfers between devices, over_all(): return lax.ppermute(x, ('sec', 'mpo'), perm)  14.3 us
    ppermute x9, waiting for transfers between devices, over_all(): return lax.ppermute(x, ('sec', 'mpo'), perm)  14.2 us
    ppermute x6, starting transfers between devices, over_mpo(): return lax.ppermute(x, 'mpo', perm)  13.3 us
    ppermute x6, waiting for transfers between devices, over_mpo(): return lax.ppermute(x, 'mpo', perm)  6.36 us
    unnamed x18, local copies, waits for them, and re-layouts  4.43 us
    pallas_call x1, Pallas kernels, make_lines(): pl.pallas_call(line_kernel, out_shape=[out, out], in_specs=[anywhere] * l...  2.95 us
    pallas_call x1, Pallas kernels, join(): pl.pallas_call(join_kernel, out_shape=jax.ShapeDtypeStruct((first.shape[0...  2.55 us
  transfers between devices with their start and end apart: 15, of which 7 were waited for; matrix products, arithmetic and copies ran while one was open for 4% of the time, Pallas kernels for 32%

profile of v2, /device:TPU:1, one launch (start us, length us, event | category | flops | bytes accessed | tf_op | source)
XLA Modules:
  0.0 87.4 jit_solution(6762049971167059505)
XLA Ops:
  0.0 1.6 %copy-done = bf16[16,8,64,128]{3,2,1,0:T(8,128)(2,1)S(1)} copy-done((bf16[16,8,64,128]{3,2,1,0:T(8,128)(2,1)S(1)}, bf16[16,8,64,128]{3,2,1,0:T(8,128)(2,1)}, u32[]{:S(2)}) %copy-start) | copy-done | bytes 2097176
  1.6 1.6 %copy-done.1 = bf16[4,16,128,128]{3,2,1,0:T(8,128)(2,1)S(1)} copy-done((bf16[4,16,128,128]{3,2,1,0:T(8,128)(2,1)S(1)}, bf16[4,16,128,128]{3,2,1,0:T(8,128)(2,1)}, u32[]{:S(2)}) %copy-start.1) | copy-done | bytes 2097176
  3.2 1.2 %copy-done.2 = bf16[4,16,64,64]{3,2,1,0:T(8,128)(2,1)S(1)} copy-done((bf16[4,16,64,64]{3,2,1,0:T(8,128)(2,1)S(1)}, bf16[4,16,64,64]{3,2,1,0:T(8,128)(2,1)}, u32[]{:S(2)}) %copy-start.2) | copy-done | bytes 524312
  4.4 2.0 %shard_map.55 = (bf16[2,16,64,128]{3,2,1,0:T(8,128)(2,1)S(1)}, bf16[64,160,128]{2,1,0:T(8,128)(2,1)}) custom-call(bf16[16,8,64,128]{3,2,1,0:T(8,128)(2,1)S(1)} %copy-done, bf16[4,16,64,64]{3,2,1,0:T(8,128)(2,1)S(1)} %copy-done.2, bf16[4,16,128,128]{3,2,1,0:T(8,128)(2,1)S(1)} %copy-done.1), custom_call_target="tpu_custom_call" | custom-call | bytes 6000000 | tf_op jit(solution)/shard_map/pallas_call | solution.py:225
  6.5 1.5 %collective-permute-start.5 = (bf16[64,160,128]{2,1,0:T(8,128)(2,1)}, bf16[64,160,128]{2,1,0:T(8,128)(2,1)}, u32[]{:S(2)}, u32[]{:S(2)}) collective-permute-start(bf16[64,160,128]{2,1,0:T(8,128)(2,1)} %get-tuple-element.19.refs_0_), channel_id=1, source_target_pairs={{0,1},{1,0},{2,3},{3,2},{4,5},{5,4},{6,7},{7,6},{8,9},{9,8},{10,11... | collective-permute-start | bytes 7864328 | tf_op jit(solution)/shard_map/ppermute | solution.py:50
  8.0 1.4 %collective-permute-start = (s32[4,16]{1,0:T(4,128)S(1)}, s32[4,16]{1,0:T(4,128)S(1)}, u32[]{:S(2)}, u32[]{:S(2)}) collective-permute-start(s32[4,16]{1,0:T(4,128)S(1)} %compare_select_fusion.24), channel_id=1, source_target_pairs={{0,6},{1,3},{2,0},{3,5},{4,2},{5,7},{6,4},{7,1},{8,14},{9,11},{10,... | collective-permute-start | bytes 776 | tf_op jit(solution)/shard_map/ppermute | solution.py:50
  9.3 2.4 %collective-permute-done = s32[4,16]{1,0:T(4,128)S(1)} collective-permute-done((s32[4,16]{1,0:T(4,128)S(1)}, s32[4,16]{1,0:T(4,128)S(1)}, u32[]{:S(2)}, u32[]{:S(2)}) %collective-permute-start) | collective-permute-done | bytes 288 | tf_op jit(solution)/shard_map/ppermute | solution.py:50
  11.7 0.1 collective-permute-start.1
  11.8 3.0 %collective-permute-start.4 = (bf16[2,16,64,128]{3,2,1,0:T(8,128)(2,1)S(1)}, bf16[2,16,64,128]{3,2,1,0:T(8,128)(2,1)}, u32[]{:S(2)}, u32[]{:S(2)}) collective-permute-start(bf16[2,16,64,128]{3,2,1,0:T(8,128)(2,1)S(1)} %get-tuple-element.20.refs_0_), channel_id=1, source_target_pairs={{0,64},{1,17},{2,66},{3,19},{4,68},{5,21},{6,70},{7,23},{8,72},{9,... | collective-permute-start | bytes 1572872 | tf_op jit(solution)/shard_map/ppermute | solution.py:46
  14.8 4.8 %collective-permute-start.6 = (s32[2,4,16]{2,1,0:T(4,128)S(1)}, s32[2,4,16]{2,1,0:T(4,128)S(1)}, u32[]{:S(2)}, u32[]{:S(2)}) collective-permute-start(s32[2,4,16]{2,1,0:T(4,128)S(1)} %pad_add_fusion.1), channel_id=1, source_target_pairs={{0,1},{1,0},{2,3},{3,2},{4,5},{5,4},{6,7},{7,6},{8,9},{9,8},{10,11... | collective-permute-start | bytes 1544 | tf_op jit(solution)/shard_map/ppermute | solution.py:50
  19.6 1.3 %collective-permute-start.2 = (bf16[2,16,64,128]{3,2,1,0:T(8,128)(2,1)S(1)}, bf16[2,16,64,128]{3,2,1,0:T(8,128)(2,1)}, u32[]{:S(2)}, u32[]{:S(2)}) collective-permute-start(bf16[2,16,64,128]{3,2,1,0:T(8,128)(2,1)S(1)} %get-tuple-element.20.refs_0_), channel_id=1, source_target_pairs={{0,32},{1,9},{2,34},{3,11},{4,36},{5,13},{6,38},{7,15},{8,40},{9,1... | collective-permute-start | bytes 1572872 | tf_op jit(solution)/shard_map/ppermute | solution.py:46
  20.9 2.3 %collective-permute-start.3 = (bf16[2,16,64,128]{3,2,1,0:T(8,128)(2,1)S(1)}, bf16[2,16,64,128]{3,2,1,0:T(8,128)(2,1)}, u32[]{:S(2)}, u32[]{:S(2)}) collective-permute-start(bf16[2,16,64,128]{3,2,1,0:T(8,128)(2,1)S(1)} %get-tuple-element.20.refs_0_), channel_id=1, source_target_pairs={{0,96},{1,25},{2,98},{3,27},{4,100},{5,29},{6,102},{7,31},{8,104},... | collective-permute-start | bytes 1572872 | tf_op jit(solution)/shard_map/ppermute | solution.py:46
  23.1 0.0 collective-permute-done.4.refs_3_
  23.2 0.0 collective-permute-done.5.refs_1_
  23.2 0.1 stack.21
  23.3 0.1 stack.20
  23.3 5.9 %collective-permute-done.2.refs_1_ = bf16[2,16,64,128]{3,2,1,0:T(8,128)(2,1)} collective-permute-done((bf16[2,16,64,128]{3,2,1,0:T(8,128)(2,1)S(1)}, bf16[2,16,64,128]{3,2,1,0:T(8,128)(2,1)}, u32[]{:S(2)}, u32[]{:S(2)}) %collective-permute-start.2) | collective-permute-done | bytes 524320 | tf_op jit(solution)/shard_map/ppermute | solution.py:46
  29.3 0.0 collective-permute-done.3.refs_2_
  29.3 3.0 %shard_map.56 = (bf16[64,64,128]{2,1,0:T(8,128)(2,1)}, bf16[64,64,128]{2,1,0:T(8,128)(2,1)}) custom-call(bf16[2,16,64,128]{3,2,1,0:T(8,128)(2,1)} %copy-done.5, bf16[2,16,64,128]{3,2,1,0:T(8,128)(2,1)} %collective-permute-done.2.refs_1_, bf16[2,16,64,128]{3,2,1,0:T(8,128)(2,1)} %collective-permute-done.3.refs_2_, ...), custom_call_target="tpu_custom_call" | custom-call | bytes 4000000 | tf_op jit(solution)/shard_map/pallas_call | solution.py:256
  32.3 0.8 collective-permute-start.7
  33.1 1.9 %collective-permute-start.8 = (bf16[64,64,128]{2,1,0:T(8,128)(2,1)}, bf16[64,64,128]{2,1,0:T(8,128)(2,1)}, u32[]{:S(2)}, u32[]{:S(2)}) collective-permute-start(bf16[64,64,128]{2,1,0:T(8,128)(2,1)} %get-tuple-element.24.refs_3_), channel_id=1, source_target_pairs={{0,24},{1,97},{2,26},{3,99},{4,28},{5,101},{6,30},{7,103},{8,0},{9... | collective-permute-start | bytes 3145736 | tf_op jit(solution)/shard_map/ppermute | solution.py:46
  35.1 1.5 %reduce-window.6 = s32[5,2,128]{2,1,0:T(2,128)S(1)} reduce-window(s32[5,2,128]{2,1,0:T(2,128)S(1)} %fusion.1, s32[]{:T(128)} %constant.126.clone.1), window={size=1x1x128 pad=0_0x0_0x127_0}, to_apply=%region_0.1 | reduce-window | flops 162560 | bytes 10244 | tf_op jit(solution)/shard_map/reduce-window
  36.6 0.1 slice.24
  36.7 0.1 copy.9
  36.8 0.1 copy.10
  36.9 0.1 select_reduce_fusion
  37.0 0.6 fusion.13
  37.6 0.5 bitcast_add_fusion
  38.1 1.7 %shard_map.57.list_ref = s32[1280]{0:T(1024)} custom-call(s32[256]{0:T(256)} %get-tuple-element.33.place_ref, s32[256]{0:T(256)} %get-tuple-element.31.entry_ref), custom_call_target="tpu_custom_call" | custom-call | tf_op jit(solution)/shard_map/pallas_call | solution.py:73
  39.9 0.1 convert_reduce_fusion.count_ref
  40.0 0.0 copy-start.6
  40.0 4.0 %collective-permute-done.1.refs_1_ = bf16[64,160,128]{2,1,0:T(8,128)(2,1)S(1)} collective-permute-done((bf16[64,160,128]{2,1,0:T(8,128)(2,1)}, bf16[64,160,128]{2,1,0:T(8,128)(2,1)S(1)}, u32[]{:S(2)}, u32[]{:S(2)}) %collective-permute-start.1) | collective-permute-done | bytes 2621472 | tf_op jit(solution)/shard_map/ppermute | solution.py:50
  44.0 3.8 %collective-permute-done.7.refs_4_ = bf16[64,64,128]{2,1,0:T(8,128)(2,1)} collective-permute-done((bf16[64,64,128]{2,1,0:T(8,128)(2,1)}, bf16[64,64,128]{2,1,0:T(8,128)(2,1)}, u32[]{:S(2)}, u32[]{:S(2)}) %collective-permute-start.7) | collective-permute-done | bytes 1048608 | tf_op jit(solution)/shard_map/ppermute | solution.py:46
  47.8 0.0 collective-permute-done.8.refs_4_
  47.8 5.4 %collective-permute-start.9 = (bf16[64,160,128]{2,1,0:T(8,128)(2,1)S(1)}, bf16[64,160,128]{2,1,0:T(8,128)(2,1)S(1)}, u32[]{:S(2)}, u32[]{:S(2)}) collective-permute-start(bf16[64,160,128]{2,1,0:T(8,128)(2,1)S(1)} %collective-permute-done.1.refs_1_), channel_id=1, source_target_pairs={{0,1},{1,0},{2,3},{3,2},{4,5},{5,4},{6,7},{7,6},{8,9},{9,8},{10,11... | collective-permute-start | bytes 7864328 | tf_op jit(solution)/shard_map/ppermute | solution.py:50
  53.3 2.3 %collective-permute-start.12 = (bf16[64,64,128]{2,1,0:T(8,128)(2,1)}, bf16[64,64,128]{2,1,0:T(8,128)(2,1)S(1)}, u32[]{:S(2)}, u32[]{:S(2)}) collective-permute-start(bf16[64,64,128]{2,1,0:T(8,128)(2,1)} %get-tuple-element.23.refs_3_), channel_id=1, source_target_pairs={{0,24},{1,97},{2,26},{3,99},{4,28},{5,101},{6,30},{7,103},{8,0},{9... | collective-permute-start | bytes 3145736 | tf_op jit(solution)/shard_map/ppermute | solution.py:46
  55.6 0.0 collective-permute-start.13
  55.6 2.7 %collective-permute-start.11 = (bf16[64,64,128]{2,1,0:T(8,128)(2,1)}, bf16[64,64,128]{2,1,0:T(8,128)(2,1)S(1)}, u32[]{:S(2)}, u32[]{:S(2)}) collective-permute-start(bf16[64,64,128]{2,1,0:T(8,128)(2,1)} %collective-permute-done.8.refs_4_), channel_id=1, source_target_pairs={{0,24},{1,97},{2,26},{3,99},{4,28},{5,101},{6,30},{7,103},{8,0},{9... | collective-permute-start | bytes 3145736 | tf_op jit(solution)/shard_map/ppermute | solution.py:46
  58.3 2.5 %shard_map.58.refs_0_ = bf16[128,160,128]{2,1,0:T(8,128)(2,1)S(1)} custom-call(bf16[64,160,128]{2,1,0:T(8,128)(2,1)} %get-tuple-element.19.refs_0_, bf16[64,160,128]{2,1,0:T(8,128)(2,1)} %collective-permute-done.5.refs_1_), custom_call_target="tpu_custom_call" | custom-call | bytes 10000000 | tf_op jit(solution)/shard_map/pallas_call | solution.py:177
  60.9 6.2 %shard_map.61.refs_5_ = f32[16,64,128]{2,1,0:T(8,128)S(1)} custom-call(s32[1280]{0:T(1024)S(1)} %copy-done.6, s32[5]{0:T(128)S(1)} %convert_reduce_fusion.count_ref, bf16[128,160,128]{2,1,0:T(8,128)(2,1)S(1)} %shard_map.58.refs_0_, bf16[64,160,128]{2,1,0:T(8,128)(2,1)S(1)} %collective-permute-done.1.refs_1_, ...), custom_call_target="tpu_custom_call" | custom-call | flops 3000000000 | bytes 12000000 | tf_op jit(solution)/shard_map/pallas_call | solution.py:150
  67.1 0.5 collective-permute-done.12.refs_3_
  67.7 3.3 %collective-permute-done.13.refs_4_ = bf16[64,64,128]{2,1,0:T(8,128)(2,1)S(1)} collective-permute-done((bf16[64,64,128]{2,1,0:T(8,128)(2,1)}, bf16[64,64,128]{2,1,0:T(8,128)(2,1)S(1)}, u32[]{:S(2)}, u32[]{:S(2)}) %collective-permute-start.13) | collective-permute-done | bytes 1048608 | tf_op jit(solution)/shard_map/ppermute | solution.py:46
  71.0 4.3 %shard_map.62 = bf16[16,64,128]{2,1,0:T(8,128)(2,1)S(1)} custom-call(s32[1280]{0:T(1024)S(1)} %copy-done.6, s32[5]{0:T(128)S(1)} %convert_reduce_fusion.count_ref, bf16[128,160,128]{2,1,0:T(8,128)(2,1)S(1)} %shard_map.58.refs_0_, bf16[64,160,128]{2,1,0:T(8,128)(2,1)S(1)} %collective-permute-done.1.refs_1_, ...), custom_call_target="tpu_custom_call" | custom-call | flops 3000000000 | bytes 12000000 | tf_op jit(solution)/shard_map/pallas_call | solution.py:150
  75.3 0.1 collective-permute-start.14
  75.4 6.2 %shard_map.59.refs_5_ = f32[16,64,128]{2,1,0:T(8,128)S(1)} custom-call(s32[1280]{0:T(1024)S(1)} %copy-done.6, s32[5]{0:T(128)S(1)} %convert_reduce_fusion.count_ref, bf16[128,160,128]{2,1,0:T(8,128)(2,1)S(1)} %shard_map.58.refs_0_, bf16[64,160,128]{2,1,0:T(8,128)(2,1)S(1)} %collective-permute-done.1.refs_1_, ...), custom_call_target="tpu_custom_call" | custom-call | flops 3000000000 | bytes 12000000 | tf_op jit(solution)/shard_map/pallas_call | solution.py:150
  81.6 0.6 collective-permute-done.10.refs_3_
  82.2 4.4 %shard_map.60 = f32[16,64,128]{2,1,0:T(8,128)S(1)} custom-call(s32[1280]{0:T(1024)S(1)} %copy-done.6, s32[5]{0:T(128)S(1)} %convert_reduce_fusion.count_ref, bf16[128,160,128]{2,1,0:T(8,128)(2,1)S(1)} %shard_map.58.refs_0_, bf16[64,160,128]{2,1,0:T(8,128)(2,1)S(1)} %collective-permute-done.1.refs_1_, ...), custom_call_target="tpu_custom_call" | custom-call | flops 3000000000 | bytes 12000000 | tf_op jit(solution)/shard_map/pallas_call | solution.py:150
  86.6 0.8 fusion
  (27 shorter events, 0.1 us)
Async XLA Ops:
  0.0 1.6 %copy-start = (bf16[16,8,64,128]{3,2,1,0:T(8,128)(2,1)S(1)}, bf16[16,8,64,128]{3,2,1,0:T(8,128)(2,1)}, u32[]{:S(2)}) copy-start(bf16[16,8,64,128]{3,2,1,0:T(8,128)(2,1)} %psi.1) | copy-start | bytes 6291460
  1.6 1.6 %copy-start.1 = (bf16[4,16,128,128]{3,2,1,0:T(8,128)(2,1)S(1)}, bf16[4,16,128,128]{3,2,1,0:T(8,128)(2,1)}, u32[]{:S(2)}) copy-start(bf16[4,16,128,128]{3,2,1,0:T(8,128)(2,1)} %right.1) | copy-start | bytes 6291460
  3.2 1.2 %copy-start.2 = (bf16[4,16,64,64]{3,2,1,0:T(8,128)(2,1)S(1)}, bf16[4,16,64,64]{3,2,1,0:T(8,128)(2,1)}, u32[]{:S(2)}) copy-start(bf16[4,16,64,64]{3,2,1,0:T(8,128)(2,1)} %left.1) | copy-start | bytes 1572868
  4.4 3.5 %copy-start.7 = (s32[4,16]{1,0:T(4,128)S(1)}, s32[4,16]{1,0:T(4,128)}, u32[]{:S(2)}) copy-start(s32[4,16]{1,0:T(4,128)} %param.8) | copy-start | bytes 772
  4.4 3.5 %copy-start.8 = (s32[4,16]{1,0:T(4,128)S(1)}, s32[4,16]{1,0:T(4,128)}, u32[]{:S(2)}) copy-start(s32[4,16]{1,0:T(4,128)} %param.9) | copy-start | bytes 772
  6.4 22.9 %copy-start.5 = (bf16[2,16,64,128]{3,2,1,0:T(8,128)(2,1)}, bf16[2,16,64,128]{3,2,1,0:T(8,128)(2,1)S(1)}, u32[]{:S(2)}) copy-start(bf16[2,16,64,128]{3,2,1,0:T(8,128)(2,1)S(1)} %get-tuple-element.20.refs_0_) | copy-start | bytes 1572868
  6.5 16.7 %collective-permute-start.5 = (bf16[64,160,128]{2,1,0:T(8,128)(2,1)}, bf16[64,160,128]{2,1,0:T(8,128)(2,1)}, u32[]{:S(2)}, u32[]{:S(2)}) collective-permute-start(bf16[64,160,128]{2,1,0:T(8,128)(2,1)} %get-tuple-element.19.refs_0_), channel_id=1, source_target_pairs={{0,1},{1,0},{2,3},{3,2},{4,5},{5,4},{6,7},{7,6},{8,9},{9,8},{10,11... | collective-permute-start | bytes 7864328 | tf_op jit(solution)/shard_map/ppermute | solution.py:50
  8.0 3.7 %collective-permute-start = (s32[4,16]{1,0:T(4,128)S(1)}, s32[4,16]{1,0:T(4,128)S(1)}, u32[]{:S(2)}, u32[]{:S(2)}) collective-permute-start(s32[4,16]{1,0:T(4,128)S(1)} %compare_select_fusion.24), channel_id=1, source_target_pairs={{0,6},{1,3},{2,0},{3,5},{4,2},{5,7},{6,4},{7,1},{8,14},{9,11},{10,... | collective-permute-start | bytes 776 | tf_op jit(solution)/shard_map/ppermute | solution.py:50
  11.7 32.3 %collective-permute-start.1 = (bf16[64,160,128]{2,1,0:T(8,128)(2,1)}, bf16[64,160,128]{2,1,0:T(8,128)(2,1)S(1)}, u32[]{:S(2)}, u32[]{:S(2)}) collective-permute-start(bf16[64,160,128]{2,1,0:T(8,128)(2,1)} %get-tuple-element.19.refs_0_), channel_id=1, source_target_pairs={{0,6},{1,3},{2,0},{3,5},{4,2},{5,7},{6,4},{7,1},{8,14},{9,11},{10,... | collective-permute-start | bytes 7864328 | tf_op jit(solution)/shard_map/ppermute | solution.py:50
  11.8 11.4 %collective-permute-start.4 = (bf16[2,16,64,128]{3,2,1,0:T(8,128)(2,1)S(1)}, bf16[2,16,64,128]{3,2,1,0:T(8,128)(2,1)}, u32[]{:S(2)}, u32[]{:S(2)}) collective-permute-start(bf16[2,16,64,128]{3,2,1,0:T(8,128)(2,1)S(1)} %get-tuple-element.20.refs_0_), channel_id=1, source_target_pairs={{0,64},{1,17},{2,66},{3,19},{4,68},{5,21},{6,70},{7,23},{8,72},{9,... | collective-permute-start | bytes 1572872 | tf_op jit(solution)/shard_map/ppermute | solution.py:46
  14.8 6.1 %collective-permute-start.6 = (s32[2,4,16]{2,1,0:T(4,128)S(1)}, s32[2,4,16]{2,1,0:T(4,128)S(1)}, u32[]{:S(2)}, u32[]{:S(2)}) collective-permute-start(s32[2,4,16]{2,1,0:T(4,128)S(1)} %pad_add_fusion.1), channel_id=1, source_target_pairs={{0,1},{1,0},{2,3},{3,2},{4,5},{5,4},{6,7},{7,6},{8,9},{9,8},{10,11... | collective-permute-start | bytes 1544 | tf_op jit(solution)/shard_map/ppermute | solution.py:50
  19.6 9.7 %collective-permute-start.2 = (bf16[2,16,64,128]{3,2,1,0:T(8,128)(2,1)S(1)}, bf16[2,16,64,128]{3,2,1,0:T(8,128)(2,1)}, u32[]{:S(2)}, u32[]{:S(2)}) collective-permute-start(bf16[2,16,64,128]{3,2,1,0:T(8,128)(2,1)S(1)} %get-tuple-element.20.refs_0_), channel_id=1, source_target_pairs={{0,32},{1,9},{2,34},{3,11},{4,36},{5,13},{6,38},{7,15},{8,40},{9,1... | collective-permute-start | bytes 1572872 | tf_op jit(solution)/shard_map/ppermute | solution.py:46
  20.9 8.4 %collective-permute-start.3 = (bf16[2,16,64,128]{3,2,1,0:T(8,128)(2,1)S(1)}, bf16[2,16,64,128]{3,2,1,0:T(8,128)(2,1)}, u32[]{:S(2)}, u32[]{:S(2)}) collective-permute-start(bf16[2,16,64,128]{3,2,1,0:T(8,128)(2,1)S(1)} %get-tuple-element.20.refs_0_), channel_id=1, source_target_pairs={{0,96},{1,25},{2,98},{3,27},{4,100},{5,29},{6,102},{7,31},{8,104},... | collective-permute-start | bytes 1572872 | tf_op jit(solution)/shard_map/ppermute | solution.py:46
  32.3 15.5 %collective-permute-start.7 = (bf16[64,64,128]{2,1,0:T(8,128)(2,1)}, bf16[64,64,128]{2,1,0:T(8,128)(2,1)}, u32[]{:S(2)}, u32[]{:S(2)}) collective-permute-start(bf16[64,64,128]{2,1,0:T(8,128)(2,1)} %get-tuple-element.23.refs_3_), channel_id=1, source_target_pairs={{0,8},{1,33},{2,10},{3,35},{4,12},{5,37},{6,14},{7,39},{8,16},{9,4... | collective-permute-start | bytes 3145736 | tf_op jit(solution)/shard_map/ppermute | solution.py:46
  33.1 14.7 %collective-permute-start.8 = (bf16[64,64,128]{2,1,0:T(8,128)(2,1)}, bf16[64,64,128]{2,1,0:T(8,128)(2,1)}, u32[]{:S(2)}, u32[]{:S(2)}) collective-permute-start(bf16[64,64,128]{2,1,0:T(8,128)(2,1)} %get-tuple-element.24.refs_3_), channel_id=1, source_target_pairs={{0,24},{1,97},{2,26},{3,99},{4,28},{5,101},{6,30},{7,103},{8,0},{9... | collective-permute-start | bytes 3145736 | tf_op jit(solution)/shard_map/ppermute | solution.py:46
  40.0 20.9 %copy-start.4 = (bf16[64,64,128]{2,1,0:T(8,128)(2,1)S(1)}, bf16[64,64,128]{2,1,0:T(8,128)(2,1)}, u32[]{:S(2)}) copy-start(bf16[64,64,128]{2,1,0:T(8,128)(2,1)} %get-tuple-element.23.refs_3_) | copy-start | bytes 3145732
  40.0 20.9 %copy-start.6 = (s32[1280]{0:T(1024)S(1)}, s32[1280]{0:T(1024)}, u32[]{:S(2)}) copy-start(s32[1280]{0:T(1024)} %shard_map.57.list_ref) | copy-start | bytes 15364
  47.8 13.0 %collective-permute-start.9 = (bf16[64,160,128]{2,1,0:T(8,128)(2,1)S(1)}, bf16[64,160,128]{2,1,0:T(8,128)(2,1)S(1)}, u32[]{:S(2)}, u32[]{:S(2)}) collective-permute-start(bf16[64,160,128]{2,1,0:T(8,128)(2,1)S(1)} %collective-permute-done.1.refs_1_), channel_id=1, source_target_pairs={{0,1},{1,0},{2,3},{3,2},{4,5},{5,4},{6,7},{7,6},{8,9},{9,8},{10,11... | collective-permute-start | bytes 7864328 | tf_op jit(solution)/shard_map/ppermute | solution.py:50
  53.3 14.4 %collective-permute-start.12 = (bf16[64,64,128]{2,1,0:T(8,128)(2,1)}, bf16[64,64,128]{2,1,0:T(8,128)(2,1)S(1)}, u32[]{:S(2)}, u32[]{:S(2)}) collective-permute-start(bf16[64,64,128]{2,1,0:T(8,128)(2,1)} %get-tuple-element.23.refs_3_), channel_id=1, source_target_pairs={{0,24},{1,97},{2,26},{3,99},{4,28},{5,101},{6,30},{7,103},{8,0},{9... | collective-permute-start | bytes 3145736 | tf_op jit(solution)/shard_map/ppermute | solution.py:46
  55.6 15.4 %collective-permute-start.13 = (bf16[64,64,128]{2,1,0:T(8,128)(2,1)}, bf16[64,64,128]{2,1,0:T(8,128)(2,1)S(1)}, u32[]{:S(2)}, u32[]{:S(2)}) collective-permute-start(bf16[64,64,128]{2,1,0:T(8,128)(2,1)} %collective-permute-done.7.refs_4_), channel_id=1, source_target_pairs={{0,8},{1,33},{2,10},{3,35},{4,12},{5,37},{6,14},{7,39},{8,16},{9,4... | collective-permute-start | bytes 3145736 | tf_op jit(solution)/shard_map/ppermute | solution.py:46
  55.6 26.6 %collective-permute-start.10 = (bf16[64,64,128]{2,1,0:T(8,128)(2,1)}, bf16[64,64,128]{2,1,0:T(8,128)(2,1)S(1)}, u32[]{:S(2)}, u32[]{:S(2)}) collective-permute-start(bf16[64,64,128]{2,1,0:T(8,128)(2,1)} %get-tuple-element.24.refs_3_), channel_id=1, source_target_pairs={{0,8},{1,33},{2,10},{3,35},{4,12},{5,37},{6,14},{7,39},{8,16},{9,4... | collective-permute-start | bytes 3145736 | tf_op jit(solution)/shard_map/ppermute | solution.py:46
  55.6 26.6 %collective-permute-start.11 = (bf16[64,64,128]{2,1,0:T(8,128)(2,1)}, bf16[64,64,128]{2,1,0:T(8,128)(2,1)S(1)}, u32[]{:S(2)}, u32[]{:S(2)}) collective-permute-start(bf16[64,64,128]{2,1,0:T(8,128)(2,1)} %collective-permute-done.8.refs_4_), channel_id=1, source_target_pairs={{0,24},{1,97},{2,26},{3,99},{4,28},{5,101},{6,30},{7,103},{8,0},{9... | collective-permute-start | bytes 3145736 | tf_op jit(solution)/shard_map/ppermute | solution.py:46
  67.1 8.3 %copy-start.3 = (bf16[64,64,128]{2,1,0:T(8,128)(2,1)S(1)}, bf16[64,64,128]{2,1,0:T(8,128)(2,1)}, u32[]{:S(2)}) copy-start(bf16[64,64,128]{2,1,0:T(8,128)(2,1)} %get-tuple-element.24.refs_3_) | copy-start | bytes 3145732
  75.3 11.3 %collective-permute-start.14 = (bf16[16,64,128]{2,1,0:T(8,128)(2,1)S(1)}, bf16[16,64,128]{2,1,0:T(8,128)(2,1)S(1)}, u32[]{:S(2)}, u32[]{:S(2)}) collective-permute-start(bf16[16,64,128]{2,1,0:T(8,128)(2,1)S(1)} %shard_map.62), channel_id=1, source_target_pairs={{0,4},{1,5},{2,6},{3,7},{4,0},{5,1},{6,2},{7,3},{8,12},{9,13},{10,... | collective-permute-start | bytes 786440 | tf_op jit(solution)/shard_map/ppermute | solution.py:50

commit v3 on v2

--- a/solution.py
+++ b/solution.py
@@ -185,81 +185,28 @@
     )(*arrays)
 
 
-def copy_all(pairs, sems):
-    copies = [pltpu.make_async_copy(x, y, sems.at[k]) for k, (x, y) in enumerate(pairs)]
-    for copy in copies:
-        copy.start()
-    for copy in copies:
-        copy.wait()
-
-
-def start_kernel(psi, left, right, own, env, left_tile, sems):
-    m = lax.axis_index("mpo")
-    w_local, sec, dl, _ = left.shape
-    dr = right.shape[3]
-    rows = dl // 2
-    takes = [pltpu.make_async_copy(psi.at[:, v], own.at[k], sems.at[k]) for k, v in enumerate((m ^ 4, m))]
-    rights = [
-        pltpu.make_async_copy(
-            right.at[w], env.at[w * sec : (w + 1) * sec, 0:dr], sems.at[2 + w]
-        )
-        for w in range(w_local)
-    ]
-    load = pltpu.make_async_copy(left, left_tile, sems.at[2 + w_local])
-    for copy in [*takes, load, *rights]:
-        copy.start()
-    load.wait()
-    for w in range(w_local):
-        tile = left_tile[w]
-        env[w * sec : (w + 1) * sec, dr : dr + rows] = jnp.concatenate(
-            [tile[:, :rows], tile[:, rows:]], axis=2
-        )
-    for copy in [*takes, *rights]:
-        copy.wait()
-
-
-def start(psi, left, right):
-    w_local, sec, dl, _ = left.shape
-    dr = right.shape[3]
-    anywhere = pl.BlockSpec(memory_space=pltpu.HBM)
-    return pl.pallas_call(
-        start_kernel,
-        out_shape=[
-            jax.ShapeDtypeStruct((2, sec, dl, dr), BF),
-            jax.ShapeDtypeStruct((w_local * sec, dr + dl // 2, dr), BF),
-        ],
-        in_specs=[anywhere] * 3,
-        out_specs=[pl.BlockSpec(memory_space=pltpu.VMEM)] * 2,
-        scratch_shapes=[
-            pltpu.VMEM(left.shape, BF),
-            pltpu.SemaphoreType.DMA((3 + w_local,)),
-        ],
-        compiler_params=pltpu.CompilerParams(vmem_limit_bytes=12 * 2**20),
-        cost_estimate=pl.CostEstimate(flops=0, bytes_accessed=int(6e6), transcendentals=0),
-    )(psi, left, right)
-
-
 def line_kernel(*refs):
-    *arrays, first, second, sems = refs
+    *arrays, first, second = refs
     size = arrays[0].shape[1]
-    pairs = []
     for v, out in enumerate((first, second)):
         for k, x in enumerate(arrays):
-            pairs.append((x.at[v], out.at[k * size : (k + 1) * size]))
-    copy_all(pairs, sems)
+            out[k * size : (k + 1) * size] = x[v]
 
 
 def make_lines(arrays):
     _, size, dl, dr = arrays[0].shape
-    out = jax.ShapeDtypeStruct((size * len(arrays), dl, dr), arrays[0].dtype)
-    anywhere = pl.BlockSpec(memory_space=pl.ANY)
+    blocks = size * len(arrays)
+    vmem = pl.BlockSpec(memory_space=pltpu.VMEM)
     return pl.pallas_call(
         line_kernel,
-        out_shape=[out, out],
-        in_specs=[anywhere] * len(arrays),
-        out_specs=[pl.BlockSpec(memory_space=pltpu.VMEM)] * 2,
-        scratch_shapes=[pltpu.SemaphoreType.DMA((2 * len(arrays),))],
-        cost_estimate=pl.CostEstimate(flops=0, bytes_accessed=int(4e6), transcendentals=0),
+        out_shape=[
+            jax.ShapeDtypeStruct(shape, BF)
+            for shape in ((blocks, dl, dr), (blocks, dl, dr))
+        ],
+        in_specs=[vmem] * len(arrays),
+        out_specs=[vmem] * 2,
+        compiler_params=pltpu.CompilerParams(vmem_limit_bytes=12 * 2**20),
+        cost_estimate=pl.CostEstimate(flops=int(7e+09), bytes_accessed=int(4e6), transcendentals=0),
     )(*arrays)
 
 
@@ -269,11 +216,14 @@
     sec = lax.axis_index("sec")
     dl, dr = psi.shape[2:]
 
-    own, env = start(psi, left_env, right_env)
+    own = jnp.stack([lax.dynamic_slice_in_dim(psi, v, 1, 1)[:, 0] for v in (m ^ 4, m)])
     up = over_all(own, A_UP)
     down = over_all(own, A_DOWN)
     across = over_all(own, A_TWO)
 
+    rows = dl // 2
+    packed = jnp.concatenate([left_env[:, :, :rows], left_env[:, :, rows:]], axis=3)
+    env = jnp.concatenate([right_env, packed], axis=2).reshape(-1, dr + rows, dr)
     env_core = over_mpo(env, CORE)
     masked = jnp.where(active > 0, source, -1)
     masked_apart = over_mpo(masked, X_APART)

time: 88.2 us -> 82.8 us (0.939)
  waiting for transfers between devices: 20.6 us -> 17.1 us
  other arithmetic: 3.72 us -> 5.77 us
  local copies, waits for them, and re-layouts: 4.88 us -> 3.43 us
  starting transfers between devices: 27.6 us -> 26.2 us
  Pallas kernels: 30.4 us -> 29.5 us
    ppermute x9, waiting for transfers between devices: 14.2 us -> 9.35 us  [over_all(): return lax.ppermute(x, ('sec', 'mpo'), perm)]
    unnamed x18 -> x8, local copies, waits for them, and re-layouts: 4.43 us -> 0.45 us
    ppermute x6, starting transfers between devices: 13.3 us -> 10.9 us  [over_mpo(): return lax.ppermute(x, 'mpo', perm)]
    pallas_call x2 -> x1, Pallas kernels: 4.97 us -> 2.79 us  [make_lines(): pl.pallas_call(line_kernel, out_shape=[jax.ShapeDtypeStruct(shape, BF) fo...]
    concatenate x0 -> x1, other arithmetic: none -> 1.95 us  [per_device(): jnp.concatenate([right_env, packed], axis=2).reshape(-1, dr + rows, dr)]
    slice x2 -> x3, local copies, waits for them, and re-layouts: 0.18 us -> 1.64 us  [the longest x1 1.46 us: per_device(): left_env[:, :, :rows]]
    ppermute x6, waiting for transfers between devices: 6.36 us -> 7.8 us  [over_mpo(): return lax.ppermute(x, 'mpo', perm)]
    pallas_call x4, Pallas kernels: 21.1 us -> 22.5 us  [add_terms(): pl.pallas_call(functools.partial(term_kernel, rows, n_vec, len(envs), acc...]
  transfers between devices with their start and end apart: 15 -> 15, of which waited for: 7 -> 4; matrix products, arithmetic and copies ran while one was open for 4% -> 6% of each run, Pallas kernels for 32% -> 36%
where the time goes in v3:
time: 82.8 us; the launch traced here: 82.2 us
  Pallas kernels  29.5 us (36%)
  starting transfers between devices  26.2 us (32%)
  waiting for transfers between devices  17.1 us (21%)
  other arithmetic  5.77 us (7%)
  local copies, waits for them, and re-layouts  3.43 us (4%)
    pallas_call x4, Pallas kernels, add_terms(): pl.pallas_call(functools.partial(term_kernel, rows, n_vec, len(envs), acc...  22.5 us
    ppermute x9, starting transfers between devices, over_all(): return lax.ppermute(x, ('sec', 'mpo'), perm)  15.3 us
    ppermute x6, starting transfers between devices, over_mpo(): return lax.ppermute(x, 'mpo', perm)  10.9 us
    ppermute x9, waiting for transfers between devices, over_all(): return lax.ppermute(x, ('sec', 'mpo'), perm)  9.35 us
    ppermute x6, waiting for transfers between devices, over_mpo(): return lax.ppermute(x, 'mpo', perm)  7.8 us
    pallas_call x1, Pallas kernels, make_lines(): pl.pallas_call(line_kernel, out_shape=[jax.ShapeDtypeStruct(shape, BF) fo...  2.79 us
    pallas_call x1, Pallas kernels, join(): pl.pallas_call(join_kernel, out_shape=jax.ShapeDtypeStruct((first.shape[0...  2.55 us
    concatenate x1, other arithmetic, per_device(): jnp.concatenate([right_env, packed], axis=2).reshape(-1, dr + rows, dr)  1.95 us
  transfers between devices with their start and end apart: 15, of which 4 were waited for; matrix products, arithmetic and copies ran while one was open for 6% of the time, Pallas kernels for 36%

profile of v3, /device:TPU:1, one launch (start us, length us, event | category | flops | bytes accessed | tf_op | source)
XLA Modules:
  0.0 82.2 jit_solution(7892074033095280620)
XLA Ops:
  0.0 1.5 %fusion.18 = (bf16[4,16,32,64]{3,2,1,0:T(8,128)(2,1)S(1)}, bf16[4,16,32,64]{3,2,1,0:T(8,128)(2,1)S(1)}) fusion(bf16[4,16,64,64]{3,2,1,0:T(8,128)(2,1)} %param.6), kind=kLoop, calls=%fused_computation.90 | loop fusion | bytes 1048576 | tf_op jit(solution)/shard_map/slice | solution.py:225
  1.5 0.4 copy-done.1
  1.9 1.9 %maximum_maximum_fusion = bf16[4,16,160,128]{3,2,1,0:T(8,128)(2,1)} fusion(bf16[4,16,32,64]{3,2,1,0:T(8,128)(2,1)S(1)} %get-tuple-element.34, bf16[4,16,32,64]{3,2,1,0:T(8,128)(2,1)S(1)} %get-tuple-element.33, bf16[4,16,128,128]{3,2,1,0:T(8,128)(2,1)S(1)} %copy-done.1), kind=kLoop, calls=%fused_computation | loop fusion | flops 7864320 | bytes 5242880 | tf_op jit(solution)/shard_map/concatenate | solution.py:226
  3.9 1.4 %collective-permute-start.5 = (bf16[64,160,128]{2,1,0:T(8,128)(2,1)}, bf16[64,160,128]{2,1,0:T(8,128)(2,1)}, u32[]{:S(2)}, u32[]{:S(2)}) collective-permute-start(bf16[64,160,128]{2,1,0:T(8,128)(2,1)} %bitcast.refs_0_), channel_id=1, source_target_pairs={{0,1},{1,0},{2,3},{3,2},{4,5},{5,4},{6,7},{7,6},{8,9},{9,8},{10,11... | collective-permute-start | bytes 7864328 | tf_op jit(solution)/shard_map/ppermute | solution.py:50
  5.3 1.4 %collective-permute-start = (s32[4,16]{1,0:T(4,128)S(1)}, s32[4,16]{1,0:T(4,128)S(1)}, u32[]{:S(2)}, u32[]{:S(2)}) collective-permute-start(s32[4,16]{1,0:T(4,128)S(1)} %compare_select_fusion.24), channel_id=1, source_target_pairs={{0,6},{1,3},{2,0},{3,5},{4,2},{5,7},{6,4},{7,1},{8,14},{9,11},{10,... | collective-permute-start | bytes 776 | tf_op jit(solution)/shard_map/ppermute | solution.py:50
  6.7 1.1 %dynamic-slice_bitcast_fusion.1 = (bf16[1,16,64,128]{3,2,1,0:T(8,128)(2,1)S(1)}, bf16[1,16,64,128]{3,2,1,0:T(8,128)(2,1)S(1)}) fusion(bf16[16,8,64,128]{3,2,1,0:T(8,128)(2,1)} %param.5, s32[]{:T(128)S(6)} %select_n.241, s32[]{:T(128)S(6)} %select_n.242), kind=kLoop, calls=%fused_computation.5 | loop fusion | bytes 1048584 | tf_op jit(solution)/shard_map/stack;squeeze | solution.py:219
  7.7 0.1 pad_maximum_fusion.refs_0_
  7.8 3.0 %collective-permute-start.4 = (bf16[2,16,64,128]{3,2,1,0:T(8,128)(2,1)S(1)}, bf16[2,16,64,128]{3,2,1,0:T(8,128)(2,1)}, u32[]{:S(2)}, u32[]{:S(2)}) collective-permute-start(bf16[2,16,64,128]{3,2,1,0:T(8,128)(2,1)S(1)} %pad_maximum_fusion.refs_0_), channel_id=1, source_target_pairs={{0,64},{1,17},{2,66},{3,19},{4,68},{5,21},{6,70},{7,23},{8,72},{9,... | collective-permute-start | bytes 1572872 | tf_op jit(solution)/shard_map/ppermute | solution.py:46
  10.8 0.0 collective-permute-done
  10.8 1.2 %collective-permute-start.1 = (bf16[64,160,128]{2,1,0:T(8,128)(2,1)}, bf16[64,160,128]{2,1,0:T(8,128)(2,1)S(1)}, u32[]{:S(2)}, u32[]{:S(2)}) collective-permute-start(bf16[64,160,128]{2,1,0:T(8,128)(2,1)} %bitcast.refs_0_), channel_id=1, source_target_pairs={{0,6},{1,3},{2,0},{3,5},{4,2},{5,7},{6,4},{7,1},{8,14},{9,11},{10,... | collective-permute-start | bytes 7864328 | tf_op jit(solution)/shard_map/ppermute | solution.py:50
  12.0 2.1 %collective-permute-start.6 = (s32[2,4,16]{2,1,0:T(4,128)S(1)}, s32[2,4,16]{2,1,0:T(4,128)S(1)}, u32[]{:S(2)}, u32[]{:S(2)}) collective-permute-start(s32[2,4,16]{2,1,0:T(4,128)S(1)} %pad_add_fusion.1), channel_id=1, source_target_pairs={{0,1},{1,0},{2,3},{3,2},{4,5},{5,4},{6,7},{7,6},{8,9},{9,8},{10,11... | collective-permute-start | bytes 1544 | tf_op jit(solution)/shard_map/ppermute | solution.py:50
  14.1 1.3 %collective-permute-start.2 = (bf16[2,16,64,128]{3,2,1,0:T(8,128)(2,1)S(1)}, bf16[2,16,64,128]{3,2,1,0:T(8,128)(2,1)}, u32[]{:S(2)}, u32[]{:S(2)}) collective-permute-start(bf16[2,16,64,128]{3,2,1,0:T(8,128)(2,1)S(1)} %pad_maximum_fusion.refs_0_), channel_id=1, source_target_pairs={{0,32},{1,9},{2,34},{3,11},{4,36},{5,13},{6,38},{7,15},{8,40},{9,1... | collective-permute-start | bytes 1572872 | tf_op jit(solution)/shard_map/ppermute | solution.py:46
  15.4 0.0 collective-permute-done.6
  15.4 2.3 %collective-permute-start.3 = (bf16[2,16,64,128]{3,2,1,0:T(8,128)(2,1)S(1)}, bf16[2,16,64,128]{3,2,1,0:T(8,128)(2,1)}, u32[]{:S(2)}, u32[]{:S(2)}) collective-permute-start(bf16[2,16,64,128]{3,2,1,0:T(8,128)(2,1)S(1)} %pad_maximum_fusion.refs_0_), channel_id=1, source_target_pairs={{0,96},{1,25},{2,98},{3,27},{4,100},{5,29},{6,102},{7,31},{8,104},... | collective-permute-start | bytes 1572872 | tf_op jit(solution)/shard_map/ppermute | solution.py:46
  17.7 0.1 collective-permute-done.4.refs_3_
  17.8 0.1 stack.25
  17.9 0.1 stack.24
  18.0 5.9 %collective-permute-done.2.refs_1_ = bf16[2,16,64,128]{3,2,1,0:T(8,128)(2,1)} collective-permute-done((bf16[2,16,64,128]{3,2,1,0:T(8,128)(2,1)S(1)}, bf16[2,16,64,128]{3,2,1,0:T(8,128)(2,1)}, u32[]{:S(2)}, u32[]{:S(2)}) %collective-permute-start.2) | collective-permute-done | bytes 524320 | tf_op jit(solution)/shard_map/ppermute | solution.py:46
  23.9 0.0 collective-permute-done.3.refs_2_
  23.9 2.8 %shard_map.55 = (bf16[64,64,128]{2,1,0:T(8,128)(2,1)}, bf16[64,64,128]{2,1,0:T(8,128)(2,1)}) custom-call(bf16[2,16,64,128]{3,2,1,0:T(8,128)(2,1)S(1)} %pad_maximum_fusion.refs_0_, bf16[2,16,64,128]{3,2,1,0:T(8,128)(2,1)} %collective-permute-done.2.refs_1_, bf16[2,16,64,128]{3,2,1,0:T(8,128)(2,1)} %collective-permute-done.3.refs_2_, ...), custom_call_target="tpu_custom_call" | custom-call | flops 7000000000 | bytes 4000000 | tf_op jit(solution)/shard_map/pallas_call | solution.py:200
  26.7 1.5 %collective-permute-start.7 = (bf16[64,64,128]{2,1,0:T(8,128)(2,1)}, bf16[64,64,128]{2,1,0:T(8,128)(2,1)}, u32[]{:S(2)}, u32[]{:S(2)}) collective-permute-start(bf16[64,64,128]{2,1,0:T(8,128)(2,1)} %get-tuple-element.19.refs_3_), channel_id=1, source_target_pairs={{0,8},{1,33},{2,10},{3,35},{4,12},{5,37},{6,14},{7,39},{8,16},{9,4... | collective-permute-start | bytes 3145736 | tf_op jit(solution)/shard_map/ppermute | solution.py:46
  28.2 2.1 %collective-permute-start.8 = (bf16[64,64,128]{2,1,0:T(8,128)(2,1)}, bf16[64,64,128]{2,1,0:T(8,128)(2,1)}, u32[]{:S(2)}, u32[]{:S(2)}) collective-permute-start(bf16[64,64,128]{2,1,0:T(8,128)(2,1)} %get-tuple-element.20.refs_3_), channel_id=1, source_target_pairs={{0,24},{1,97},{2,26},{3,99},{4,28},{5,101},{6,30},{7,103},{8,0},{9... | collective-permute-start | bytes 3145736 | tf_op jit(solution)/shard_map/ppermute | solution.py:46
  30.4 1.5 %reduce-window.6 = s32[5,2,128]{2,1,0:T(2,128)S(1)} reduce-window(s32[5,2,128]{2,1,0:T(2,128)S(1)} %fusion.1, s32[]{:T(128)} %constant.127.clone.1), window={size=1x1x128 pad=0_0x0_0x127_0}, to_apply=%region_0.1 | reduce-window | flops 162560 | bytes 10244 | tf_op jit(solution)/shard_map/reduce-window
  31.9 0.1 slice.32
  32.0 0.1 copy.9
  32.1 0.1 copy.10
  32.2 0.1 select_reduce_fusion
  32.3 0.6 fusion.13
  32.9 0.5 bitcast_add_fusion
  33.5 1.7 %shard_map.56.list_ref = s32[1280]{0:T(1024)} custom-call(s32[256]{0:T(256)} %get-tuple-element.29.place_ref, s32[256]{0:T(256)} %get-tuple-element.27.entry_ref), custom_call_target="tpu_custom_call" | custom-call | tf_op jit(solution)/shard_map/pallas_call | solution.py:73
  35.2 0.1 convert_reduce_fusion.count_ref
  35.3 7.8 %collective-permute-done.1.refs_1_ = bf16[64,160,128]{2,1,0:T(8,128)(2,1)S(1)} collective-permute-done((bf16[64,160,128]{2,1,0:T(8,128)(2,1)}, bf16[64,160,128]{2,1,0:T(8,128)(2,1)S(1)}, u32[]{:S(2)}, u32[]{:S(2)}) %collective-permute-start.1) | collective-permute-done | bytes 2621472 | tf_op jit(solution)/shard_map/ppermute | solution.py:50
  43.1 0.0 collective-permute-done.8.refs_4_
  43.1 3.6 %collective-permute-start.9 = (bf16[64,160,128]{2,1,0:T(8,128)(2,1)S(1)}, bf16[64,160,128]{2,1,0:T(8,128)(2,1)S(1)}, u32[]{:S(2)}, u32[]{:S(2)}) collective-permute-start(bf16[64,160,128]{2,1,0:T(8,128)(2,1)S(1)} %collective-permute-done.1.refs_1_), channel_id=1, source_target_pairs={{0,1},{1,0},{2,3},{3,2},{4,5},{5,4},{6,7},{7,6},{8,9},{9,8},{10,11... | collective-permute-start | bytes 7864328 | tf_op jit(solution)/shard_map/ppermute | solution.py:50
  46.7 2.4 %collective-permute-start.12 = (bf16[64,64,128]{2,1,0:T(8,128)(2,1)}, bf16[64,64,128]{2,1,0:T(8,128)(2,1)S(1)}, u32[]{:S(2)}, u32[]{:S(2)}) collective-permute-start(bf16[64,64,128]{2,1,0:T(8,128)(2,1)} %get-tuple-element.19.refs_3_), channel_id=1, source_target_pairs={{0,24},{1,97},{2,26},{3,99},{4,28},{5,101},{6,30},{7,103},{8,0},{9... | collective-permute-start | bytes 3145736 | tf_op jit(solution)/shard_map/ppermute | solution.py:46
  49.1 0.0 collective-permute-start.10
  49.1 2.7 %collective-permute-start.11 = (bf16[64,64,128]{2,1,0:T(8,128)(2,1)}, bf16[64,64,128]{2,1,0:T(8,128)(2,1)S(1)}, u32[]{:S(2)}, u32[]{:S(2)}) collective-permute-start(bf16[64,64,128]{2,1,0:T(8,128)(2,1)} %collective-permute-done.8.refs_4_), channel_id=1, source_target_pairs={{0,24},{1,97},{2,26},{3,99},{4,28},{5,101},{6,30},{7,103},{8,0},{9... | collective-permute-start | bytes 3145736 | tf_op jit(solution)/shard_map/ppermute | solution.py:46
  51.8 2.5 %shard_map.57.refs_0_ = bf16[128,160,128]{2,1,0:T(8,128)(2,1)S(1)} custom-call(bf16[64,160,128]{2,1,0:T(8,128)(2,1)} %bitcast.refs_0_, bf16[64,160,128]{2,1,0:T(8,128)(2,1)} %collective-permute-done.5.refs_1_), custom_call_target="tpu_custom_call" | custom-call | bytes 10000000 | tf_op jit(solution)/shard_map/pallas_call | solution.py:177
  54.3 0.0 collective-permute-done.9.refs_2_
  54.4 6.7 %shard_map.60.refs_5_ = f32[16,64,128]{2,1,0:T(8,128)S(1)} custom-call(s32[1280]{0:T(1024)S(1)} %copy-done, s32[5]{0:T(128)S(1)} %convert_reduce_fusion.count_ref, bf16[128,160,128]{2,1,0:T(8,128)(2,1)S(1)} %shard_map.57.refs_0_, bf16[64,160,128]{2,1,0:T(8,128)(2,1)S(1)} %collective-permute-done.1.refs_1_, ...), custom_call_target="tpu_custom_call" | custom-call | flops 3000000000 | bytes 12000000 | tf_op jit(solution)/shard_map/pallas_call | solution.py:150
  61.1 0.0 collective-permute-done.12.refs_3_
  61.1 3.3 %collective-permute-done.13.refs_4_ = bf16[64,64,128]{2,1,0:T(8,128)(2,1)S(1)} collective-permute-done((bf16[64,64,128]{2,1,0:T(8,128)(2,1)}, bf16[64,64,128]{2,1,0:T(8,128)(2,1)S(1)}, u32[]{:S(2)}, u32[]{:S(2)}) %collective-permute-start.13) | collective-permute-done | bytes 1048608 | tf_op jit(solution)/shard_map/ppermute | solution.py:46
  64.4 4.5 %shard_map.61 = bf16[16,64,128]{2,1,0:T(8,128)(2,1)S(1)} custom-call(s32[1280]{0:T(1024)S(1)} %copy-done, s32[5]{0:T(128)S(1)} %convert_reduce_fusion.count_ref, bf16[128,160,128]{2,1,0:T(8,128)(2,1)S(1)} %shard_map.57.refs_0_, bf16[64,160,128]{2,1,0:T(8,128)(2,1)S(1)} %collective-permute-done.1.refs_1_, ...), custom_call_target="tpu_custom_call" | custom-call | flops 3000000000 | bytes 12000000 | tf_op jit(solution)/shard_map/pallas_call | solution.py:150
  69.0 1.2 %collective-permute-start.14 = (bf16[16,64,128]{2,1,0:T(8,128)(2,1)S(1)}, bf16[16,64,128]{2,1,0:T(8,128)(2,1)S(1)}, u32[]{:S(2)}, u32[]{:S(2)}) collective-permute-start(bf16[16,64,128]{2,1,0:T(8,128)(2,1)S(1)} %shard_map.61), channel_id=1, source_target_pairs={{0,4},{1,5},{2,6},{3,7},{4,0},{5,1},{6,2},{7,3},{8,12},{9,13},{10,... | collective-permute-start | bytes 786440 | tf_op jit(solution)/shard_map/ppermute | solution.py:50
  70.2 6.7 %shard_map.58.refs_5_ = f32[16,64,128]{2,1,0:T(8,128)S(1)} custom-call(s32[1280]{0:T(1024)S(1)} %copy-done, s32[5]{0:T(128)S(1)} %convert_reduce_fusion.count_ref, bf16[128,160,128]{2,1,0:T(8,128)(2,1)S(1)} %shard_map.57.refs_0_, bf16[64,160,128]{2,1,0:T(8,128)(2,1)S(1)} %collective-permute-done.1.refs_1_, ...), custom_call_target="tpu_custom_call" | custom-call | flops 3000000000 | bytes 12000000 | tf_op jit(solution)/shard_map/pallas_call | solution.py:150
  76.9 0.0 collective-permute-done.11.refs_4_
  76.9 4.5 %shard_map.59 = f32[16,64,128]{2,1,0:T(8,128)S(1)} custom-call(s32[1280]{0:T(1024)S(1)} %copy-done, s32[5]{0:T(128)S(1)} %convert_reduce_fusion.count_ref, bf16[128,160,128]{2,1,0:T(8,128)(2,1)S(1)} %shard_map.57.refs_0_, bf16[64,160,128]{2,1,0:T(8,128)(2,1)S(1)} %collective-permute-done.1.refs_1_, bf16[64,160,128]{2,1,0:T(8,128)(2,1)S(1)} %collective-permute-done.9.refs_2_, ...), custom_call_target="tpu_custom_call" | custom-call | flops 3000000000 | bytes 12000000 | tf_op jit(solution)/shard_map/pallas_call | solution.py:150
  81.5 0.8 fusion
  (20 shorter events, 0.1 us)
Async XLA Ops:
  0.0 1.9 %copy-start.1 = (bf16[4,16,128,128]{3,2,1,0:T(8,128)(2,1)S(1)}, bf16[4,16,128,128]{3,2,1,0:T(8,128)(2,1)}, u32[]{:S(2)}) copy-start(bf16[4,16,128,128]{3,2,1,0:T(8,128)(2,1)} %param.7) | copy-start | bytes 6291460
  1.9 3.4 %copy-start.2 = (s32[4,16]{1,0:T(4,128)S(1)}, s32[4,16]{1,0:T(4,128)}, u32[]{:S(2)}) copy-start(s32[4,16]{1,0:T(4,128)} %param.8) | copy-start | bytes 772
  1.9 3.4 %copy-start.3 = (s32[4,16]{1,0:T(4,128)S(1)}, s32[4,16]{1,0:T(4,128)}, u32[]{:S(2)}) copy-start(s32[4,16]{1,0:T(4,128)} %param.9) | copy-start | bytes 772
  3.9 13.9 %collective-permute-start.5 = (bf16[64,160,128]{2,1,0:T(8,128)(2,1)}, bf16[64,160,128]{2,1,0:T(8,128)(2,1)}, u32[]{:S(2)}, u32[]{:S(2)}) collective-permute-start(bf16[64,160,128]{2,1,0:T(8,128)(2,1)} %bitcast.refs_0_), channel_id=1, source_target_pairs={{0,1},{1,0},{2,3},{3,2},{4,5},{5,4},{6,7},{7,6},{8,9},{9,8},{10,11... | collective-permute-start | bytes 7864328 | tf_op jit(solution)/shard_map/ppermute | solution.py:50
  5.3 5.5 %collective-permute-start = (s32[4,16]{1,0:T(4,128)S(1)}, s32[4,16]{1,0:T(4,128)S(1)}, u32[]{:S(2)}, u32[]{:S(2)}) collective-permute-start(s32[4,16]{1,0:T(4,128)S(1)} %compare_select_fusion.24), channel_id=1, source_target_pairs={{0,6},{1,3},{2,0},{3,5},{4,2},{5,7},{6,4},{7,1},{8,14},{9,11},{10,... | collective-permute-start | bytes 776 | tf_op jit(solution)/shard_map/ppermute | solution.py:50
  7.8 10.0 %collective-permute-start.4 = (bf16[2,16,64,128]{3,2,1,0:T(8,128)(2,1)S(1)}, bf16[2,16,64,128]{3,2,1,0:T(8,128)(2,1)}, u32[]{:S(2)}, u32[]{:S(2)}) collective-permute-start(bf16[2,16,64,128]{3,2,1,0:T(8,128)(2,1)S(1)} %pad_maximum_fusion.refs_0_), channel_id=1, source_target_pairs={{0,64},{1,17},{2,66},{3,19},{4,68},{5,21},{6,70},{7,23},{8,72},{9,... | collective-permute-start | bytes 1572872 | tf_op jit(solution)/shard_map/ppermute | solution.py:46
  10.8 32.3 %collective-permute-start.1 = (bf16[64,160,128]{2,1,0:T(8,128)(2,1)}, bf16[64,160,128]{2,1,0:T(8,128)(2,1)S(1)}, u32[]{:S(2)}, u32[]{:S(2)}) collective-permute-start(bf16[64,160,128]{2,1,0:T(8,128)(2,1)} %bitcast.refs_0_), channel_id=1, source_target_pairs={{0,6},{1,3},{2,0},{3,5},{4,2},{5,7},{6,4},{7,1},{8,14},{9,11},{10,... | collective-permute-start | bytes 7864328 | tf_op jit(solution)/shard_map/ppermute | solution.py:50
  12.0 3.4 %collective-permute-start.6 = (s32[2,4,16]{2,1,0:T(4,128)S(1)}, s32[2,4,16]{2,1,0:T(4,128)S(1)}, u32[]{:S(2)}, u32[]{:S(2)}) collective-permute-start(s32[2,4,16]{2,1,0:T(4,128)S(1)} %pad_add_fusion.1), channel_id=1, source_target_pairs={{0,1},{1,0},{2,3},{3,2},{4,5},{5,4},{6,7},{7,6},{8,9},{9,8},{10,11... | collective-permute-start | bytes 1544 | tf_op jit(solution)/shard_map/ppermute | solution.py:50
  14.1 9.7 %collective-permute-start.2 = (bf16[2,16,64,128]{3,2,1,0:T(8,128)(2,1)S(1)}, bf16[2,16,64,128]{3,2,1,0:T(8,128)(2,1)}, u32[]{:S(2)}, u32[]{:S(2)}) collective-permute-start(bf16[2,16,64,128]{3,2,1,0:T(8,128)(2,1)S(1)} %pad_maximum_fusion.refs_0_), channel_id=1, source_target_pairs={{0,32},{1,9},{2,34},{3,11},{4,36},{5,13},{6,38},{7,15},{8,40},{9,1... | collective-permute-start | bytes 1572872 | tf_op jit(solution)/shard_map/ppermute | solution.py:46
  15.4 8.4 %collective-permute-start.3 = (bf16[2,16,64,128]{3,2,1,0:T(8,128)(2,1)S(1)}, bf16[2,16,64,128]{3,2,1,0:T(8,128)(2,1)}, u32[]{:S(2)}, u32[]{:S(2)}) collective-permute-start(bf16[2,16,64,128]{3,2,1,0:T(8,128)(2,1)S(1)} %pad_maximum_fusion.refs_0_), channel_id=1, source_target_pairs={{0,96},{1,25},{2,98},{3,27},{4,100},{5,29},{6,102},{7,31},{8,104},... | collective-permute-start | bytes 1572872 | tf_op jit(solution)/shard_map/ppermute | solution.py:46
  26.7 16.5 %collective-permute-start.7 = (bf16[64,64,128]{2,1,0:T(8,128)(2,1)}, bf16[64,64,128]{2,1,0:T(8,128)(2,1)}, u32[]{:S(2)}, u32[]{:S(2)}) collective-permute-start(bf16[64,64,128]{2,1,0:T(8,128)(2,1)} %get-tuple-element.19.refs_3_), channel_id=1, source_target_pairs={{0,8},{1,33},{2,10},{3,35},{4,12},{5,37},{6,14},{7,39},{8,16},{9,4... | collective-permute-start | bytes 3145736 | tf_op jit(solution)/shard_map/ppermute | solution.py:46
  28.2 14.9 %collective-permute-start.8 = (bf16[64,64,128]{2,1,0:T(8,128)(2,1)}, bf16[64,64,128]{2,1,0:T(8,128)(2,1)}, u32[]{:S(2)}, u32[]{:S(2)}) collective-permute-start(bf16[64,64,128]{2,1,0:T(8,128)(2,1)} %get-tuple-element.20.refs_3_), channel_id=1, source_target_pairs={{0,24},{1,97},{2,26},{3,99},{4,28},{5,101},{6,30},{7,103},{8,0},{9... | collective-permute-start | bytes 3145736 | tf_op jit(solution)/shard_map/ppermute | solution.py:46
  35.3 19.0 %copy-start = (s32[1280]{0:T(1024)S(1)}, s32[1280]{0:T(1024)}, u32[]{:S(2)}) copy-start(s32[1280]{0:T(1024)} %shard_map.56.list_ref) | copy-start | bytes 15364
  43.1 11.2 %collective-permute-start.9 = (bf16[64,160,128]{2,1,0:T(8,128)(2,1)S(1)}, bf16[64,160,128]{2,1,0:T(8,128)(2,1)S(1)}, u32[]{:S(2)}, u32[]{:S(2)}) collective-permute-start(bf16[64,160,128]{2,1,0:T(8,128)(2,1)S(1)} %collective-permute-done.1.refs_1_), channel_id=1, source_target_pairs={{0,1},{1,0},{2,3},{3,2},{4,5},{5,4},{6,7},{7,6},{8,9},{9,8},{10,11... | collective-permute-start | bytes 7864328 | tf_op jit(solution)/shard_map/ppermute | solution.py:50
  46.7 14.5 %collective-permute-start.12 = (bf16[64,64,128]{2,1,0:T(8,128)(2,1)}, bf16[64,64,128]{2,1,0:T(8,128)(2,1)S(1)}, u32[]{:S(2)}, u32[]{:S(2)}) collective-permute-start(bf16[64,64,128]{2,1,0:T(8,128)(2,1)} %get-tuple-element.19.refs_3_), channel_id=1, source_target_pairs={{0,24},{1,97},{2,26},{3,99},{4,28},{5,101},{6,30},{7,103},{8,0},{9... | collective-permute-start | bytes 3145736 | tf_op jit(solution)/shard_map/ppermute | solution.py:46
  49.1 15.4 %collective-permute-start.13 = (bf16[64,64,128]{2,1,0:T(8,128)(2,1)}, bf16[64,64,128]{2,1,0:T(8,128)(2,1)S(1)}, u32[]{:S(2)}, u32[]{:S(2)}) collective-permute-start(bf16[64,64,128]{2,1,0:T(8,128)(2,1)} %collective-permute-done.7.refs_4_), channel_id=1, source_target_pairs={{0,8},{1,33},{2,10},{3,35},{4,12},{5,37},{6,14},{7,39},{8,16},{9,4... | collective-permute-start | bytes 3145736 | tf_op jit(solution)/shard_map/ppermute | solution.py:46
  49.1 27.8 %collective-permute-start.10 = (bf16[64,64,128]{2,1,0:T(8,128)(2,1)}, bf16[64,64,128]{2,1,0:T(8,128)(2,1)S(1)}, u32[]{:S(2)}, u32[]{:S(2)}) collective-permute-start(bf16[64,64,128]{2,1,0:T(8,128)(2,1)} %get-tuple-element.20.refs_3_), channel_id=1, source_target_pairs={{0,8},{1,33},{2,10},{3,35},{4,12},{5,37},{6,14},{7,39},{8,16},{9,4... | collective-permute-start | bytes 3145736 | tf_op jit(solution)/shard_map/ppermute | solution.py:46
  49.1 27.8 %collective-permute-start.11 = (bf16[64,64,128]{2,1,0:T(8,128)(2,1)}, bf16[64,64,128]{2,1,0:T(8,128)(2,1)S(1)}, u32[]{:S(2)}, u32[]{:S(2)}) collective-permute-start(bf16[64,64,128]{2,1,0:T(8,128)(2,1)} %collective-permute-done.8.refs_4_), channel_id=1, source_target_pairs={{0,24},{1,97},{2,26},{3,99},{4,28},{5,101},{6,30},{7,103},{8,0},{9... | collective-permute-start | bytes 3145736 | tf_op jit(solution)/shard_map/ppermute | solution.py:46
  69.0 12.5 %collective-permute-start.14 = (bf16[16,64,128]{2,1,0:T(8,128)(2,1)S(1)}, bf16[16,64,128]{2,1,0:T(8,128)(2,1)S(1)}, u32[]{:S(2)}, u32[]{:S(2)}) collective-permute-start(bf16[16,64,128]{2,1,0:T(8,128)(2,1)S(1)} %shard_map.61), channel_id=1, source_target_pairs={{0,4},{1,5},{2,6},{3,7},{4,0},{5,1},{6,2},{7,3},{8,12},{9,13},{10,... | collective-permute-start | bytes 786440 | tf_op jit(solution)/shard_map/ppermute | solution.py:50

commit v4 on v3

--- a/solution.py
+++ b/solution.py
@@ -13,7 +13,7 @@
 F32 = jnp.float32
 PIECE, PIECES = 64, 4
 PAIRS = 256
-UNROLL = 16
+UNROLL = 24
 
 
 def mpo_perm(fn):
@@ -79,9 +79,9 @@
     return lists, jnp.sum(chosen, axis=1)
 
 
-def term_kernel(lines, n_vec, n_env, fresh, list_ref, count_ref, *refs):
-    envs, refs = refs[:n_env], refs[n_env:]
-    psi_refs, refs = refs[: len(lines) * n_vec], refs[len(lines) * n_vec :]
+def term_kernel(plan, n_vec, n_env, fresh, list_ref, count_ref, *refs):
+    envs, refs = refs[:n_env], list(refs[n_env:])
+    psis = [[refs.pop(0) for _ in vectors] for _, vectors in plan]
     if not fresh:
         acc_refs, refs = refs[:n_vec], refs[n_vec:]
     out_refs, totals = refs[:n_vec], refs[n_vec:]
@@ -102,7 +102,7 @@
             start += size
         return value
 
-    def add(psis, line):
+    def add(psis, vectors, line):
         count = count_ref[line]
 
         def step(i, carry):
@@ -117,47 +117,44 @@
                 packed = rows_of(pair, dr, dr + dl // 2)
                 left = jnp.concatenate([packed[:, :dl], packed[:, dl:]], axis=0)
                 blocks = [psi[at] for psi in psis]
-                block = blocks[0] if n_vec == 1 else jnp.concatenate(blocks, axis=1)
+                block = blocks[0] if len(psis) == 1 else jnp.concatenate(blocks, axis=1)
                 value = jnp.dot(left, block, preferred_element_type=F32).astype(BF)
-                if n_vec > 1:
-                    value = jnp.concatenate(
-                        [value[:, v * dr : (v + 1) * dr] for v in range(n_vec)], axis=0
-                    )
+                if len(psis) > 1:
+                    parts = [value[:, k * dr : (k + 1) * dr] for k in range(len(psis))]
+                    value = jnp.concatenate(parts, axis=0)
                 values.append(value)
             terms = []
             for value, (_, pair, _) in zip(values, entries):
                 right = rows_of(pair, 0, dr)
                 terms.append(jnp.dot(value, right, preferred_element_type=F32))
             for term, (_, _, to) in zip(terms, entries):
-                for v in range(n_vec):
-                    totals[v][to] += term[v * dl : (v + 1) * dl]
+                for k, v in enumerate(vectors):
+                    totals[v][to] += term[k * dl : (k + 1) * dl]
             return carry
 
         lax.fori_loop(0, (count + UNROLL - 1) // UNROLL, step, 0)
 
-    for p, line in enumerate(lines):
-        add(psi_refs[p * n_vec : (p + 1) * n_vec], line)
+    for arrays, (line, vectors) in zip(psis, plan):
+        add(arrays, vectors, line)
     for v in range(n_vec):
         out_refs[v][...] = totals[v][0:sec].astype(out_refs[v].dtype)
 
 
-def add_terms(rows, lists, counts, envs, psis, accs, sec, dtype=F32):
-    n_vec = len(psis[0])
-    flat = [x for piece in psis for x in piece]
-    _, dl, dr = flat[0].shape
+def add_terms(plan, lists, counts, envs, psis, accs, n_vec, sec, dtype=F32):
+    dl, dr = psis[0].shape[1:]
     smem = pl.BlockSpec(memory_space=pltpu.SMEM)
     vmem = pl.BlockSpec(memory_space=pltpu.VMEM)
     return pl.pallas_call(
-        functools.partial(term_kernel, rows, n_vec, len(envs), accs is None),
+        functools.partial(term_kernel, plan, n_vec, len(envs), accs is None),
         out_shape=[jax.ShapeDtypeStruct((sec, dl, dr), dtype)] * n_vec,
-        in_specs=[smem, smem] + [vmem] * (len(envs) + len(flat) + len(accs or [])),
+        in_specs=[smem, smem] + [vmem] * (len(envs) + len(psis) + len(accs or [])),
         out_specs=[vmem] * n_vec,
         scratch_shapes=[pltpu.VMEM((sec + 1, dl, dr), F32)] * n_vec,
         compiler_params=pltpu.CompilerParams(vmem_limit_bytes=24 * 2**20),
         cost_estimate=pl.CostEstimate(
             flops=int(3e9), bytes_accessed=int(1.2e7), transcendentals=0
         ),
-    )(lists, counts, *envs, *flat, *(accs or []))
+    )(lists, counts, *envs, *psis, *(accs or []))
 
 
 def join_kernel(*refs):
@@ -180,7 +177,7 @@
         in_specs=[pl.BlockSpec(memory_space=pl.ANY)] * len(arrays),
         out_specs=pl.BlockSpec(memory_space=pltpu.VMEM),
         scratch_shapes=[pltpu.SemaphoreType.DMA((len(arrays),))],
-        compiler_params=pltpu.CompilerParams(vmem_limit_bytes=12 * 2**20),
+        compiler_params=pltpu.CompilerParams(vmem_limit_bytes=16 * 2**20),
         cost_estimate=pl.CostEstimate(flops=0, bytes_accessed=int(1e7), transcendentals=0),
     )(*arrays)
 
@@ -251,15 +248,18 @@
     env_apart, _, _, lists, counts = lax.optimization_barrier(
         (env_apart, lines_up[0], lines_down[1], lists, counts)
     )
-    envs = [join([env, env_core]), env_apart, over_mpo(env_apart, CORE)]
-    pieces = [[x[v] for x in (lines, lines_up, lines_down, lasts)] for v in range(2)]
-
-    def added(v, rows, sums, kind=F32):
-        return add_terms(rows, lists, counts, envs, [[pieces[v][k]] for k in rows], sums, sec_local, kind)
-
-    (away,) = added(0, (2, 3), added(0, (0, 1), None), BF)
+    envs = [join([env, env_core, env_apart, over_mpo(env_apart, CORE)])]
+
+    def added(plan, psis, sums, kind=F32):
+        n_vec = 1 if sums else 2
+        return add_terms(plan, lists, counts, envs, psis, sums, n_vec, sec_local, kind)
+
+    plan = [(0, (0, 1)), (1, (0,))]
+    away, home = added(plan, [lines[0], lines[1], lines_up[0]], None)
+    (away,) = added([(2, (0,)), (3, (0,))], [lines_down[0], lasts[0]], [away], BF)
     arrived = over_mpo(away, FAR)
-    (home,) = added(1, (1, 3), added(1, (0, 2), None))
+    (home,) = added([(2, (0,))], [lines_down[1]], [home])
+    (home,) = added([(1, (0,)), (3, (0,))], [lines_up[1], lasts[1]], [home])
     return (home + arrived.astype(F32)).astype(BF)[:, None]
 
 

time: 82.8 us -> 78.8 us (0.952)
  Pallas kernels: 29.5 us -> 22.5 us
  waiting for transfers between devices: 17.1 us -> 22.4 us
  other arithmetic: 5.77 us -> 4.28 us
    pallas_call x4, Pallas kernels: 22.5 us -> 15.2 us  [add_terms(): pl.pallas_call(functools.partial(term_kernel, plan, n_vec, len(envs), acc...]
    ppermute x9, waiting for transfers between devices: 9.35 us -> 14.9 us  [over_all(): return lax.ppermute(x, ('sec', 'mpo'), perm)]
    concatenate x1, other arithmetic: 1.95 us -> 0.44 us  [per_device(): jnp.concatenate([right_env, packed], axis=2).reshape(-1, dr + rows, dr)]
  transfers between devices with their start and end apart: 15 -> 15, of which waited for: 4 -> 6; matrix products, arithmetic and copies ran while one was open for 6% -> 6% of each run, Pallas kernels for 36% -> 29%
where the time goes in v4:
time: 78.8 us; the launch traced here: 78.6 us
  starting transfers between devices  25.8 us (33%)
  Pallas kernels  22.5 us (29%)
  waiting for transfers between devices  22.4 us (28%)
  other arithmetic  4.28 us (5%)
  local copies, waits for them, and re-layouts  3.43 us (4%)
    pallas_call x4, Pallas kernels, add_terms(): pl.pallas_call(functools.partial(term_kernel, plan, n_vec, len(envs), acc...  15.2 us
    ppermute x9, starting transfers between devices, over_all(): return lax.ppermute(x, ('sec', 'mpo'), perm)  15.2 us
    ppermute x9, waiting for transfers between devices, over_all(): return lax.ppermute(x, ('sec', 'mpo'), perm)  14.9 us
    ppermute x6, starting transfers between devices, over_mpo(): return lax.ppermute(x, 'mpo', perm)  10.6 us
    ppermute x6, waiting for transfers between devices, over_mpo(): return lax.ppermute(x, 'mpo', perm)  7.54 us
    pallas_call x1, Pallas kernels, make_lines(): pl.pallas_call(line_kernel, out_shape=[jax.ShapeDtypeStruct(shape, BF) fo...  2.81 us
    pallas_call x1, Pallas kernels, join(): pl.pallas_call(join_kernel, out_shape=jax.ShapeDtypeStruct((first.shape[0...  2.74 us
    pallas_call x1, Pallas kernels, make_lists(): pl.pallas_call(list_kernel, out_shape=jax.ShapeDtypeStruct(((PIECES + 1)...  1.74 us
  transfers between devices with their start and end apart: 15, of which 6 were waited for; matrix products, arithmetic and copies ran while one was open for 6% of the time, Pallas kernels for 29%

profile of v4, /device:TPU:1, one launch (start us, length us, event | category | flops | bytes accessed | tf_op | source)
XLA Modules:
  0.0 78.6 jit_solution(4223598534441135808)
XLA Ops:
  0.0 1.5 %fusion.18 = (bf16[4,16,32,64]{3,2,1,0:T(8,128)(2,1)S(1)}, bf16[4,16,32,64]{3,2,1,0:T(8,128)(2,1)S(1)}) fusion(bf16[4,16,64,64]{3,2,1,0:T(8,128)(2,1)} %param.6), kind=kLoop, calls=%fused_computation.90 | loop fusion | bytes 1048576 | tf_op jit(solution)/shard_map/slice | solution.py:222
  1.5 0.4 copy-done.1
  1.9 0.4 maximum_maximum_fusion
  2.4 1.5 %collective-permute-start.5 = (bf16[64,160,128]{2,1,0:T(8,128)(2,1)S(1)}, bf16[64,160,128]{2,1,0:T(8,128)(2,1)}, u32[]{:S(2)}, u32[]{:S(2)}) collective-permute-start(bf16[64,160,128]{2,1,0:T(8,128)(2,1)S(1)} %bitcast.14), channel_id=1, source_target_pairs={{0,1},{1,0},{2,3},{3,2},{4,5},{5,4},{6,7},{7,6},{8,9},{9,8},{10,11... | collective-permute-start | bytes 7864328 | tf_op jit(solution)/shard_map/ppermute | solution.py:50
  3.9 1.4 %collective-permute-start = (s32[4,16]{1,0:T(4,128)S(1)}, s32[4,16]{1,0:T(4,128)S(1)}, u32[]{:S(2)}, u32[]{:S(2)}) collective-permute-start(s32[4,16]{1,0:T(4,128)S(1)} %compare_select_fusion.24), channel_id=1, source_target_pairs={{0,6},{1,3},{2,0},{3,5},{4,2},{5,7},{6,4},{7,1},{8,14},{9,11},{10,... | collective-permute-start | bytes 776 | tf_op jit(solution)/shard_map/ppermute | solution.py:50
  5.2 1.1 %dynamic-slice_bitcast_fusion.1 = (bf16[1,16,64,128]{3,2,1,0:T(8,128)(2,1)S(1)}, bf16[1,16,64,128]{3,2,1,0:T(8,128)(2,1)S(1)}) fusion(bf16[16,8,64,128]{3,2,1,0:T(8,128)(2,1)} %param.5, s32[]{:T(128)S(6)} %select_n.241, s32[]{:T(128)S(6)} %select_n.242), kind=kLoop, calls=%fused_computation.5 | loop fusion | bytes 1048584 | tf_op jit(solution)/shard_map/stack;squeeze | solution.py:216
  6.3 0.1 pad_maximum_fusion.refs_0_
  6.4 3.0 %collective-permute-start.4 = (bf16[2,16,64,128]{3,2,1,0:T(8,128)(2,1)S(1)}, bf16[2,16,64,128]{3,2,1,0:T(8,128)(2,1)}, u32[]{:S(2)}, u32[]{:S(2)}) collective-permute-start(bf16[2,16,64,128]{3,2,1,0:T(8,128)(2,1)S(1)} %pad_maximum_fusion.refs_0_), channel_id=1, source_target_pairs={{0,64},{1,17},{2,66},{3,19},{4,68},{5,21},{6,70},{7,23},{8,72},{9,... | collective-permute-start | bytes 1572872 | tf_op jit(solution)/shard_map/ppermute | solution.py:46
  9.4 0.0 collective-permute-done
  9.4 1.2 %collective-permute-start.1 = (bf16[64,160,128]{2,1,0:T(8,128)(2,1)S(1)}, bf16[64,160,128]{2,1,0:T(8,128)(2,1)}, u32[]{:S(2)}, u32[]{:S(2)}) collective-permute-start(bf16[64,160,128]{2,1,0:T(8,128)(2,1)S(1)} %bitcast.15), channel_id=1, source_target_pairs={{0,6},{1,3},{2,0},{3,5},{4,2},{5,7},{6,4},{7,1},{8,14},{9,11},{10,... | collective-permute-start | bytes 7864328 | tf_op jit(solution)/shard_map/ppermute | solution.py:50
  10.6 2.2 %collective-permute-start.6 = (s32[2,4,16]{2,1,0:T(4,128)S(1)}, s32[2,4,16]{2,1,0:T(4,128)S(1)}, u32[]{:S(2)}, u32[]{:S(2)}) collective-permute-start(s32[2,4,16]{2,1,0:T(4,128)S(1)} %pad_add_fusion.1), channel_id=1, source_target_pairs={{0,1},{1,0},{2,3},{3,2},{4,5},{5,4},{6,7},{7,6},{8,9},{9,8},{10,11... | collective-permute-start | bytes 1544 | tf_op jit(solution)/shard_map/ppermute | solution.py:50
  12.8 1.3 %collective-permute-start.2 = (bf16[2,16,64,128]{3,2,1,0:T(8,128)(2,1)S(1)}, bf16[2,16,64,128]{3,2,1,0:T(8,128)(2,1)}, u32[]{:S(2)}, u32[]{:S(2)}) collective-permute-start(bf16[2,16,64,128]{3,2,1,0:T(8,128)(2,1)S(1)} %pad_maximum_fusion.refs_0_), channel_id=1, source_target_pairs={{0,32},{1,9},{2,34},{3,11},{4,36},{5,13},{6,38},{7,15},{8,40},{9,1... | collective-permute-start | bytes 1572872 | tf_op jit(solution)/shard_map/ppermute | solution.py:46
  14.1 2.3 %collective-permute-start.3 = (bf16[2,16,64,128]{3,2,1,0:T(8,128)(2,1)S(1)}, bf16[2,16,64,128]{3,2,1,0:T(8,128)(2,1)}, u32[]{:S(2)}, u32[]{:S(2)}) collective-permute-start(bf16[2,16,64,128]{3,2,1,0:T(8,128)(2,1)S(1)} %pad_maximum_fusion.refs_0_), channel_id=1, source_target_pairs={{0,96},{1,25},{2,98},{3,27},{4,100},{5,29},{6,102},{7,31},{8,104},... | collective-permute-start | bytes 1572872 | tf_op jit(solution)/shard_map/ppermute | solution.py:46
  16.4 0.0 collective-permute-done.4.refs_3_
  16.4 0.0 collective-permute-done.5.refs_1_
  16.4 0.1 stack.25
  16.5 0.1 stack.24
  16.6 5.9 %collective-permute-done.2.refs_1_ = bf16[2,16,64,128]{3,2,1,0:T(8,128)(2,1)} collective-permute-done((bf16[2,16,64,128]{3,2,1,0:T(8,128)(2,1)S(1)}, bf16[2,16,64,128]{3,2,1,0:T(8,128)(2,1)}, u32[]{:S(2)}, u32[]{:S(2)}) %collective-permute-start.2) | collective-permute-done | bytes 524320 | tf_op jit(solution)/shard_map/ppermute | solution.py:46
  22.5 0.0 collective-permute-done.3.refs_2_
  22.5 2.8 %shard_map.55 = (bf16[64,64,128]{2,1,0:T(8,128)(2,1)}, bf16[64,64,128]{2,1,0:T(8,128)(2,1)}) custom-call(bf16[2,16,64,128]{3,2,1,0:T(8,128)(2,1)S(1)} %pad_maximum_fusion.refs_0_, bf16[2,16,64,128]{3,2,1,0:T(8,128)(2,1)} %collective-permute-done.2.refs_1_, bf16[2,16,64,128]{3,2,1,0:T(8,128)(2,1)} %collective-permute-done.3.refs_2_, ...), custom_call_target="tpu_custom_call" | custom-call | flops 7000000000 | bytes 4000000 | tf_op jit(solution)/shard_map/pallas_call | solution.py:197
  25.3 1.4 %collective-permute-start.7 = (bf16[64,64,128]{2,1,0:T(8,128)(2,1)}, bf16[64,64,128]{2,1,0:T(8,128)(2,1)}, u32[]{:S(2)}, u32[]{:S(2)}) collective-permute-start(bf16[64,64,128]{2,1,0:T(8,128)(2,1)} %get-tuple-element.21.refs_1_), channel_id=1, source_target_pairs={{0,8},{1,33},{2,10},{3,35},{4,12},{5,37},{6,14},{7,39},{8,16},{9,4... | collective-permute-start | bytes 3145736 | tf_op jit(solution)/shard_map/ppermute | solution.py:46
  26.8 2.1 %collective-permute-start.8 = (bf16[64,64,128]{2,1,0:T(8,128)(2,1)}, bf16[64,64,128]{2,1,0:T(8,128)(2,1)}, u32[]{:S(2)}, u32[]{:S(2)}) collective-permute-start(bf16[64,64,128]{2,1,0:T(8,128)(2,1)} %get-tuple-element.22.refs_2_), channel_id=1, source_target_pairs={{0,24},{1,97},{2,26},{3,99},{4,28},{5,101},{6,30},{7,103},{8,0},{9... | collective-permute-start | bytes 3145736 | tf_op jit(solution)/shard_map/ppermute | solution.py:46
  29.0 1.5 %reduce-window.6 = s32[5,2,128]{2,1,0:T(2,128)S(1)} reduce-window(s32[5,2,128]{2,1,0:T(2,128)S(1)} %fusion.1, s32[]{:T(128)} %constant.127.clone.1), window={size=1x1x128 pad=0_0x0_0x127_0}, to_apply=%region_0.1 | reduce-window | flops 162560 | bytes 10244 | tf_op jit(solution)/shard_map/reduce-window
  30.5 0.1 slice.32
  30.6 0.1 copy.9
  30.7 0.1 copy.10
  30.8 0.1 select_reduce_fusion
  30.9 0.6 fusion.13
  31.5 0.6 bitcast_add_fusion
  32.1 1.7 %shard_map.56.list_ref = s32[1280]{0:T(1024)} custom-call(s32[256]{0:T(256)} %get-tuple-element.33.place_ref, s32[256]{0:T(256)} %get-tuple-element.31.entry_ref), custom_call_target="tpu_custom_call" | custom-call | tf_op jit(solution)/shard_map/pallas_call | solution.py:73
  33.8 0.1 convert_reduce_fusion.count_ref
  34.0 7.5 %collective-permute-done.1.refs_2_ = bf16[64,160,128]{2,1,0:T(8,128)(2,1)} collective-permute-done((bf16[64,160,128]{2,1,0:T(8,128)(2,1)S(1)}, bf16[64,160,128]{2,1,0:T(8,128)(2,1)}, u32[]{:S(2)}, u32[]{:S(2)}) %collective-permute-start.1) | collective-permute-done | bytes 2621472 | tf_op jit(solution)/shard_map/ppermute | solution.py:50
  41.5 0.2 collective-permute-done.7.refs_3_
  41.7 0.0 collective-permute-done.8.refs_1_
  41.7 3.7 %collective-permute-start.9 = (bf16[64,160,128]{2,1,0:T(8,128)(2,1)}, bf16[64,160,128]{2,1,0:T(8,128)(2,1)S(1)}, u32[]{:S(2)}, u32[]{:S(2)}) collective-permute-start(bf16[64,160,128]{2,1,0:T(8,128)(2,1)} %collective-permute-done.1.refs_2_), channel_id=1, source_target_pairs={{0,1},{1,0},{2,3},{3,2},{4,5},{5,4},{6,7},{7,6},{8,9},{9,8},{10,11... | collective-permute-start | bytes 7864328 | tf_op jit(solution)/shard_map/ppermute | solution.py:50
  45.4 2.4 %collective-permute-start.12 = (bf16[64,64,128]{2,1,0:T(8,128)(2,1)}, bf16[64,64,128]{2,1,0:T(8,128)(2,1)S(1)}, u32[]{:S(2)}, u32[]{:S(2)}) collective-permute-start(bf16[64,64,128]{2,1,0:T(8,128)(2,1)} %get-tuple-element.21.refs_1_), channel_id=1, source_target_pairs={{0,24},{1,97},{2,26},{3,99},{4,28},{5,101},{6,30},{7,103},{8,0},{9... | collective-permute-start | bytes 3145736 | tf_op jit(solution)/shard_map/ppermute | solution.py:46
  47.8 0.0 collective-permute-start.13
  47.8 2.7 %collective-permute-start.11 = (bf16[64,64,128]{2,1,0:T(8,128)(2,1)}, bf16[64,64,128]{2,1,0:T(8,128)(2,1)S(1)}, u32[]{:S(2)}, u32[]{:S(2)}) collective-permute-start(bf16[64,64,128]{2,1,0:T(8,128)(2,1)} %collective-permute-done.8.refs_1_), channel_id=1, source_target_pairs={{0,24},{1,97},{2,26},{3,99},{4,28},{5,101},{6,30},{7,103},{8,0},{9... | collective-permute-start | bytes 3145736 | tf_op jit(solution)/shard_map/ppermute | solution.py:46
  50.5 2.7 %shard_map.57.refs_0_ = bf16[256,160,128]{2,1,0:T(8,128)(2,1)S(1)} custom-call(bf16[64,160,128]{2,1,0:T(8,128)(2,1)S(1)} %bitcast.16, bf16[64,160,128]{2,1,0:T(8,128)(2,1)} %collective-permute-done.5.refs_1_, bf16[64,160,128]{2,1,0:T(8,128)(2,1)} %collective-permute-done.1.refs_2_, bf16[64,160,128]{2,1,0:T(8,128)(2,1)S(1)} %collective-permute-done.9.refs_3_), custom_call_target="tpu_custom_call" | custom-call | bytes 10000000 | tf_op jit(solution)/shard_map/pallas_call | solution.py:174
  53.2 5.8 %shard_map.58 = (f32[16,64,128]{2,1,0:T(8,128)S(1)}, f32[16,64,128]{2,1,0:T(8,128)S(1)}) custom-call(s32[1280]{0:T(1024)S(1)} %copy-done, s32[5]{0:T(128)S(1)} %convert_reduce_fusion.count_ref, bf16[256,160,128]{2,1,0:T(8,128)(2,1)S(1)} %shard_map.57.refs_0_, bf16[64,64,128]{2,1,0:T(8,128)(2,1)} %get-tuple-element.21.refs_1_, ...), custom_call_target="tpu_custom_call" | custom-call | flops 3000000000 | bytes 12000000 | tf_op jit(solution)/shard_map/pallas_call | solution.py:147
  59.0 0.8 %collective-permute-done.12.refs_1_ = bf16[64,64,128]{2,1,0:T(8,128)(2,1)S(1)} collective-permute-done((bf16[64,64,128]{2,1,0:T(8,128)(2,1)}, bf16[64,64,128]{2,1,0:T(8,128)(2,1)S(1)}, u32[]{:S(2)}, u32[]{:S(2)}) %collective-permute-start.12) | collective-permute-done | bytes 1048608 | tf_op jit(solution)/shard_map/ppermute | solution.py:46
  59.8 3.3 %collective-permute-done.13.refs_2_ = bf16[64,64,128]{2,1,0:T(8,128)(2,1)S(1)} collective-permute-done((bf16[64,64,128]{2,1,0:T(8,128)(2,1)}, bf16[64,64,128]{2,1,0:T(8,128)(2,1)S(1)}, u32[]{:S(2)}, u32[]{:S(2)}) %collective-permute-start.13) | collective-permute-done | bytes 1048608 | tf_op jit(solution)/shard_map/ppermute | solution.py:46
  63.1 3.4 %shard_map.61 = bf16[16,64,128]{2,1,0:T(8,128)(2,1)S(1)} custom-call(s32[1280]{0:T(1024)S(1)} %copy-done, s32[5]{0:T(128)S(1)} %convert_reduce_fusion.count_ref, bf16[256,160,128]{2,1,0:T(8,128)(2,1)S(1)} %shard_map.57.refs_0_, bf16[64,64,128]{2,1,0:T(8,128)(2,1)S(1)} %collective-permute-done.12.refs_1_, ...), custom_call_target="tpu_custom_call" | custom-call | flops 3000000000 | bytes 12000000 | tf_op jit(solution)/shard_map/pallas_call | solution.py:147
  66.5 0.6 collective-permute-start.14
  67.1 2.7 %shard_map.59.refs_3_ = f32[16,64,128]{2,1,0:T(8,128)S(1)} custom-call(s32[1280]{0:T(1024)S(1)} %copy-done, s32[5]{0:T(128)S(1)} %convert_reduce_fusion.count_ref, bf16[256,160,128]{2,1,0:T(8,128)(2,1)S(1)} %shard_map.57.refs_0_, bf16[64,64,128]{2,1,0:T(8,128)(2,1)} %collective-permute-done.8.refs_1_, f32[16,64,128]{2,1,0:T(8,128)S(1)} %get-tuple-element.29.refs_2_), custom_call_target="tpu_custom_call" | custom-call | flops 3000000000 | bytes 12000000 | tf_op jit(solution)/shard_map/pallas_call | solution.py:147
  69.8 4.6 %collective-permute-done.10.refs_1_ = bf16[64,64,128]{2,1,0:T(8,128)(2,1)S(1)} collective-permute-done((bf16[64,64,128]{2,1,0:T(8,128)(2,1)}, bf16[64,64,128]{2,1,0:T(8,128)(2,1)S(1)}, u32[]{:S(2)}, u32[]{:S(2)}) %collective-permute-start.10) | collective-permute-done | bytes 1048608 | tf_op jit(solution)/shard_map/ppermute | solution.py:46
  74.4 3.4 %shard_map.60 = f32[16,64,128]{2,1,0:T(8,128)S(1)} custom-call(s32[1280]{0:T(1024)S(1)} %copy-done, s32[5]{0:T(128)S(1)} %convert_reduce_fusion.count_ref, bf16[256,160,128]{2,1,0:T(8,128)(2,1)S(1)} %shard_map.57.refs_0_, bf16[64,64,128]{2,1,0:T(8,128)(2,1)S(1)} %collective-permute-done.10.refs_1_, bf16[64,64,128]{2,1,0:T(8,128)(2,1)S(1)} %collective-permute-done.11.refs_2_, ...), custom_call_target="tpu_custom_call" | custom-call | flops 3000000000 | bytes 12000000 | tf_op jit(solution)/shard_map/pallas_call | solution.py:147
  77.8 0.8 fusion
  (20 shorter events, 0.1 us)
Async XLA Ops:
  0.0 1.9 %copy-start.1 = (bf16[4,16,128,128]{3,2,1,0:T(8,128)(2,1)S(1)}, bf16[4,16,128,128]{3,2,1,0:T(8,128)(2,1)}, u32[]{:S(2)}) copy-start(bf16[4,16,128,128]{3,2,1,0:T(8,128)(2,1)} %param.7) | copy-start | bytes 6291460
  1.9 2.0 %copy-start.2 = (s32[4,16]{1,0:T(4,128)S(1)}, s32[4,16]{1,0:T(4,128)}, u32[]{:S(2)}) copy-start(s32[4,16]{1,0:T(4,128)} %param.8) | copy-start | bytes 772
  1.9 2.0 %copy-start.3 = (s32[4,16]{1,0:T(4,128)S(1)}, s32[4,16]{1,0:T(4,128)}, u32[]{:S(2)}) copy-start(s32[4,16]{1,0:T(4,128)} %param.9) | copy-start | bytes 772
  2.4 14.0 %collective-permute-start.5 = (bf16[64,160,128]{2,1,0:T(8,128)(2,1)S(1)}, bf16[64,160,128]{2,1,0:T(8,128)(2,1)}, u32[]{:S(2)}, u32[]{:S(2)}) collective-permute-start(bf16[64,160,128]{2,1,0:T(8,128)(2,1)S(1)} %bitcast.14), channel_id=1, source_target_pairs={{0,1},{1,0},{2,3},{3,2},{4,5},{5,4},{6,7},{7,6},{8,9},{9,8},{10,11... | collective-permute-start | bytes 7864328 | tf_op jit(solution)/shard_map/ppermute | solution.py:50
  3.9 5.5 %collective-permute-start = (s32[4,16]{1,0:T(4,128)S(1)}, s32[4,16]{1,0:T(4,128)S(1)}, u32[]{:S(2)}, u32[]{:S(2)}) collective-permute-start(s32[4,16]{1,0:T(4,128)S(1)} %compare_select_fusion.24), channel_id=1, source_target_pairs={{0,6},{1,3},{2,0},{3,5},{4,2},{5,7},{6,4},{7,1},{8,14},{9,11},{10,... | collective-permute-start | bytes 776 | tf_op jit(solution)/shard_map/ppermute | solution.py:50
  6.4 10.0 %collective-permute-start.4 = (bf16[2,16,64,128]{3,2,1,0:T(8,128)(2,1)S(1)}, bf16[2,16,64,128]{3,2,1,0:T(8,128)(2,1)}, u32[]{:S(2)}, u32[]{:S(2)}) collective-permute-start(bf16[2,16,64,128]{3,2,1,0:T(8,128)(2,1)S(1)} %pad_maximum_fusion.refs_0_), channel_id=1, source_target_pairs={{0,64},{1,17},{2,66},{3,19},{4,68},{5,21},{6,70},{7,23},{8,72},{9,... | collective-permute-start | bytes 1572872 | tf_op jit(solution)/shard_map/ppermute | solution.py:46
  9.4 32.1 %collective-permute-start.1 = (bf16[64,160,128]{2,1,0:T(8,128)(2,1)S(1)}, bf16[64,160,128]{2,1,0:T(8,128)(2,1)}, u32[]{:S(2)}, u32[]{:S(2)}) collective-permute-start(bf16[64,160,128]{2,1,0:T(8,128)(2,1)S(1)} %bitcast.15), channel_id=1, source_target_pairs={{0,6},{1,3},{2,0},{3,5},{4,2},{5,7},{6,4},{7,1},{8,14},{9,11},{10,... | collective-permute-start | bytes 7864328 | tf_op jit(solution)/shard_map/ppermute | solution.py:50
  10.6 3.5 %collective-permute-start.6 = (s32[2,4,16]{2,1,0:T(4,128)S(1)}, s32[2,4,16]{2,1,0:T(4,128)S(1)}, u32[]{:S(2)}, u32[]{:S(2)}) collective-permute-start(s32[2,4,16]{2,1,0:T(4,128)S(1)} %pad_add_fusion.1), channel_id=1, source_target_pairs={{0,1},{1,0},{2,3},{3,2},{4,5},{5,4},{6,7},{7,6},{8,9},{9,8},{10,11... | collective-permute-start | bytes 1544 | tf_op jit(solution)/shard_map/ppermute | solution.py:50
  12.8 9.7 %collective-permute-start.2 = (bf16[2,16,64,128]{3,2,1,0:T(8,128)(2,1)S(1)}, bf16[2,16,64,128]{3,2,1,0:T(8,128)(2,1)}, u32[]{:S(2)}, u32[]{:S(2)}) collective-permute-start(bf16[2,16,64,128]{3,2,1,0:T(8,128)(2,1)S(1)} %pad_maximum_fusion.refs_0_), channel_id=1, source_target_pairs={{0,32},{1,9},{2,34},{3,11},{4,36},{5,13},{6,38},{7,15},{8,40},{9,1... | collective-permute-start | bytes 1572872 | tf_op jit(solution)/shard_map/ppermute | solution.py:46
  14.1 8.4 %collective-permute-start.3 = (bf16[2,16,64,128]{3,2,1,0:T(8,128)(2,1)S(1)}, bf16[2,16,64,128]{3,2,1,0:T(8,128)(2,1)}, u32[]{:S(2)}, u32[]{:S(2)}) collective-permute-start(bf16[2,16,64,128]{3,2,1,0:T(8,128)(2,1)S(1)} %pad_maximum_fusion.refs_0_), channel_id=1, source_target_pairs={{0,96},{1,25},{2,98},{3,27},{4,100},{5,29},{6,102},{7,31},{8,104},... | collective-permute-start | bytes 1572872 | tf_op jit(solution)/shard_map/ppermute | solution.py:46
  25.3 16.4 %collective-permute-start.7 = (bf16[64,64,128]{2,1,0:T(8,128)(2,1)}, bf16[64,64,128]{2,1,0:T(8,128)(2,1)}, u32[]{:S(2)}, u32[]{:S(2)}) collective-permute-start(bf16[64,64,128]{2,1,0:T(8,128)(2,1)} %get-tuple-element.21.refs_1_), channel_id=1, source_target_pairs={{0,8},{1,33},{2,10},{3,35},{4,12},{5,37},{6,14},{7,39},{8,16},{9,4... | collective-permute-start | bytes 3145736 | tf_op jit(solution)/shard_map/ppermute | solution.py:46
  26.8 14.9 %collective-permute-start.8 = (bf16[64,64,128]{2,1,0:T(8,128)(2,1)}, bf16[64,64,128]{2,1,0:T(8,128)(2,1)}, u32[]{:S(2)}, u32[]{:S(2)}) collective-permute-start(bf16[64,64,128]{2,1,0:T(8,128)(2,1)} %get-tuple-element.22.refs_2_), channel_id=1, source_target_pairs={{0,24},{1,97},{2,26},{3,99},{4,28},{5,101},{6,30},{7,103},{8,0},{9... | collective-permute-start | bytes 3145736 | tf_op jit(solution)/shard_map/ppermute | solution.py:46
  33.9 19.3 %copy-start = (s32[1280]{0:T(1024)S(1)}, s32[1280]{0:T(1024)}, u32[]{:S(2)}) copy-start(s32[1280]{0:T(1024)} %shard_map.56.list_ref) | copy-start | bytes 15364
  41.7 8.8 %collective-permute-start.9 = (bf16[64,160,128]{2,1,0:T(8,128)(2,1)}, bf16[64,160,128]{2,1,0:T(8,128)(2,1)S(1)}, u32[]{:S(2)}, u32[]{:S(2)}) collective-permute-start(bf16[64,160,128]{2,1,0:T(8,128)(2,1)} %collective-permute-done.1.refs_2_), channel_id=1, source_target_pairs={{0,1},{1,0},{2,3},{3,2},{4,5},{5,4},{6,7},{7,6},{8,9},{9,8},{10,11... | collective-permute-start | bytes 7864328 | tf_op jit(solution)/shard_map/ppermute | solution.py:50
  45.4 14.5 %collective-permute-start.12 = (bf16[64,64,128]{2,1,0:T(8,128)(2,1)}, bf16[64,64,128]{2,1,0:T(8,128)(2,1)S(1)}, u32[]{:S(2)}, u32[]{:S(2)}) collective-permute-start(bf16[64,64,128]{2,1,0:T(8,128)(2,1)} %get-tuple-element.21.refs_1_), channel_id=1, source_target_pairs={{0,24},{1,97},{2,26},{3,99},{4,28},{5,101},{6,30},{7,103},{8,0},{9... | collective-permute-start | bytes 3145736 | tf_op jit(solution)/shard_map/ppermute | solution.py:46
  47.8 15.4 %collective-permute-start.13 = (bf16[64,64,128]{2,1,0:T(8,128)(2,1)}, bf16[64,64,128]{2,1,0:T(8,128)(2,1)S(1)}, u32[]{:S(2)}, u32[]{:S(2)}) collective-permute-start(bf16[64,64,128]{2,1,0:T(8,128)(2,1)} %collective-permute-done.7.refs_3_), channel_id=1, source_target_pairs={{0,8},{1,33},{2,10},{3,35},{4,12},{5,37},{6,14},{7,39},{8,16},{9,4... | collective-permute-start | bytes 3145736 | tf_op jit(solution)/shard_map/ppermute | solution.py:46
  47.8 26.6 %collective-permute-start.10 = (bf16[64,64,128]{2,1,0:T(8,128)(2,1)}, bf16[64,64,128]{2,1,0:T(8,128)(2,1)S(1)}, u32[]{:S(2)}, u32[]{:S(2)}) collective-permute-start(bf16[64,64,128]{2,1,0:T(8,128)(2,1)} %get-tuple-element.22.refs_2_), channel_id=1, source_target_pairs={{0,8},{1,33},{2,10},{3,35},{4,12},{5,37},{6,14},{7,39},{8,16},{9,4... | collective-permute-start | bytes 3145736 | tf_op jit(solution)/shard_map/ppermute | solution.py:46
  47.8 26.6 %collective-permute-start.11 = (bf16[64,64,128]{2,1,0:T(8,128)(2,1)}, bf16[64,64,128]{2,1,0:T(8,128)(2,1)S(1)}, u32[]{:S(2)}, u32[]{:S(2)}) collective-permute-start(bf16[64,64,128]{2,1,0:T(8,128)(2,1)} %collective-permute-done.8.refs_1_), channel_id=1, source_target_pairs={{0,24},{1,97},{2,26},{3,99},{4,28},{5,101},{6,30},{7,103},{8,0},{9... | collective-permute-start | bytes 3145736 | tf_op jit(solution)/shard_map/ppermute | solution.py:46
  66.5 11.2 %collective-permute-start.14 = (bf16[16,64,128]{2,1,0:T(8,128)(2,1)S(1)}, bf16[16,64,128]{2,1,0:T(8,128)(2,1)S(1)}, u32[]{:S(2)}, u32[]{:S(2)}) collective-permute-start(bf16[16,64,128]{2,1,0:T(8,128)(2,1)S(1)} %shard_map.61), channel_id=1, source_target_pairs={{0,4},{1,5},{2,6},{3,7},{4,0},{5,1},{6,2},{7,3},{8,12},{9,13},{10,... | collective-permute-start | bytes 786440 | tf_op jit(solution)/shard_map/ppermute | solution.py:50

commit v5 on v4

--- a/solution.py
+++ b/solution.py
@@ -256,7 +256,8 @@
 
     plan = [(0, (0, 1)), (1, (0,))]
     away, home = added(plan, [lines[0], lines[1], lines_up[0]], None)
-    (away,) = added([(2, (0,)), (3, (0,))], [lines_down[0], lasts[0]], [away], BF)
+    (away,) = added([(3, (0,))], [lasts[0]], [away])
+    (away,) = added([(2, (0,))], [lines_down[0]], [away], BF)
     arrived = over_mpo(away, FAR)
     (home,) = added([(2, (0,))], [lines_down[1]], [home])
     (home,) = added([(1, (0,)), (3, (0,))], [lines_up[1], lasts[1]], [home])

time: 78.8 us -> 77 us (0.977)
  waiting for transfers between devices: 22.4 us -> 18.9 us
  Pallas kernels: 22.5 us -> 24.6 us
    ppermute x9, waiting for transfers between devices: 14.9 us -> 11.4 us  [over_all(): return lax.ppermute(x, ('sec', 'mpo'), perm)]
    pallas_call x4 -> x5, Pallas kernels: 15.2 us -> 17.3 us  [add_terms(): pl.pallas_call(functools.partial(term_kernel, plan, n_vec, len(envs), acc...]
  transfers between devices with their start and end apart: 15 -> 15, of which waited for: 6 -> 5; matrix products, arithmetic and copies ran while one was open for 6% -> 6% of each run, Pallas kernels for 29% -> 32%
where the time goes in v5:
time: 77 us; the launch traced here: 76.9 us
  starting transfers between devices  25.5 us (33%)
  Pallas kernels  24.6 us (32%)
  waiting for transfers between devices  18.9 us (25%)
  other arithmetic  4.28 us (6%)
  local copies, waits for them, and re-layouts  3.43 us (4%)
    pallas_call x5, Pallas kernels, add_terms(): pl.pallas_call(functools.partial(term_kernel, plan, n_vec, len(envs), acc...  17.3 us
    ppermute x9, starting transfers between devices, over_all(): return lax.ppermute(x, ('sec', 'mpo'), perm)  15.5 us
    ppermute x9, waiting for transfers between devices, over_all(): return lax.ppermute(x, ('sec', 'mpo'), perm)  11.4 us
    ppermute x6, starting transfers between devices, over_mpo(): return lax.ppermute(x, 'mpo', perm)  10 us
    ppermute x6, waiting for transfers between devices, over_mpo(): return lax.ppermute(x, 'mpo', perm)  7.54 us
    pallas_call x1, Pallas kernels, make_lines(): pl.pallas_call(line_kernel, out_shape=[jax.ShapeDtypeStruct(shape, BF) fo...  2.81 us
    pallas_call x1, Pallas kernels, join(): pl.pallas_call(join_kernel, out_shape=jax.ShapeDtypeStruct((first.shape[0...  2.74 us
    pallas_call x1, Pallas kernels, make_lists(): pl.pallas_call(list_kernel, out_shape=jax.ShapeDtypeStruct(((PIECES + 1)...  1.74 us
  transfers between devices with their start and end apart: 15, of which 5 were waited for; matrix products, arithmetic and copies ran while one was open for 6% of the time, Pallas kernels for 32%

profile of v5, /device:TPU:1, one launch (start us, length us, event | category | flops | bytes accessed | tf_op | source)
XLA Modules:
  0.0 76.9 jit_solution(2712206651357885920)
XLA Ops:
  0.0 1.5 %fusion.18 = (bf16[4,16,32,64]{3,2,1,0:T(8,128)(2,1)S(1)}, bf16[4,16,32,64]{3,2,1,0:T(8,128)(2,1)S(1)}) fusion(bf16[4,16,64,64]{3,2,1,0:T(8,128)(2,1)} %param.6), kind=kLoop, calls=%fused_computation.90 | loop fusion | bytes 1048576 | tf_op jit(solution)/shard_map/slice | solution.py:222
  1.5 0.4 copy-done.1
  1.9 0.4 maximum_maximum_fusion
  2.4 1.5 %collective-permute-start.5 = (bf16[64,160,128]{2,1,0:T(8,128)(2,1)S(1)}, bf16[64,160,128]{2,1,0:T(8,128)(2,1)}, u32[]{:S(2)}, u32[]{:S(2)}) collective-permute-start(bf16[64,160,128]{2,1,0:T(8,128)(2,1)S(1)} %bitcast.14), channel_id=1, source_target_pairs={{0,1},{1,0},{2,3},{3,2},{4,5},{5,4},{6,7},{7,6},{8,9},{9,8},{10,11... | collective-permute-start | bytes 7864328 | tf_op jit(solution)/shard_map/ppermute | solution.py:50
  3.9 1.4 %collective-permute-start = (s32[4,16]{1,0:T(4,128)S(1)}, s32[4,16]{1,0:T(4,128)S(1)}, u32[]{:S(2)}, u32[]{:S(2)}) collective-permute-start(s32[4,16]{1,0:T(4,128)S(1)} %compare_select_fusion.24), channel_id=1, source_target_pairs={{0,6},{1,3},{2,0},{3,5},{4,2},{5,7},{6,4},{7,1},{8,14},{9,11},{10,... | collective-permute-start | bytes 776 | tf_op jit(solution)/shard_map/ppermute | solution.py:50
  5.2 1.1 %dynamic-slice_bitcast_fusion.1 = (bf16[1,16,64,128]{3,2,1,0:T(8,128)(2,1)S(1)}, bf16[1,16,64,128]{3,2,1,0:T(8,128)(2,1)S(1)}) fusion(bf16[16,8,64,128]{3,2,1,0:T(8,128)(2,1)} %param.5, s32[]{:T(128)S(6)} %select_n.241, s32[]{:T(128)S(6)} %select_n.242), kind=kLoop, calls=%fused_computation.5 | loop fusion | bytes 1048584 | tf_op jit(solution)/shard_map/stack;squeeze | solution.py:216
  6.3 0.1 pad_maximum_fusion.refs_0_
  6.4 3.0 %collective-permute-start.4 = (bf16[2,16,64,128]{3,2,1,0:T(8,128)(2,1)S(1)}, bf16[2,16,64,128]{3,2,1,0:T(8,128)(2,1)}, u32[]{:S(2)}, u32[]{:S(2)}) collective-permute-start(bf16[2,16,64,128]{3,2,1,0:T(8,128)(2,1)S(1)} %pad_maximum_fusion.refs_0_), channel_id=1, source_target_pairs={{0,64},{1,17},{2,66},{3,19},{4,68},{5,21},{6,70},{7,23},{8,72},{9,... | collective-permute-start | bytes 1572872 | tf_op jit(solution)/shard_map/ppermute | solution.py:46
  9.4 1.2 %collective-permute-start.1 = (bf16[64,160,128]{2,1,0:T(8,128)(2,1)S(1)}, bf16[64,160,128]{2,1,0:T(8,128)(2,1)}, u32[]{:S(2)}, u32[]{:S(2)}) collective-permute-start(bf16[64,160,128]{2,1,0:T(8,128)(2,1)S(1)} %bitcast.15), channel_id=1, source_target_pairs={{0,6},{1,3},{2,0},{3,5},{4,2},{5,7},{6,4},{7,1},{8,14},{9,11},{10,... | collective-permute-start | bytes 7864328 | tf_op jit(solution)/shard_map/ppermute | solution.py:50
  10.6 2.2 %collective-permute-start.6 = (s32[2,4,16]{2,1,0:T(4,128)S(1)}, s32[2,4,16]{2,1,0:T(4,128)S(1)}, u32[]{:S(2)}, u32[]{:S(2)}) collective-permute-start(s32[2,4,16]{2,1,0:T(4,128)S(1)} %pad_add_fusion.1), channel_id=1, source_target_pairs={{0,1},{1,0},{2,3},{3,2},{4,5},{5,4},{6,7},{7,6},{8,9},{9,8},{10,11... | collective-permute-start | bytes 1544 | tf_op jit(solution)/shard_map/ppermute | solution.py:50
  12.8 1.3 %collective-permute-start.2 = (bf16[2,16,64,128]{3,2,1,0:T(8,128)(2,1)S(1)}, bf16[2,16,64,128]{3,2,1,0:T(8,128)(2,1)}, u32[]{:S(2)}, u32[]{:S(2)}) collective-permute-start(bf16[2,16,64,128]{3,2,1,0:T(8,128)(2,1)S(1)} %pad_maximum_fusion.refs_0_), channel_id=1, source_target_pairs={{0,32},{1,9},{2,34},{3,11},{4,36},{5,13},{6,38},{7,15},{8,40},{9,1... | collective-permute-start | bytes 1572872 | tf_op jit(solution)/shard_map/ppermute | solution.py:46
  14.1 0.0 collective-permute-done.6
  14.1 2.3 %collective-permute-start.3 = (bf16[2,16,64,128]{3,2,1,0:T(8,128)(2,1)S(1)}, bf16[2,16,64,128]{3,2,1,0:T(8,128)(2,1)}, u32[]{:S(2)}, u32[]{:S(2)}) collective-permute-start(bf16[2,16,64,128]{3,2,1,0:T(8,128)(2,1)S(1)} %pad_maximum_fusion.refs_0_), channel_id=1, source_target_pairs={{0,96},{1,25},{2,98},{3,27},{4,100},{5,29},{6,102},{7,31},{8,104},... | collective-permute-start | bytes 1572872 | tf_op jit(solution)/shard_map/ppermute | solution.py:46
  16.4 0.0 collective-permute-done.4.refs_3_
  16.4 0.1 stack.25
  16.5 0.1 stack.24
  16.6 5.9 %collective-permute-done.2.refs_1_ = bf16[2,16,64,128]{3,2,1,0:T(8,128)(2,1)} collective-permute-done((bf16[2,16,64,128]{3,2,1,0:T(8,128)(2,1)S(1)}, bf16[2,16,64,128]{3,2,1,0:T(8,128)(2,1)}, u32[]{:S(2)}, u32[]{:S(2)}) %collective-permute-start.2) | collective-permute-done | bytes 524320 | tf_op jit(solution)/shard_map/ppermute | solution.py:46
  22.5 0.0 collective-permute-done.3.refs_2_
  22.5 2.8 %shard_map.55 = (bf16[64,64,128]{2,1,0:T(8,128)(2,1)}, bf16[64,64,128]{2,1,0:T(8,128)(2,1)}) custom-call(bf16[2,16,64,128]{3,2,1,0:T(8,128)(2,1)S(1)} %pad_maximum_fusion.refs_0_, bf16[2,16,64,128]{3,2,1,0:T(8,128)(2,1)} %collective-permute-done.2.refs_1_, bf16[2,16,64,128]{3,2,1,0:T(8,128)(2,1)} %collective-permute-done.3.refs_2_, ...), custom_call_target="tpu_custom_call" | custom-call | flops 7000000000 | bytes 4000000 | tf_op jit(solution)/shard_map/pallas_call | solution.py:197
  25.3 1.4 %collective-permute-start.7 = (bf16[64,64,128]{2,1,0:T(8,128)(2,1)}, bf16[64,64,128]{2,1,0:T(8,128)(2,1)}, u32[]{:S(2)}, u32[]{:S(2)}) collective-permute-start(bf16[64,64,128]{2,1,0:T(8,128)(2,1)} %get-tuple-element.21.refs_1_), channel_id=1, source_target_pairs={{0,8},{1,33},{2,10},{3,35},{4,12},{5,37},{6,14},{7,39},{8,16},{9,4... | collective-permute-start | bytes 3145736 | tf_op jit(solution)/shard_map/ppermute | solution.py:46
  26.8 2.1 %collective-permute-start.8 = (bf16[64,64,128]{2,1,0:T(8,128)(2,1)}, bf16[64,64,128]{2,1,0:T(8,128)(2,1)}, u32[]{:S(2)}, u32[]{:S(2)}) collective-permute-start(bf16[64,64,128]{2,1,0:T(8,128)(2,1)} %get-tuple-element.22.refs_2_), channel_id=1, source_target_pairs={{0,24},{1,97},{2,26},{3,99},{4,28},{5,101},{6,30},{7,103},{8,0},{9... | collective-permute-start | bytes 3145736 | tf_op jit(solution)/shard_map/ppermute | solution.py:46
  29.0 1.5 %reduce-window.6 = s32[5,2,128]{2,1,0:T(2,128)S(1)} reduce-window(s32[5,2,128]{2,1,0:T(2,128)S(1)} %fusion.1, s32[]{:T(128)} %constant.127.clone.1), window={size=1x1x128 pad=0_0x0_0x127_0}, to_apply=%region_0.1 | reduce-window | flops 162560 | bytes 10244 | tf_op jit(solution)/shard_map/reduce-window
  30.5 0.1 slice.32
  30.6 0.1 copy.9
  30.7 0.1 copy.10
  30.8 0.1 select_reduce_fusion
  30.9 0.6 fusion.13
  31.5 0.6 bitcast_add_fusion
  32.1 1.7 %shard_map.56.list_ref = s32[1280]{0:T(1024)} custom-call(s32[256]{0:T(256)} %get-tuple-element.33.place_ref, s32[256]{0:T(256)} %get-tuple-element.31.entry_ref), custom_call_target="tpu_custom_call" | custom-call | tf_op jit(solution)/shard_map/pallas_call | solution.py:73
  33.8 0.1 convert_reduce_fusion.count_ref
  34.0 7.5 %collective-permute-done.1.refs_2_ = bf16[64,160,128]{2,1,0:T(8,128)(2,1)} collective-permute-done((bf16[64,160,128]{2,1,0:T(8,128)(2,1)S(1)}, bf16[64,160,128]{2,1,0:T(8,128)(2,1)}, u32[]{:S(2)}, u32[]{:S(2)}) %collective-permute-start.1) | collective-permute-done | bytes 2621472 | tf_op jit(solution)/shard_map/ppermute | solution.py:50
  41.5 0.2 collective-permute-done.7.refs_3_
  41.7 0.0 collective-permute-done.8.refs_1_
  41.7 3.7 %collective-permute-start.9 = (bf16[64,160,128]{2,1,0:T(8,128)(2,1)}, bf16[64,160,128]{2,1,0:T(8,128)(2,1)S(1)}, u32[]{:S(2)}, u32[]{:S(2)}) collective-permute-start(bf16[64,160,128]{2,1,0:T(8,128)(2,1)} %collective-permute-done.1.refs_2_), channel_id=1, source_target_pairs={{0,1},{1,0},{2,3},{3,2},{4,5},{5,4},{6,7},{7,6},{8,9},{9,8},{10,11... | collective-permute-start | bytes 7864328 | tf_op jit(solution)/shard_map/ppermute | solution.py:50
  45.4 0.8 %collective-permute-start.13 = (bf16[64,64,128]{2,1,0:T(8,128)(2,1)}, bf16[64,64,128]{2,1,0:T(8,128)(2,1)S(1)}, u32[]{:S(2)}, u32[]{:S(2)}) collective-permute-start(bf16[64,64,128]{2,1,0:T(8,128)(2,1)} %collective-permute-done.7.refs_3_), channel_id=1, source_target_pairs={{0,8},{1,33},{2,10},{3,35},{4,12},{5,37},{6,14},{7,39},{8,16},{9,4... | collective-permute-start | bytes 3145736 | tf_op jit(solution)/shard_map/ppermute | solution.py:46
  46.1 1.9 %collective-permute-start.12 = (bf16[64,64,128]{2,1,0:T(8,128)(2,1)}, bf16[64,64,128]{2,1,0:T(8,128)(2,1)S(1)}, u32[]{:S(2)}, u32[]{:S(2)}) collective-permute-start(bf16[64,64,128]{2,1,0:T(8,128)(2,1)} %get-tuple-element.21.refs_1_), channel_id=1, source_target_pairs={{0,24},{1,97},{2,26},{3,99},{4,28},{5,101},{6,30},{7,103},{8,0},{9... | collective-permute-start | bytes 3145736 | tf_op jit(solution)/shard_map/ppermute | solution.py:46
  48.0 0.0 collective-permute-start.10
  48.0 2.7 %collective-permute-start.11 = (bf16[64,64,128]{2,1,0:T(8,128)(2,1)}, bf16[64,64,128]{2,1,0:T(8,128)(2,1)S(1)}, u32[]{:S(2)}, u32[]{:S(2)}) collective-permute-start(bf16[64,64,128]{2,1,0:T(8,128)(2,1)} %collective-permute-done.8.refs_1_), channel_id=1, source_target_pairs={{0,24},{1,97},{2,26},{3,99},{4,28},{5,101},{6,30},{7,103},{8,0},{9... | collective-permute-start | bytes 3145736 | tf_op jit(solution)/shard_map/ppermute | solution.py:46
  50.7 2.7 %shard_map.57.refs_0_ = bf16[256,160,128]{2,1,0:T(8,128)(2,1)S(1)} custom-call(bf16[64,160,128]{2,1,0:T(8,128)(2,1)S(1)} %bitcast.16, bf16[64,160,128]{2,1,0:T(8,128)(2,1)} %collective-permute-done.5.refs_1_, bf16[64,160,128]{2,1,0:T(8,128)(2,1)} %collective-permute-done.1.refs_2_, bf16[64,160,128]{2,1,0:T(8,128)(2,1)S(1)} %collective-permute-done.9.refs_3_), custom_call_target="tpu_custom_call" | custom-call | bytes 10000000 | tf_op jit(solution)/shard_map/pallas_call | solution.py:174
  53.5 5.8 %shard_map.58 = (f32[16,64,128]{2,1,0:T(8,128)S(1)}, f32[16,64,128]{2,1,0:T(8,128)S(1)}) custom-call(s32[1280]{0:T(1024)S(1)} %copy-done, s32[5]{0:T(128)S(1)} %convert_reduce_fusion.count_ref, bf16[256,160,128]{2,1,0:T(8,128)(2,1)S(1)} %shard_map.57.refs_0_, bf16[64,64,128]{2,1,0:T(8,128)(2,1)} %get-tuple-element.21.refs_1_, ...), custom_call_target="tpu_custom_call" | custom-call | flops 3000000000 | bytes 12000000 | tf_op jit(solution)/shard_map/pallas_call | solution.py:147
  59.2 1.5 %collective-permute-done.13.refs_1_ = bf16[64,64,128]{2,1,0:T(8,128)(2,1)S(1)} collective-permute-done((bf16[64,64,128]{2,1,0:T(8,128)(2,1)}, bf16[64,64,128]{2,1,0:T(8,128)(2,1)S(1)}, u32[]{:S(2)}, u32[]{:S(2)}) %collective-permute-start.13) | collective-permute-done | bytes 1048608 | tf_op jit(solution)/shard_map/ppermute | solution.py:46
  60.7 2.7 %shard_map.61.refs_2_ = f32[16,64,128]{2,1,0:T(8,128)S(1)} custom-call(s32[1280]{0:T(1024)S(1)} %copy-done, s32[5]{0:T(128)S(1)} %convert_reduce_fusion.count_ref, bf16[256,160,128]{2,1,0:T(8,128)(2,1)S(1)} %shard_map.57.refs_0_, bf16[64,64,128]{2,1,0:T(8,128)(2,1)S(1)} %collective-permute-done.13.refs_1_, f32[16,64,128]{2,1,0:T(8,128)S(1)} %get-tuple-element.30.refs_2_), custom_call_target="tpu_custom_call" | custom-call | flops 3000000000 | bytes 12000000 | tf_op jit(solution)/shard_map/pallas_call | solution.py:147
  63.5 2.0 %shard_map.62 = bf16[16,64,128]{2,1,0:T(8,128)(2,1)S(1)} custom-call(s32[1280]{0:T(1024)S(1)} %copy-done, s32[5]{0:T(128)S(1)} %convert_reduce_fusion.count_ref, bf16[256,160,128]{2,1,0:T(8,128)(2,1)S(1)} %shard_map.57.refs_0_, bf16[64,64,128]{2,1,0:T(8,128)(2,1)S(1)} %collective-permute-done.12.refs_1_, f32[16,64,128]{2,1,0:T(8,128)S(1)} %shard_map.61.refs_2_), custom_call_target="tpu_custom_call" | custom-call | flops 3000000000 | bytes 12000000 | tf_op jit(solution)/shard_map/pallas_call | solution.py:147
  65.5 0.1 collective-permute-start.14
  65.6 2.7 %shard_map.59.refs_3_ = f32[16,64,128]{2,1,0:T(8,128)S(1)} custom-call(s32[1280]{0:T(1024)S(1)} %copy-done, s32[5]{0:T(128)S(1)} %convert_reduce_fusion.count_ref, bf16[256,160,128]{2,1,0:T(8,128)(2,1)S(1)} %shard_map.57.refs_0_, bf16[64,64,128]{2,1,0:T(8,128)(2,1)} %collective-permute-done.8.refs_1_, f32[16,64,128]{2,1,0:T(8,128)S(1)} %get-tuple-element.29.refs_2_), custom_call_target="tpu_custom_call" | custom-call | flops 3000000000 | bytes 12000000 | tf_op jit(solution)/shard_map/pallas_call | solution.py:147
  68.3 3.7 %collective-permute-done.10.refs_1_ = bf16[64,64,128]{2,1,0:T(8,128)(2,1)S(1)} collective-permute-done((bf16[64,64,128]{2,1,0:T(8,128)(2,1)}, bf16[64,64,128]{2,1,0:T(8,128)(2,1)S(1)}, u32[]{:S(2)}, u32[]{:S(2)}) %collective-permute-start.10) | collective-permute-done | bytes 1048608 | tf_op jit(solution)/shard_map/ppermute | solution.py:46
  72.0 4.1 %shard_map.60 = f32[16,64,128]{2,1,0:T(8,128)S(1)} custom-call(s32[1280]{0:T(1024)S(1)} %copy-done, s32[5]{0:T(128)S(1)} %convert_reduce_fusion.count_ref, bf16[256,160,128]{2,1,0:T(8,128)(2,1)S(1)} %shard_map.57.refs_0_, bf16[64,64,128]{2,1,0:T(8,128)(2,1)S(1)} %collective-permute-done.10.refs_1_, bf16[64,64,128]{2,1,0:T(8,128)(2,1)S(1)} %collective-permute-done.11.refs_2_, ...), custom_call_target="tpu_custom_call" | custom-call | flops 3000000000 | bytes 12000000 | tf_op jit(solution)/shard_map/pallas_call | solution.py:147
  76.1 0.8 %fusion = bf16[16,1,64,128]{3,2,1,0:T(8,128)(2,1)} fusion(f32[16,64,128]{2,1,0:T(8,128)S(1)} %shard_map.60, bf16[16,64,128]{2,1,0:T(8,128)(2,1)S(1)} %collective-permute-done.14), kind=kLoop, calls=%fused_computation.3 | loop fusion | flops 393216 | bytes 1048576 | tf_op jit(solution)/shard_map/broadcast_in_dim | solution.py:264
  (21 shorter events, 0.1 us)
Async XLA Ops:
  0.0 1.9 %copy-start.1 = (bf16[4,16,128,128]{3,2,1,0:T(8,128)(2,1)S(1)}, bf16[4,16,128,128]{3,2,1,0:T(8,128)(2,1)}, u32[]{:S(2)}) copy-start(bf16[4,16,128,128]{3,2,1,0:T(8,128)(2,1)} %param.7) | copy-start | bytes 6291460
  1.9 2.0 %copy-start.2 = (s32[4,16]{1,0:T(4,128)S(1)}, s32[4,16]{1,0:T(4,128)}, u32[]{:S(2)}) copy-start(s32[4,16]{1,0:T(4,128)} %param.8) | copy-start | bytes 772
  1.9 2.0 %copy-start.3 = (s32[4,16]{1,0:T(4,128)S(1)}, s32[4,16]{1,0:T(4,128)}, u32[]{:S(2)}) copy-start(s32[4,16]{1,0:T(4,128)} %param.9) | copy-start | bytes 772
  2.4 14.0 %collective-permute-start.5 = (bf16[64,160,128]{2,1,0:T(8,128)(2,1)S(1)}, bf16[64,160,128]{2,1,0:T(8,128)(2,1)}, u32[]{:S(2)}, u32[]{:S(2)}) collective-permute-start(bf16[64,160,128]{2,1,0:T(8,128)(2,1)S(1)} %bitcast.14), channel_id=1, source_target_pairs={{0,1},{1,0},{2,3},{3,2},{4,5},{5,4},{6,7},{7,6},{8,9},{9,8},{10,11... | collective-permute-start | bytes 7864328 | tf_op jit(solution)/shard_map/ppermute | solution.py:50
  3.9 5.5 %collective-permute-start = (s32[4,16]{1,0:T(4,128)S(1)}, s32[4,16]{1,0:T(4,128)S(1)}, u32[]{:S(2)}, u32[]{:S(2)}) collective-permute-start(s32[4,16]{1,0:T(4,128)S(1)} %compare_select_fusion.24), channel_id=1, source_target_pairs={{0,6},{1,3},{2,0},{3,5},{4,2},{5,7},{6,4},{7,1},{8,14},{9,11},{10,... | collective-permute-start | bytes 776 | tf_op jit(solution)/shard_map/ppermute | solution.py:50
  6.4 10.0 %collective-permute-start.4 = (bf16[2,16,64,128]{3,2,1,0:T(8,128)(2,1)S(1)}, bf16[2,16,64,128]{3,2,1,0:T(8,128)(2,1)}, u32[]{:S(2)}, u32[]{:S(2)}) collective-permute-start(bf16[2,16,64,128]{3,2,1,0:T(8,128)(2,1)S(1)} %pad_maximum_fusion.refs_0_), channel_id=1, source_target_pairs={{0,64},{1,17},{2,66},{3,19},{4,68},{5,21},{6,70},{7,23},{8,72},{9,... | collective-permute-start | bytes 1572872 | tf_op jit(solution)/shard_map/ppermute | solution.py:46
  9.4 32.1 %collective-permute-start.1 = (bf16[64,160,128]{2,1,0:T(8,128)(2,1)S(1)}, bf16[64,160,128]{2,1,0:T(8,128)(2,1)}, u32[]{:S(2)}, u32[]{:S(2)}) collective-permute-start(bf16[64,160,128]{2,1,0:T(8,128)(2,1)S(1)} %bitcast.15), channel_id=1, source_target_pairs={{0,6},{1,3},{2,0},{3,5},{4,2},{5,7},{6,4},{7,1},{8,14},{9,11},{10,... | collective-permute-start | bytes 7864328 | tf_op jit(solution)/shard_map/ppermute | solution.py:50
  10.6 3.5 %collective-permute-start.6 = (s32[2,4,16]{2,1,0:T(4,128)S(1)}, s32[2,4,16]{2,1,0:T(4,128)S(1)}, u32[]{:S(2)}, u32[]{:S(2)}) collective-permute-start(s32[2,4,16]{2,1,0:T(4,128)S(1)} %pad_add_fusion.1), channel_id=1, source_target_pairs={{0,1},{1,0},{2,3},{3,2},{4,5},{5,4},{6,7},{7,6},{8,9},{9,8},{10,11... | collective-permute-start | bytes 1544 | tf_op jit(solution)/shard_map/ppermute | solution.py:50
  12.8 9.7 %collective-permute-start.2 = (bf16[2,16,64,128]{3,2,1,0:T(8,128)(2,1)S(1)}, bf16[2,16,64,128]{3,2,1,0:T(8,128)(2,1)}, u32[]{:S(2)}, u32[]{:S(2)}) collective-permute-start(bf16[2,16,64,128]{3,2,1,0:T(8,128)(2,1)S(1)} %pad_maximum_fusion.refs_0_), channel_id=1, source_target_pairs={{0,32},{1,9},{2,34},{3,11},{4,36},{5,13},{6,38},{7,15},{8,40},{9,1... | collective-permute-start | bytes 1572872 | tf_op jit(solution)/shard_map/ppermute | solution.py:46
  14.1 8.4 %collective-permute-start.3 = (bf16[2,16,64,128]{3,2,1,0:T(8,128)(2,1)S(1)}, bf16[2,16,64,128]{3,2,1,0:T(8,128)(2,1)}, u32[]{:S(2)}, u32[]{:S(2)}) collective-permute-start(bf16[2,16,64,128]{3,2,1,0:T(8,128)(2,1)S(1)} %pad_maximum_fusion.refs_0_), channel_id=1, source_target_pairs={{0,96},{1,25},{2,98},{3,27},{4,100},{5,29},{6,102},{7,31},{8,104},... | collective-permute-start | bytes 1572872 | tf_op jit(solution)/shard_map/ppermute | solution.py:46
  25.3 16.4 %collective-permute-start.7 = (bf16[64,64,128]{2,1,0:T(8,128)(2,1)}, bf16[64,64,128]{2,1,0:T(8,128)(2,1)}, u32[]{:S(2)}, u32[]{:S(2)}) collective-permute-start(bf16[64,64,128]{2,1,0:T(8,128)(2,1)} %get-tuple-element.21.refs_1_), channel_id=1, source_target_pairs={{0,8},{1,33},{2,10},{3,35},{4,12},{5,37},{6,14},{7,39},{8,16},{9,4... | collective-permute-start | bytes 3145736 | tf_op jit(solution)/shard_map/ppermute | solution.py:46
  26.8 14.9 %collective-permute-start.8 = (bf16[64,64,128]{2,1,0:T(8,128)(2,1)}, bf16[64,64,128]{2,1,0:T(8,128)(2,1)}, u32[]{:S(2)}, u32[]{:S(2)}) collective-permute-start(bf16[64,64,128]{2,1,0:T(8,128)(2,1)} %get-tuple-element.22.refs_2_), channel_id=1, source_target_pairs={{0,24},{1,97},{2,26},{3,99},{4,28},{5,101},{6,30},{7,103},{8,0},{9... | collective-permute-start | bytes 3145736 | tf_op jit(solution)/shard_map/ppermute | solution.py:46
  34.0 19.5 %copy-start = (s32[1280]{0:T(1024)S(1)}, s32[1280]{0:T(1024)}, u32[]{:S(2)}) copy-start(s32[1280]{0:T(1024)} %shard_map.56.list_ref) | copy-start | bytes 15364
  41.7 9.0 %collective-permute-start.9 = (bf16[64,160,128]{2,1,0:T(8,128)(2,1)}, bf16[64,160,128]{2,1,0:T(8,128)(2,1)S(1)}, u32[]{:S(2)}, u32[]{:S(2)}) collective-permute-start(bf16[64,160,128]{2,1,0:T(8,128)(2,1)} %collective-permute-done.1.refs_2_), channel_id=1, source_target_pairs={{0,1},{1,0},{2,3},{3,2},{4,5},{5,4},{6,7},{7,6},{8,9},{9,8},{10,11... | collective-permute-start | bytes 7864328 | tf_op jit(solution)/shard_map/ppermute | solution.py:50
  45.4 15.4 %collective-permute-start.13 = (bf16[64,64,128]{2,1,0:T(8,128)(2,1)}, bf16[64,64,128]{2,1,0:T(8,128)(2,1)S(1)}, u32[]{:S(2)}, u32[]{:S(2)}) collective-permute-start(bf16[64,64,128]{2,1,0:T(8,128)(2,1)} %collective-permute-done.7.refs_3_), channel_id=1, source_target_pairs={{0,8},{1,33},{2,10},{3,35},{4,12},{5,37},{6,14},{7,39},{8,16},{9,4... | collective-permute-start | bytes 3145736 | tf_op jit(solution)/shard_map/ppermute | solution.py:46
  46.1 17.3 %collective-permute-start.12 = (bf16[64,64,128]{2,1,0:T(8,128)(2,1)}, bf16[64,64,128]{2,1,0:T(8,128)(2,1)S(1)}, u32[]{:S(2)}, u32[]{:S(2)}) collective-permute-start(bf16[64,64,128]{2,1,0:T(8,128)(2,1)} %get-tuple-element.21.refs_1_), channel_id=1, source_target_pairs={{0,24},{1,97},{2,26},{3,99},{4,28},{5,101},{6,30},{7,103},{8,0},{9... | collective-permute-start | bytes 3145736 | tf_op jit(solution)/shard_map/ppermute | solution.py:46
  48.0 23.9 %collective-permute-start.10 = (bf16[64,64,128]{2,1,0:T(8,128)(2,1)}, bf16[64,64,128]{2,1,0:T(8,128)(2,1)S(1)}, u32[]{:S(2)}, u32[]{:S(2)}) collective-permute-start(bf16[64,64,128]{2,1,0:T(8,128)(2,1)} %get-tuple-element.22.refs_2_), channel_id=1, source_target_pairs={{0,8},{1,33},{2,10},{3,35},{4,12},{5,37},{6,14},{7,39},{8,16},{9,4... | collective-permute-start | bytes 3145736 | tf_op jit(solution)/shard_map/ppermute | solution.py:46
  48.0 23.9 %collective-permute-start.11 = (bf16[64,64,128]{2,1,0:T(8,128)(2,1)}, bf16[64,64,128]{2,1,0:T(8,128)(2,1)S(1)}, u32[]{:S(2)}, u32[]{:S(2)}) collective-permute-start(bf16[64,64,128]{2,1,0:T(8,128)(2,1)} %collective-permute-done.8.refs_1_), channel_id=1, source_target_pairs={{0,24},{1,97},{2,26},{3,99},{4,28},{5,101},{6,30},{7,103},{8,0},{9... | collective-permute-start | bytes 3145736 | tf_op jit(solution)/shard_map/ppermute | solution.py:46
  65.5 10.6 %collective-permute-start.14 = (bf16[16,64,128]{2,1,0:T(8,128)(2,1)S(1)}, bf16[16,64,128]{2,1,0:T(8,128)(2,1)S(1)}, u32[]{:S(2)}, u32[]{:S(2)}) collective-permute-start(bf16[16,64,128]{2,1,0:T(8,128)(2,1)S(1)} %shard_map.62), channel_id=1, source_target_pairs={{0,4},{1,5},{2,6},{3,7},{4,0},{5,1},{6,2},{7,3},{8,12},{9,13},{10,... | collective-permute-start | bytes 786440 | tf_op jit(solution)/shard_map/ppermute | solution.py:50

commit v6 on v5

--- a/solution.py
+++ b/solution.py
@@ -229,7 +229,7 @@
     to_send, both = lax.optimization_barrier((env, both))
     env_apart = over_mpo(to_send, X_APART)
 
-    across, env_core, both, both_core = lax.optimization_barrier((across, env_core, both, both_core))
+    across, both, both_core = lax.optimization_barrier((across, both, both_core))
     lines = make_lines([own, up, down, across])
 
     wanted = jnp.stack([both[0], both_core[0], both[1], both_core[1]])

time: 77 us -> 75 us (0.974)
  local copies, waits for them, and re-layouts: 3.43 us -> 1.77 us
  Pallas kernels: 24.6 us -> 23.2 us
  waiting for transfers between devices: 18.9 us -> 18.1 us
    ppermute x6, waiting for transfers between devices: 7.54 us -> 1.26 us  [over_mpo(): return lax.ppermute(x, 'mpo', perm)]
    ppermute x9, waiting for transfers between devices: 11.4 us -> 16.9 us  [over_all(): return lax.ppermute(x, ('sec', 'mpo'), perm)]
    ppermute x6, starting transfers between devices: 10 us -> 11.5 us  [over_mpo(): return lax.ppermute(x, 'mpo', perm)]
    slice x1, local copies, waits for them, and re-layouts: 1.46 us -> 0.09 us  [per_device(): left_env[:, :, :rows]]
    pallas_call x5, Pallas kernels: 17.3 us -> 15.9 us  [add_terms(): pl.pallas_call(functools.partial(term_kernel, plan, n_vec, len(envs), acc...]
    select_n x1, other arithmetic: 0.01 us -> 0.79 us  [per_device(): masked = jnp.where(active > 0, source, -1)]
  transfers between devices with their start and end apart: 15 -> 15, of which waited for: 5 -> 7; matrix products, arithmetic and copies ran while one was open for 6% -> 7% of each run, Pallas kernels for 32% -> 31%
where the time goes in v6:
time: 75 us; the launch traced here: 74.5 us
  starting transfers between devices  26.2 us (35%)
  Pallas kernels  23.2 us (31%)
  waiting for transfers between devices  18.1 us (24%)
  other arithmetic  5.03 us (7%)
  local copies, waits for them, and re-layouts  1.77 us (2%)
    ppermute x9, waiting for transfers between devices, over_all(): return lax.ppermute(x, ('sec', 'mpo'), perm)  16.9 us
    pallas_call x5, Pallas kernels, add_terms(): pl.pallas_call(functools.partial(term_kernel, plan, n_vec, len(envs), acc...  15.9 us
    ppermute x9, starting transfers between devices, over_all(): return lax.ppermute(x, ('sec', 'mpo'), perm)  14.8 us
    ppermute x6, starting transfers between devices, over_mpo(): return lax.ppermute(x, 'mpo', perm)  11.5 us
    pallas_call x1, Pallas kernels, make_lines(): pl.pallas_call(line_kernel, out_shape=[jax.ShapeDtypeStruct(shape, BF) fo...  2.8 us
    pallas_call x1, Pallas kernels, join(): pl.pallas_call(join_kernel, out_shape=jax.ShapeDtypeStruct((first.shape[0...  2.74 us
    pallas_call x1, Pallas kernels, make_lists(): pl.pallas_call(list_kernel, out_shape=jax.ShapeDtypeStruct(((PIECES + 1)...  1.74 us
    another operation x2, other arithmetic  1.56 us
  transfers between devices with their start and end apart: 15, of which 7 were waited for; matrix products, arithmetic and copies ran while one was open for 7% of the time, Pallas kernels for 31%

profile of v6, /device:TPU:1, one launch (start us, length us, event | category | flops | bytes accessed | tf_op | source)
XLA Modules:
  0.0 74.5 jit_solution(13546702111407520523)
XLA Ops:
  0.0 0.8 %compare_select_fusion.24 = s32[4,16]{1,0:T(4,128)S(1)} fusion(s32[4,16]{1,0:T(4,128)} %param.8, s32[4,16]{1,0:T(4,128)} %param.9), kind=kLoop, calls=%fused_computation.52 | loop fusion | flops 128 | bytes 768 | tf_op jit(solution)/shard_map/jit(_where)/select_n | solution.py:225
  0.8 2.0 %collective-permute-start = (s32[4,16]{1,0:T(4,128)S(1)}, s32[4,16]{1,0:T(4,128)S(1)}, u32[]{:S(2)}, u32[]{:S(2)}) collective-permute-start(s32[4,16]{1,0:T(4,128)S(1)} %compare_select_fusion.24), channel_id=1, source_target_pairs={{0,6},{1,3},{2,0},{3,5},{4,2},{5,7},{6,4},{7,1},{8,14},{9,11},{10,... | collective-permute-start | bytes 776 | tf_op jit(solution)/shard_map/ppermute | solution.py:50
  2.8 1.2 %dynamic-slice_bitcast_fusion.1 = (bf16[1,16,64,128]{3,2,1,0:T(8,128)(2,1)S(1)}, bf16[1,16,64,128]{3,2,1,0:T(8,128)(2,1)S(1)}) fusion(bf16[16,8,64,128]{3,2,1,0:T(8,128)(2,1)} %param.5, s32[]{:T(128)S(6)} %select_n.241, s32[]{:T(128)S(6)} %select_n.242), kind=kLoop, calls=%fused_computation.5 | loop fusion | bytes 1048584 | tf_op jit(solution)/shard_map/stack;squeeze | solution.py:216
  4.1 0.1 pad_maximum_fusion.refs_0_
  4.1 3.0 %collective-permute-start.4 = (bf16[2,16,64,128]{3,2,1,0:T(8,128)(2,1)S(1)}, bf16[2,16,64,128]{3,2,1,0:T(8,128)(2,1)}, u32[]{:S(2)}, u32[]{:S(2)}) collective-permute-start(bf16[2,16,64,128]{3,2,1,0:T(8,128)(2,1)S(1)} %pad_maximum_fusion.refs_0_), channel_id=1, source_target_pairs={{0,64},{1,17},{2,66},{3,19},{4,68},{5,21},{6,70},{7,23},{8,72},{9,... | collective-permute-start | bytes 1572872 | tf_op jit(solution)/shard_map/ppermute | solution.py:46
  7.1 0.1 fusion.18
  7.2 0.4 maximum_maximum_fusion
  7.7 0.0 collective-permute-done
  7.7 1.3 %collective-permute-start.1 = (bf16[64,160,128]{2,1,0:T(8,128)(2,1)S(1)}, bf16[64,160,128]{2,1,0:T(8,128)(2,1)}, u32[]{:S(2)}, u32[]{:S(2)}) collective-permute-start(bf16[64,160,128]{2,1,0:T(8,128)(2,1)S(1)} %bitcast.14), channel_id=1, source_target_pairs={{0,6},{1,3},{2,0},{3,5},{4,2},{5,7},{6,4},{7,1},{8,14},{9,11},{10,... | collective-permute-start | bytes 7864328 | tf_op jit(solution)/shard_map/ppermute | solution.py:50
  9.0 0.4 collective-permute-start.2
  9.4 2.3 %collective-permute-start.3 = (bf16[2,16,64,128]{3,2,1,0:T(8,128)(2,1)S(1)}, bf16[2,16,64,128]{3,2,1,0:T(8,128)(2,1)}, u32[]{:S(2)}, u32[]{:S(2)}) collective-permute-start(bf16[2,16,64,128]{3,2,1,0:T(8,128)(2,1)S(1)} %pad_maximum_fusion.refs_0_), channel_id=1, source_target_pairs={{0,96},{1,25},{2,98},{3,27},{4,100},{5,29},{6,102},{7,31},{8,104},... | collective-permute-start | bytes 1572872 | tf_op jit(solution)/shard_map/ppermute | solution.py:46
  11.6 3.4 %collective-permute-start.5 = (s32[2,4,16]{2,1,0:T(4,128)S(1)}, s32[2,4,16]{2,1,0:T(4,128)S(1)}, u32[]{:S(2)}, u32[]{:S(2)}) collective-permute-start(s32[2,4,16]{2,1,0:T(4,128)S(1)} %pad_add_fusion.1), channel_id=1, source_target_pairs={{0,1},{1,0},{2,3},{3,2},{4,5},{5,4},{6,7},{7,6},{8,9},{9,8},{10,11... | collective-permute-start | bytes 1544 | tf_op jit(solution)/shard_map/ppermute | solution.py:50
  15.0 0.8 %collective-permute-done.5 = s32[2,4,16]{2,1,0:T(4,128)S(1)} collective-permute-done((s32[2,4,16]{2,1,0:T(4,128)S(1)}, s32[2,4,16]{2,1,0:T(4,128)S(1)}, u32[]{:S(2)}, u32[]{:S(2)}) %collective-permute-start.5) | collective-permute-done | bytes 544 | tf_op jit(solution)/shard_map/ppermute | solution.py:50
  15.8 0.3 collective-permute-start.8
  16.2 0.0 collective-permute-done.4.refs_3_
  16.2 0.1 stack.25
  16.3 0.1 stack.24
  16.4 3.4 %collective-permute-done.2.refs_1_ = bf16[2,16,64,128]{3,2,1,0:T(8,128)(2,1)} collective-permute-done((bf16[2,16,64,128]{3,2,1,0:T(8,128)(2,1)S(1)}, bf16[2,16,64,128]{3,2,1,0:T(8,128)(2,1)}, u32[]{:S(2)}, u32[]{:S(2)}) %collective-permute-start.2) | collective-permute-done | bytes 524320 | tf_op jit(solution)/shard_map/ppermute | solution.py:46
  19.7 0.3 collective-permute-done.3.refs_2_
  20.1 2.8 %shard_map.55 = (bf16[64,64,128]{2,1,0:T(8,128)(2,1)}, bf16[64,64,128]{2,1,0:T(8,128)(2,1)}) custom-call(bf16[2,16,64,128]{3,2,1,0:T(8,128)(2,1)S(1)} %pad_maximum_fusion.refs_0_, bf16[2,16,64,128]{3,2,1,0:T(8,128)(2,1)} %collective-permute-done.2.refs_1_, bf16[2,16,64,128]{3,2,1,0:T(8,128)(2,1)} %collective-permute-done.3.refs_2_, ...), custom_call_target="tpu_custom_call" | custom-call | flops 7000000000 | bytes 4000000 | tf_op jit(solution)/shard_map/pallas_call | solution.py:197
  22.9 1.6 %collective-permute-start.6 = (bf16[64,64,128]{2,1,0:T(8,128)(2,1)}, bf16[64,64,128]{2,1,0:T(8,128)(2,1)}, u32[]{:S(2)}, u32[]{:S(2)}) collective-permute-start(bf16[64,64,128]{2,1,0:T(8,128)(2,1)} %get-tuple-element.20.refs_1_), channel_id=1, source_target_pairs={{0,8},{1,33},{2,10},{3,35},{4,12},{5,37},{6,14},{7,39},{8,16},{9,4... | collective-permute-start | bytes 3145736 | tf_op jit(solution)/shard_map/ppermute | solution.py:46
  24.5 2.1 %collective-permute-start.7 = (bf16[64,64,128]{2,1,0:T(8,128)(2,1)}, bf16[64,64,128]{2,1,0:T(8,128)(2,1)}, u32[]{:S(2)}, u32[]{:S(2)}) collective-permute-start(bf16[64,64,128]{2,1,0:T(8,128)(2,1)} %get-tuple-element.21.refs_2_), channel_id=1, source_target_pairs={{0,24},{1,97},{2,26},{3,99},{4,28},{5,101},{6,30},{7,103},{8,0},{9... | collective-permute-start | bytes 3145736 | tf_op jit(solution)/shard_map/ppermute | solution.py:46
  26.7 1.5 %reduce-window.6 = s32[5,2,128]{2,1,0:T(2,128)S(1)} reduce-window(s32[5,2,128]{2,1,0:T(2,128)S(1)} %fusion.1, s32[]{:T(128)} %constant.127.clone.1), window={size=1x1x128 pad=0_0x0_0x127_0}, to_apply=%region_0.1 | reduce-window | flops 162560 | bytes 10244 | tf_op jit(solution)/shard_map/reduce-window
  28.2 0.1 slice.32
  28.3 0.1 copy.9
  28.4 0.1 copy.10
  28.5 0.1 select_reduce_fusion
  28.6 0.6 fusion.13
  29.2 0.5 bitcast_add_fusion
  29.8 1.7 %shard_map.56.list_ref = s32[1280]{0:T(1024)} custom-call(s32[256]{0:T(256)} %get-tuple-element.31.place_ref, s32[256]{0:T(256)} %get-tuple-element.29.entry_ref), custom_call_target="tpu_custom_call" | custom-call | tf_op jit(solution)/shard_map/pallas_call | solution.py:73
  31.5 0.1 convert_reduce_fusion.count_ref
  31.7 7.8 %collective-permute-done.6.refs_3_ = bf16[64,64,128]{2,1,0:T(8,128)(2,1)} collective-permute-done((bf16[64,64,128]{2,1,0:T(8,128)(2,1)}, bf16[64,64,128]{2,1,0:T(8,128)(2,1)}, u32[]{:S(2)}, u32[]{:S(2)}) %collective-permute-start.6) | collective-permute-done | bytes 1048608 | tf_op jit(solution)/shard_map/ppermute | solution.py:46
  39.4 0.4 collective-permute-done.1.refs_2_
  39.9 3.8 %collective-permute-start.9 = (bf16[64,160,128]{2,1,0:T(8,128)(2,1)}, bf16[64,160,128]{2,1,0:T(8,128)(2,1)S(1)}, u32[]{:S(2)}, u32[]{:S(2)}) collective-permute-start(bf16[64,160,128]{2,1,0:T(8,128)(2,1)} %collective-permute-done.1.refs_2_), channel_id=1, source_target_pairs={{0,1},{1,0},{2,3},{3,2},{4,5},{5,4},{6,7},{7,6},{8,9},{9,8},{10,11... | collective-permute-start | bytes 7864328 | tf_op jit(solution)/shard_map/ppermute | solution.py:50
  43.7 0.8 %collective-permute-start.13 = (bf16[64,64,128]{2,1,0:T(8,128)(2,1)}, bf16[64,64,128]{2,1,0:T(8,128)(2,1)S(1)}, u32[]{:S(2)}, u32[]{:S(2)}) collective-permute-start(bf16[64,64,128]{2,1,0:T(8,128)(2,1)} %collective-permute-done.6.refs_3_), channel_id=1, source_target_pairs={{0,8},{1,33},{2,10},{3,35},{4,12},{5,37},{6,14},{7,39},{8,16},{9,4... | collective-permute-start | bytes 3145736 | tf_op jit(solution)/shard_map/ppermute | solution.py:46
  44.5 1.9 %collective-permute-start.12 = (bf16[64,64,128]{2,1,0:T(8,128)(2,1)}, bf16[64,64,128]{2,1,0:T(8,128)(2,1)S(1)}, u32[]{:S(2)}, u32[]{:S(2)}) collective-permute-start(bf16[64,64,128]{2,1,0:T(8,128)(2,1)} %get-tuple-element.20.refs_1_), channel_id=1, source_target_pairs={{0,24},{1,97},{2,26},{3,99},{4,28},{5,101},{6,30},{7,103},{8,0},{9... | collective-permute-start | bytes 3145736 | tf_op jit(solution)/shard_map/ppermute | solution.py:46
  46.4 2.7 %collective-permute-start.11 = (bf16[64,64,128]{2,1,0:T(8,128)(2,1)}, bf16[64,64,128]{2,1,0:T(8,128)(2,1)S(1)}, u32[]{:S(2)}, u32[]{:S(2)}) collective-permute-start(bf16[64,64,128]{2,1,0:T(8,128)(2,1)} %collective-permute-done.7.refs_1_), channel_id=1, source_target_pairs={{0,24},{1,97},{2,26},{3,99},{4,28},{5,101},{6,30},{7,103},{8,0},{9... | collective-permute-start | bytes 3145736 | tf_op jit(solution)/shard_map/ppermute | solution.py:46
  49.0 0.0 collective-permute-done.9.refs_3_
  49.0 2.7 %shard_map.57.refs_0_ = bf16[256,160,128]{2,1,0:T(8,128)(2,1)S(1)} custom-call(bf16[64,160,128]{2,1,0:T(8,128)(2,1)S(1)} %bitcast.16, bf16[64,160,128]{2,1,0:T(8,128)(2,1)} %collective-permute-done.8.refs_1_, bf16[64,160,128]{2,1,0:T(8,128)(2,1)} %collective-permute-done.1.refs_2_, bf16[64,160,128]{2,1,0:T(8,128)(2,1)S(1)} %collective-permute-done.9.refs_3_), custom_call_target="tpu_custom_call" | custom-call | bytes 10000000 | tf_op jit(solution)/shard_map/pallas_call | solution.py:174
  51.8 5.7 %shard_map.58 = (f32[16,64,128]{2,1,0:T(8,128)S(1)}, f32[16,64,128]{2,1,0:T(8,128)S(1)}) custom-call(s32[1280]{0:T(1024)S(1)} %copy-done, s32[5]{0:T(128)S(1)} %convert_reduce_fusion.count_ref, bf16[256,160,128]{2,1,0:T(8,128)(2,1)S(1)} %shard_map.57.refs_0_, bf16[64,64,128]{2,1,0:T(8,128)(2,1)} %get-tuple-element.20.refs_1_, ...), custom_call_target="tpu_custom_call" | custom-call | flops 3000000000 | bytes 12000000 | tf_op jit(solution)/shard_map/pallas_call | solution.py:147
  57.6 1.5 %collective-permute-done.13.refs_1_ = bf16[64,64,128]{2,1,0:T(8,128)(2,1)S(1)} collective-permute-done((bf16[64,64,128]{2,1,0:T(8,128)(2,1)}, bf16[64,64,128]{2,1,0:T(8,128)(2,1)S(1)}, u32[]{:S(2)}, u32[]{:S(2)}) %collective-permute-start.13) | collective-permute-done | bytes 1048608 | tf_op jit(solution)/shard_map/ppermute | solution.py:46
  59.0 2.0 %shard_map.61.refs_2_ = f32[16,64,128]{2,1,0:T(8,128)S(1)} custom-call(s32[1280]{0:T(1024)S(1)} %copy-done, s32[5]{0:T(128)S(1)} %convert_reduce_fusion.count_ref, bf16[256,160,128]{2,1,0:T(8,128)(2,1)S(1)} %shard_map.57.refs_0_, bf16[64,64,128]{2,1,0:T(8,128)(2,1)S(1)} %collective-permute-done.13.refs_1_, f32[16,64,128]{2,1,0:T(8,128)S(1)} %get-tuple-element.28.refs_2_), custom_call_target="tpu_custom_call" | custom-call | flops 3000000000 | bytes 12000000 | tf_op jit(solution)/shard_map/pallas_call | solution.py:147
  61.1 2.0 %shard_map.62 = bf16[16,64,128]{2,1,0:T(8,128)(2,1)S(1)} custom-call(s32[1280]{0:T(1024)S(1)} %copy-done, s32[5]{0:T(128)S(1)} %convert_reduce_fusion.count_ref, bf16[256,160,128]{2,1,0:T(8,128)(2,1)S(1)} %shard_map.57.refs_0_, bf16[64,64,128]{2,1,0:T(8,128)(2,1)S(1)} %collective-permute-done.12.refs_1_, f32[16,64,128]{2,1,0:T(8,128)S(1)} %shard_map.61.refs_2_), custom_call_target="tpu_custom_call" | custom-call | flops 3000000000 | bytes 12000000 | tf_op jit(solution)/shard_map/pallas_call | solution.py:147
  63.2 0.6 collective-permute-start.14
  63.8 2.7 %shard_map.59.refs_3_ = f32[16,64,128]{2,1,0:T(8,128)S(1)} custom-call(s32[1280]{0:T(1024)S(1)} %copy-done, s32[5]{0:T(128)S(1)} %convert_reduce_fusion.count_ref, bf16[256,160,128]{2,1,0:T(8,128)(2,1)S(1)} %shard_map.57.refs_0_, bf16[64,64,128]{2,1,0:T(8,128)(2,1)} %collective-permute-done.7.refs_1_, f32[16,64,128]{2,1,0:T(8,128)S(1)} %get-tuple-element.27.refs_2_), custom_call_target="tpu_custom_call" | custom-call | flops 3000000000 | bytes 12000000 | tf_op jit(solution)/shard_map/pallas_call | solution.py:147
  66.4 3.9 %collective-permute-done.10.refs_1_ = bf16[64,64,128]{2,1,0:T(8,128)(2,1)S(1)} collective-permute-done((bf16[64,64,128]{2,1,0:T(8,128)(2,1)}, bf16[64,64,128]{2,1,0:T(8,128)(2,1)S(1)}, u32[]{:S(2)}, u32[]{:S(2)}) %collective-permute-start.10) | collective-permute-done | bytes 1048608 | tf_op jit(solution)/shard_map/ppermute | solution.py:46
  70.3 3.4 %shard_map.60 = f32[16,64,128]{2,1,0:T(8,128)S(1)} custom-call(s32[1280]{0:T(1024)S(1)} %copy-done, s32[5]{0:T(128)S(1)} %convert_reduce_fusion.count_ref, bf16[256,160,128]{2,1,0:T(8,128)(2,1)S(1)} %shard_map.57.refs_0_, bf16[64,64,128]{2,1,0:T(8,128)(2,1)S(1)} %collective-permute-done.10.refs_1_, bf16[64,64,128]{2,1,0:T(8,128)(2,1)S(1)} %collective-permute-done.11.refs_2_, ...), custom_call_target="tpu_custom_call" | custom-call | flops 3000000000 | bytes 12000000 | tf_op jit(solution)/shard_map/pallas_call | solution.py:147
  73.7 0.8 %fusion = bf16[16,1,64,128]{3,2,1,0:T(8,128)(2,1)} fusion(f32[16,64,128]{2,1,0:T(8,128)S(1)} %shard_map.60, bf16[16,64,128]{2,1,0:T(8,128)(2,1)S(1)} %collective-permute-done.14), kind=kLoop, calls=%fused_computation.3 | loop fusion | flops 393216 | bytes 1048576 | tf_op jit(solution)/shard_map/broadcast_in_dim | solution.py:264
  (19 shorter events, 0.1 us)
Async XLA Ops:
  0.0 7.1 %copy-start.2 = (bf16[4,16,64,64]{3,2,1,0:T(8,128)(2,1)S(1)}, bf16[4,16,64,64]{3,2,1,0:T(8,128)(2,1)}, u32[]{:S(2)}) copy-start(bf16[4,16,64,64]{3,2,1,0:T(8,128)(2,1)} %param.6) | copy-start | bytes 1572868
  0.8 6.9 %collective-permute-start = (s32[4,16]{1,0:T(4,128)S(1)}, s32[4,16]{1,0:T(4,128)S(1)}, u32[]{:S(2)}, u32[]{:S(2)}) collective-permute-start(s32[4,16]{1,0:T(4,128)S(1)} %compare_select_fusion.24), channel_id=1, source_target_pairs={{0,6},{1,3},{2,0},{3,5},{4,2},{5,7},{6,4},{7,1},{8,14},{9,11},{10,... | collective-permute-start | bytes 776 | tf_op jit(solution)/shard_map/ppermute | solution.py:50
  2.8 4.4 %copy-start.1 = (bf16[4,16,128,128]{3,2,1,0:T(8,128)(2,1)S(1)}, bf16[4,16,128,128]{3,2,1,0:T(8,128)(2,1)}, u32[]{:S(2)}) copy-start(bf16[4,16,128,128]{3,2,1,0:T(8,128)(2,1)} %param.7) | copy-start | bytes 6291460
  4.1 12.1 %collective-permute-start.4 = (bf16[2,16,64,128]{3,2,1,0:T(8,128)(2,1)S(1)}, bf16[2,16,64,128]{3,2,1,0:T(8,128)(2,1)}, u32[]{:S(2)}, u32[]{:S(2)}) collective-permute-start(bf16[2,16,64,128]{3,2,1,0:T(8,128)(2,1)S(1)} %pad_maximum_fusion.refs_0_), channel_id=1, source_target_pairs={{0,64},{1,17},{2,66},{3,19},{4,68},{5,21},{6,70},{7,23},{8,72},{9,... | collective-permute-start | bytes 1572872 | tf_op jit(solution)/shard_map/ppermute | solution.py:46
  7.7 32.2 %collective-permute-start.1 = (bf16[64,160,128]{2,1,0:T(8,128)(2,1)S(1)}, bf16[64,160,128]{2,1,0:T(8,128)(2,1)}, u32[]{:S(2)}, u32[]{:S(2)}) collective-permute-start(bf16[64,160,128]{2,1,0:T(8,128)(2,1)S(1)} %bitcast.14), channel_id=1, source_target_pairs={{0,6},{1,3},{2,0},{3,5},{4,2},{5,7},{6,4},{7,1},{8,14},{9,11},{10,... | collective-permute-start | bytes 7864328 | tf_op jit(solution)/shard_map/ppermute | solution.py:50
  9.0 10.8 %collective-permute-start.2 = (bf16[2,16,64,128]{3,2,1,0:T(8,128)(2,1)S(1)}, bf16[2,16,64,128]{3,2,1,0:T(8,128)(2,1)}, u32[]{:S(2)}, u32[]{:S(2)}) collective-permute-start(bf16[2,16,64,128]{3,2,1,0:T(8,128)(2,1)S(1)} %pad_maximum_fusion.refs_0_), channel_id=1, source_target_pairs={{0,32},{1,9},{2,34},{3,11},{4,36},{5,13},{6,38},{7,15},{8,40},{9,1... | collective-permute-start | bytes 1572872 | tf_op jit(solution)/shard_map/ppermute | solution.py:46
  9.4 10.7 %collective-permute-start.3 = (bf16[2,16,64,128]{3,2,1,0:T(8,128)(2,1)S(1)}, bf16[2,16,64,128]{3,2,1,0:T(8,128)(2,1)}, u32[]{:S(2)}, u32[]{:S(2)}) collective-permute-start(bf16[2,16,64,128]{3,2,1,0:T(8,128)(2,1)S(1)} %pad_maximum_fusion.refs_0_), channel_id=1, source_target_pairs={{0,96},{1,25},{2,98},{3,27},{4,100},{5,29},{6,102},{7,31},{8,104},... | collective-permute-start | bytes 1572872 | tf_op jit(solution)/shard_map/ppermute | solution.py:46
  11.6 4.2 %collective-permute-start.5 = (s32[2,4,16]{2,1,0:T(4,128)S(1)}, s32[2,4,16]{2,1,0:T(4,128)S(1)}, u32[]{:S(2)}, u32[]{:S(2)}) collective-permute-start(s32[2,4,16]{2,1,0:T(4,128)S(1)} %pad_add_fusion.1), channel_id=1, source_target_pairs={{0,1},{1,0},{2,3},{3,2},{4,5},{5,4},{6,7},{7,6},{8,9},{9,8},{10,11... | collective-permute-start | bytes 1544 | tf_op jit(solution)/shard_map/ppermute | solution.py:50
  15.8 30.5 %collective-permute-start.8 = (bf16[64,160,128]{2,1,0:T(8,128)(2,1)S(1)}, bf16[64,160,128]{2,1,0:T(8,128)(2,1)}, u32[]{:S(2)}, u32[]{:S(2)}) collective-permute-start(bf16[64,160,128]{2,1,0:T(8,128)(2,1)S(1)} %bitcast.15), channel_id=1, source_target_pairs={{0,1},{1,0},{2,3},{3,2},{4,5},{5,4},{6,7},{7,6},{8,9},{9,8},{10,11... | collective-permute-start | bytes 7864328 | tf_op jit(solution)/shard_map/ppermute | solution.py:50
  22.9 16.6 %collective-permute-start.6 = (bf16[64,64,128]{2,1,0:T(8,128)(2,1)}, bf16[64,64,128]{2,1,0:T(8,128)(2,1)}, u32[]{:S(2)}, u32[]{:S(2)}) collective-permute-start(bf16[64,64,128]{2,1,0:T(8,128)(2,1)} %get-tuple-element.20.refs_1_), channel_id=1, source_target_pairs={{0,8},{1,33},{2,10},{3,35},{4,12},{5,37},{6,14},{7,39},{8,16},{9,4... | collective-permute-start | bytes 3145736 | tf_op jit(solution)/shard_map/ppermute | solution.py:46
  24.5 14.9 %collective-permute-start.7 = (bf16[64,64,128]{2,1,0:T(8,128)(2,1)}, bf16[64,64,128]{2,1,0:T(8,128)(2,1)}, u32[]{:S(2)}, u32[]{:S(2)}) collective-permute-start(bf16[64,64,128]{2,1,0:T(8,128)(2,1)} %get-tuple-element.21.refs_2_), channel_id=1, source_target_pairs={{0,24},{1,97},{2,26},{3,99},{4,28},{5,101},{6,30},{7,103},{8,0},{9... | collective-permute-start | bytes 3145736 | tf_op jit(solution)/shard_map/ppermute | solution.py:46
  31.7 20.1 %copy-start = (s32[1280]{0:T(1024)S(1)}, s32[1280]{0:T(1024)}, u32[]{:S(2)}) copy-start(s32[1280]{0:T(1024)} %shard_map.56.list_ref) | copy-start | bytes 15364
  39.9 9.2 %collective-permute-start.9 = (bf16[64,160,128]{2,1,0:T(8,128)(2,1)}, bf16[64,160,128]{2,1,0:T(8,128)(2,1)S(1)}, u32[]{:S(2)}, u32[]{:S(2)}) collective-permute-start(bf16[64,160,128]{2,1,0:T(8,128)(2,1)} %collective-permute-done.1.refs_2_), channel_id=1, source_target_pairs={{0,1},{1,0},{2,3},{3,2},{4,5},{5,4},{6,7},{7,6},{8,9},{9,8},{10,11... | collective-permute-start | bytes 7864328 | tf_op jit(solution)/shard_map/ppermute | solution.py:50
  43.7 15.4 %collective-permute-start.13 = (bf16[64,64,128]{2,1,0:T(8,128)(2,1)}, bf16[64,64,128]{2,1,0:T(8,128)(2,1)S(1)}, u32[]{:S(2)}, u32[]{:S(2)}) collective-permute-start(bf16[64,64,128]{2,1,0:T(8,128)(2,1)} %collective-permute-done.6.refs_3_), channel_id=1, source_target_pairs={{0,8},{1,33},{2,10},{3,35},{4,12},{5,37},{6,14},{7,39},{8,16},{9,4... | collective-permute-start | bytes 3145736 | tf_op jit(solution)/shard_map/ppermute | solution.py:46
  44.5 16.6 %collective-permute-start.12 = (bf16[64,64,128]{2,1,0:T(8,128)(2,1)}, bf16[64,64,128]{2,1,0:T(8,128)(2,1)S(1)}, u32[]{:S(2)}, u32[]{:S(2)}) collective-permute-start(bf16[64,64,128]{2,1,0:T(8,128)(2,1)} %get-tuple-element.20.refs_1_), channel_id=1, source_target_pairs={{0,24},{1,97},{2,26},{3,99},{4,28},{5,101},{6,30},{7,103},{8,0},{9... | collective-permute-start | bytes 3145736 | tf_op jit(solution)/shard_map/ppermute | solution.py:46
  46.4 23.9 %collective-permute-start.10 = (bf16[64,64,128]{2,1,0:T(8,128)(2,1)}, bf16[64,64,128]{2,1,0:T(8,128)(2,1)S(1)}, u32[]{:S(2)}, u32[]{:S(2)}) collective-permute-start(bf16[64,64,128]{2,1,0:T(8,128)(2,1)} %get-tuple-element.21.refs_2_), channel_id=1, source_target_pairs={{0,8},{1,33},{2,10},{3,35},{4,12},{5,37},{6,14},{7,39},{8,16},{9,4... | collective-permute-start | bytes 3145736 | tf_op jit(solution)/shard_map/ppermute | solution.py:46
  46.4 23.9 %collective-permute-start.11 = (bf16[64,64,128]{2,1,0:T(8,128)(2,1)}, bf16[64,64,128]{2,1,0:T(8,128)(2,1)S(1)}, u32[]{:S(2)}, u32[]{:S(2)}) collective-permute-start(bf16[64,64,128]{2,1,0:T(8,128)(2,1)} %collective-permute-done.7.refs_1_), channel_id=1, source_target_pairs={{0,24},{1,97},{2,26},{3,99},{4,28},{5,101},{6,30},{7,103},{8,0},{9... | collective-permute-start | bytes 3145736 | tf_op jit(solution)/shard_map/ppermute | solution.py:46
  63.2 10.6 %collective-permute-start.14 = (bf16[16,64,128]{2,1,0:T(8,128)(2,1)S(1)}, bf16[16,64,128]{2,1,0:T(8,128)(2,1)S(1)}, u32[]{:S(2)}, u32[]{:S(2)}) collective-permute-start(bf16[16,64,128]{2,1,0:T(8,128)(2,1)S(1)} %shard_map.62), channel_id=1, source_target_pairs={{0,4},{1,5},{2,6},{3,7},{4,0},{5,1},{6,2},{7,3},{8,12},{9,13},{10,... | collective-permute-start | bytes 786440 | tf_op jit(solution)/shard_map/ppermute | solution.py:50
